TPU v7x, 128 devices: a whole 4x4x4 slice. The times are simulated.
128 devices in a mesh: section: 8 (over y_lo, z), head: 16 (over x, y_hi, core).
Axes of the slice: x: 4, y: 4 (y_hi: 2, y_lo: 2; y = y_hi * 2 + y_lo), z: 4, core: 2. Of those that a mesh axis runs over, the one named last changes fastest.
Arguments:
- section_inputs: bfloat16 [8, 256, 1024], P('section'), may hold values from -6 to 6
- section_cotangents: bfloat16 [8, 256, 1024], P('section'), may hold values from -6 to 6
- fresh_tokens: bfloat16 [2, 256, 1024], replicated, may hold values from -6 to 6
- fresh_cotangents: bfloat16 [2, 256, 1024], replicated, may hold values from -6 to 6
- norm_gain: float32 [8, 1024], P('section'), may hold values from 0.1 to 1.9
- query_weight: bfloat16 [8, 1024, 16384], P('section', None, 'head'), as said below
- key_weight: bfloat16 [8, 1024, 16384], P('section', None, 'head'), may hold values from -0.1875 to 0.1875
- value_weight: bfloat16 [8, 1024, 16384], P('section', None, 'head'), may hold values from -0.1875 to 0.1875
- out_weight: bfloat16 [8, 16384, 1024], P('section', 'head'), may hold values from -0.1875 to 0.1875
- saved_inputs: bfloat16 [8, 4, 256, 1024], P('section', None, None, 'head'), may hold values from -6 to 6
- reload_slot: int32 [2, 8], replicated, may hold values from 0 to 3
Outputs:
- next_inputs: bfloat16 [8, 256, 1024], P('section')
- next_cotangents: bfloat16 [8, 256, 1024], P('section')
- saved_after: bfloat16 [8, 4, 256, 1024], P('section', None, None, 'head')
- query_grad: bfloat16 [8, 1024, 16384], P('section', None, 'head')
- key_grad: bfloat16 [8, 1024, 16384], P('section', None, 'head')
- value_grad: bfloat16 [8, 1024, 16384], P('section', None, 'head')
- out_grad: bfloat16 [8, 16384, 1024], P('section', 'head')
- gain_grad: float32 [8, 1024], P('section', 'head')
Inputs may be any that keep to these rules, and one draw needn't show every extreme that they name: `query_weight`: independent entries.
All inputs are finite; a program needn't handle non-finite values.
Results may differ from a plain program's by a relative error of at most 0.015.
The roundings to bfloat16 on the way count: a program that leaves them out, or rounds other values in their place, can miss the bound.
Values may be sent and summed in bfloat16 or wider, within the bound.
No kernel may reach another device: no remote copies, remote signals or barrier semaphores. Data moves between devices by JAX's collectives and lax.ppermute only.
A program may use at most 128 MiB of HBM per device.

v0:
```python
import jax
import jax.numpy as jnp
from jax import lax
from jax.sharding import PartitionSpec as P

DK = 128
TICKS = 2


epsilon = 1e-06


def passed_along(value, axis, by):
    count = lax.axis_size(axis)
    pairs = [(i, i + by) for i in range(count) if 0 <= i + by < count]
    return lax.ppermute(value, axis, pairs)


def swapped(value, axis, distance):
    mask = 2**distance
    pairs = [(source, source ^ mask) for source in range(lax.axis_size(axis))]
    return lax.ppermute(value, axis, pairs)


def normalize(rows, gain_row):
    floats = rows.astype(jnp.float32)
    inverse = lax.rsqrt(jnp.mean(floats * floats, axis=-1, keepdims=True) + epsilon)
    unit_rows = floats * inverse
    return ((unit_rows * gain_row).astype(jnp.bfloat16), unit_rows, inverse)


def split_heads(rows):
    return rows.reshape(rows.shape[0], -1, DK)


def attend(normed, query_part, key_part, value_part):
    queries = jnp.dot(normed, query_part, preferred_element_type=jnp.float32).astype(jnp.bfloat16)
    key_rows = jnp.dot(normed, key_part, preferred_element_type=jnp.float32).astype(jnp.bfloat16)
    value_rows = jnp.dot(normed, value_part, preferred_element_type=jnp.float32).astype(
        jnp.bfloat16
    )
    scores = jnp.einsum(
        "qhd,khd->hqk",
        split_heads(queries),
        split_heads(key_rows),
        preferred_element_type=jnp.float32,
    ) * DK ** (-0.5)
    highest = jnp.max(scores, axis=-1, keepdims=True)
    exponent = jnp.exp(scores - highest)
    softmax_rows = exponent / jnp.sum(exponent, axis=-1, keepdims=True)
    softmax_low = softmax_rows.astype(jnp.bfloat16)
    context = jnp.einsum(
        "hqk,khd->qhd", softmax_low, split_heads(value_rows), preferred_element_type=jnp.float32
    )
    context = context.astype(jnp.bfloat16).reshape(normed.shape[0], -1)
    return (queries, key_rows, value_rows, softmax_rows, softmax_low, context)


def ahead(rows, weights):
    gain_row, query_part, key_part, value_part, out_part = weights
    normed, unit_rows, inverse = normalize(rows, gain_row)
    context = attend(normed, query_part, key_part, value_part)[5]
    partial_value = jnp.dot(context, out_part, preferred_element_type=jnp.float32)
    total = lax.psum(partial_value, "head")
    output_rows = (rows.astype(jnp.float32) + total).astype(jnp.bfloat16)
    moved = passed_along(output_rows, "section", 1)
    return moved


def behind(rows, upstream, weights, column_start, share_width):
    gain_row, query_part, key_part, value_part, out_part = weights
    normed, unit_rows, inverse = normalize(rows, gain_row)
    queries, key_rows, value_rows, softmax_rows, softmax_low, context = attend(
        normed, query_part, key_part, value_part
    )
    token_count = rows.shape[0]
    out_term = jnp.dot(context.T, upstream, preferred_element_type=jnp.float32)
    context_grad = jnp.dot(upstream, out_part.T, preferred_element_type=jnp.float32).astype(
        jnp.bfloat16
    )
    softmax_grad = jnp.einsum(
        "qhd,khd->hqk",
        split_heads(context_grad),
        split_heads(value_rows),
        preferred_element_type=jnp.float32,
    )
    value_rows_grad = jnp.einsum(
        "hqk,qhd->khd", softmax_low, split_heads(context_grad), preferred_element_type=jnp.float32
    )
    value_rows_grad = value_rows_grad.astype(jnp.bfloat16).reshape(token_count, -1)
    inner = jnp.sum(softmax_rows * softmax_grad, axis=-1, keepdims=True)
    score_grad = (softmax_rows * (softmax_grad - inner) * DK ** (-0.5)).astype(jnp.bfloat16)
    queries_grad = jnp.einsum(
        "hqk,khd->qhd", score_grad, split_heads(key_rows), preferred_element_type=jnp.float32
    )
    queries_grad = queries_grad.astype(jnp.bfloat16).reshape(token_count, -1)
    key_rows_grad = jnp.einsum(
        "hqk,qhd->khd", score_grad, split_heads(queries), preferred_element_type=jnp.float32
    )
    key_rows_grad = key_rows_grad.astype(jnp.bfloat16).reshape(token_count, -1)
    query_term = jnp.dot(normed.T, queries_grad, preferred_element_type=jnp.float32)
    key_term = jnp.dot(normed.T, key_rows_grad, preferred_element_type=jnp.float32)
    value_term = jnp.dot(normed.T, value_rows_grad, preferred_element_type=jnp.float32)
    normed_part = jnp.dot(queries_grad, query_part.T, preferred_element_type=jnp.float32)
    normed_part = normed_part + jnp.dot(
        key_rows_grad, key_part.T, preferred_element_type=jnp.float32
    )
    normed_part = normed_part + jnp.dot(
        value_rows_grad, value_part.T, preferred_element_type=jnp.float32
    )
    normed_grad = lax.psum(normed_part, "head")
    gain_full = jnp.sum(normed_grad * unit_rows, axis=0)
    unit_grad = normed_grad * gain_row
    along = jnp.mean(unit_grad * unit_rows, axis=-1, keepdims=True)
    returned_rows = (
        upstream.astype(jnp.float32) + inverse * (unit_grad - unit_rows * along)
    ).astype(jnp.bfloat16)
    moved = passed_along(returned_rows, "section", -1)
    gain_term = lax.dynamic_slice_in_dim(gain_full, column_start, share_width, 0)
    return (moved, (query_term, key_term, value_term, out_term, gain_term))


def per_device(
    section_inputs,
    section_cotangents,
    fresh_tokens,
    fresh_cotangents,
    norm_gain,
    query_weight,
    key_weight,
    value_weight,
    out_weight,
    saved_inputs,
    reload_slot,
):
    section_count = lax.axis_size("section")
    section_index = lax.axis_index("section")
    head_index = lax.axis_index("head")
    mirror_index = section_count - 1 - section_index
    share_width = saved_inputs.shape[3]
    column_start = head_index * share_width
    weights = (norm_gain[0], query_weight[0], key_weight[0], value_weight[0], out_weight[0])
    current = section_inputs[0]
    upstream = section_cotangents[0]
    store = saved_inputs[0]
    sums = (
        jnp.zeros(query_weight.shape[1:], jnp.float32),
        jnp.zeros(key_weight.shape[1:], jnp.float32),
        jnp.zeros(value_weight.shape[1:], jnp.float32),
        jnp.zeros(out_weight.shape[1:], jnp.float32),
        jnp.zeros((share_width,), jnp.float32),
    )
    hop_count = section_count.bit_length() - 1
    for tick_number in range(TICKS):
        held_slot = lax.dynamic_index_in_dim(
            reload_slot[tick_number], mirror_index, 0, keepdims=False
        )
        held_block = lax.dynamic_index_in_dim(store, held_slot, 0, keepdims=False)
        own_share = lax.dynamic_slice_in_dim(current, column_start, share_width, 1)
        travel = (own_share, held_block)
        for bit_number in range(hop_count):
            travel = swapped((travel[0], travel[1]), "section", bit_number)
        arrived, reloaded = travel
        store = lax.dynamic_update_index_in_dim(store, arrived, held_slot, 0)
        restored = lax.all_gather(reloaded, "head", axis=1, tiled=True)
        produced = ahead(current, weights)
        returned, terms = behind(restored, upstream, weights, column_start, share_width)
        sums = tuple((total + term for total, term in zip(sums, terms)))
        current = jnp.where(section_index == 0, fresh_tokens[tick_number], produced)
        upstream = jnp.where(
            section_index == section_count - 1, fresh_cotangents[tick_number], returned
        )
    return (
        current[None],
        upstream[None],
        store[None],
        sums[0].astype(jnp.bfloat16)[None],
        sums[1].astype(jnp.bfloat16)[None],
        sums[2].astype(jnp.bfloat16)[None],
        sums[3].astype(jnp.bfloat16)[None],
        sums[4][None],
    )


def solution(mesh):
    placed = (
        P("section", None, None),
        P("section", None, None),
        P(),
        P(),
        P("section", None),
        P("section", None, "head"),
        P("section", None, "head"),
        P("section", None, "head"),
        P("section", "head", None),
        P("section", None, None, "head"),
        P(),
    )
    return jax.shard_map(
        per_device,
        mesh=mesh,
        in_specs=placed,
        out_specs=(
            P("section", None, None),
            P("section", None, None),
            P("section", None, None, "head"),
            P("section", None, "head"),
            P("section", None, "head"),
            P("section", None, "head"),
            P("section", "head", None),
            P("section", "head"),
        ),
        check_vma=False,
    )
```

profile of v0, /device:TPU:9, one launch (start us, length us, event | category | flops | bytes accessed | tf_op | source)
XLA Modules:
  0.0 480.7 jit_solution(17155322201146027762)
XLA Ops:
  15.7 3.4 fusion.161
  21.6 3.3 fusion.278
  27.0 3.5 collective-permute-start.3
  37.6 27.3 %all_gather.6 = bf16[256,1024]{0,1:T(8,128)(2,1)S(1)} all-gather(bf16[256,64]{0,1:T(8,128)(2,1)S(1)} %collective-permute-done.4), channel_id=1, replica_groups=mesh['section'=8,'head'=16] {'head'}, dimensions={1}, use_global_device_ids=true | all-gather | bytes 557056 | tf_op jit(solution)/shard_map/all_gather | solution.py:165
  65.3 3.3 fusion.116
  80.8 3.4 fusion.283
  88.3 4.4 fusion.107
  92.7 5.4 %fusion.104 = bf16[8,128,256]{2,1,0:T(8,128)(2,1)} fusion(bf16[256,8,128]{0,2,1:T(8,128)(2,1)} %bitcast.312, f32[8,256,256]{1,2,0:T(8,128)} %fusion.290, f32[8,256,256]{1,2,0:T(8,128)} %get-tuple-element.23, f32[8,256]{1,0:T(8,128)S(1)} %get-tuple-element.22), kind=kOutput, calls=%fused_computation.107 | convolution fusion | flops 138152192 | bytes 5251072 | tf_op jit(solution)/shard_map/hqk,khd->qhd/dot_general | solution.py:93
  103.8 3.4 collective-permute-start.10
  113.0 34.4 %all_gather.7 = bf16[256,1024]{0,1:T(8,128)(2,1)} all-gather(bf16[256,64]{0,1:T(8,128)(2,1)S(1)} %collective-permute-done.11), channel_id=1, replica_groups=mesh['section'=8,'head'=16] {'head'}, dimensions={1}, use_global_device_ids=true | all-gather | bytes 557056 | tf_op jit(solution)/shard_map/all_gather | solution.py:165
  148.8 3.2 fusion.119
  162.9 3.4 fusion.289
  166.2 81.2 %all-reduce.7.cloned.1.call-done = (f32[256,1024]{1,0:T(8,128)}, f32[256,1024]{1,0:T(8,128)}) async-done(((f32[256,1024]{1,0:T(8,128)}, f32[256,1024]{1,0:T(8,128)}), (f32[256,1024]{1,0:T(8,128)}, f32[256,1024]{1,0:T(8,128)})) %all-reduce.7.cloned.1.call-update) | async-done | bytes 2097168 | tf_op jit(solution)/shard_map/psum | solution.py:64
  249.1 3.2 collective-permute-start
  253.2 4.3 collective-permute-start.5
  257.5 7.8 %collective-permute-done = bf16[256,1024]{1,0:T(8,128)(2,1)S(1)} collective-permute-done((bf16[256,1024]{1,0:T(8,128)(2,1)S(1)}, bf16[256,1024]{1,0:T(8,128)(2,1)S(1)}, u32[]{:S(2)}, u32[]{:S(2)}) %collective-permute-start) | collective-permute-done | bytes 524320 | tf_op jit(solution)/shard_map/ppermute | solution.py:16
  279.3 5.2 %fusion.101 = bf16[8,128,256]{2,1,0:T(8,128)(2,1)} fusion(bf16[256,8,128]{0,2,1:T(8,128)(2,1)} %bitcast.306, f32[8,256,256]{1,2,0:T(8,128)} %fusion.291, f32[8,256,256]{1,2,0:T(8,128)} %get-tuple-element.27, f32[8,256]{1,0:T(8,128)S(1)} %get-tuple-element.26), kind=kOutput, calls=%fused_computation.106 | convolution fusion | flops 138152192 | bytes 5251072 | tf_op jit(solution)/shard_map/hqk,qhd->khd/dot_general | solution.py:97
  284.5 5.2 %fusion.98 = bf16[8,128,256]{2,1,0:T(8,128)(2,1)} fusion(bf16[256,8,128]{0,2,1:T(8,128)(2,1)} %bitcast.308, f32[8,256,256]{1,2,0:T(8,128)} %fusion.291, f32[8,256,256]{1,2,0:T(8,128)} %get-tuple-element.27, f32[8,256]{1,0:T(8,128)S(1)} %get-tuple-element.26), kind=kOutput, calls=%fused_computation.105 | convolution fusion | flops 138152192 | bytes 5251072 | tf_op jit(solution)/shard_map/hqk,khd->qhd/dot_general | solution.py:93
  291.7 3.3 fusion.284
  304.2 3.9 fusion.207
  322.2 123.9 %all-reduce.5.cloned.1.call-done = (f32[256,1024]{1,0:T(8,128)}, f32[256,1024]{1,0:T(8,128)}) async-done(((f32[256,1024]{1,0:T(8,128)}, f32[256,1024]{1,0:T(8,128)}), (f32[256,1024]{1,0:T(8,128)}, f32[256,1024]{1,0:T(8,128)})) %all-reduce.5.cloned.1.call-update) | async-done | bytes 2097168 | tf_op jit(solution)/shard_map/psum | solution.py:64
  450.1 5.4 %collective-permute-start.12 = (bf16[256,1024]{1,0:T(8,128)(2,1)}, bf16[256,1024]{1,0:T(8,128)(2,1)}, u32[]{:S(2)}, u32[]{:S(2)}) collective-permute-start(bf16[256,1024]{1,0:T(8,128)(2,1)} %fusion.177), channel_id=1, source_target_pairs={{16,0},{32,16},{48,32},{64,48},{80,64},{96,80},{112,96},{17,1},{33... | collective-permute-start | bytes 1572872 | tf_op jit(solution)/shard_map/ppermute | solution.py:16
  460.3 5.6 %collective-permute-done.12 = bf16[256,1024]{1,0:T(8,128)(2,1)} collective-permute-done((bf16[256,1024]{1,0:T(8,128)(2,1)}, bf16[256,1024]{1,0:T(8,128)(2,1)}, u32[]{:S(2)}, u32[]{:S(2)}) %collective-permute-start.12) | collective-permute-done | bytes 524320 | tf_op jit(solution)/shard_map/ppermute | solution.py:16
  467.9 3.8 collective-permute-done.1
  (195 shorter events, 110.9 us)
Async XLA Ops:
  7.2 11.9 %copy-start = (bf16[1,1024,1024]{2,1,0:T(8,128)(2,1)S(1)}, bf16[1,1024,1024]{2,1,0:T(8,128)(2,1)}, u32[]{:S(2)}) copy-start(bf16[1,1024,1024]{2,1,0:T(8,128)(2,1)} %param.17) | copy-start | bytes 6291460
  7.2 240.3 %all-reduce.7.cloned.1.call-start = ((), (), s32[]{:S(2)}) async-start(), calls=%async_computation.1 | async-start | bytes 4194304 | tf_op jit(solution)/shard_map/psum | solution.py:64
  9.3 22.9 %collective-permute-start.6 = (bf16[256,64]{0,1:T(8,128)(2,1)S(1)}, bf16[256,64]{0,1:T(8,128)(2,1)S(1)}, u32[]{:S(2)}, u32[]{:S(2)}) collective-permute-start(bf16[256,64]{0,1:T(8,128)(2,1)S(1)} %bitcast.340), channel_id=1, source_target_pairs={{0,16},{16,0},{32,48},{48,32},{64,80},{80,64},{96,112},{112,96},{1... | collective-permute-start | bytes 98312 | tf_op jit(solution)/shard_map/ppermute | solution.py:22
  14.3 12.7 %collective-permute-start.2 = (bf16[256,64]{0,1:T(8,128)(2,1)S(1)}, bf16[256,64]{0,1:T(8,128)(2,1)S(1)}, u32[]{:S(2)}, u32[]{:S(2)}) collective-permute-start(bf16[256,64]{0,1:T(8,128)(2,1)S(1)} %dynamic-slice_bitcast_fusion.1), channel_id=1, source_target_pairs={{0,16},{16,0},{32,48},{48,32},{64,80},{80,64},{96,112},{112,96},{1... | collective-permute-start | bytes 98312 | tf_op jit(solution)/shard_map/ppermute | solution.py:22
  27.0 5.2 %collective-permute-start.3 = (bf16[256,64]{0,1:T(8,128)(2,1)S(1)}, bf16[256,64]{0,1:T(8,128)(2,1)S(1)}, u32[]{:S(2)}, u32[]{:S(2)}) collective-permute-start(bf16[256,64]{0,1:T(8,128)(2,1)S(1)} %collective-permute-done.2), channel_id=1, source_target_pairs={{0,32},{16,48},{32,0},{48,16},{64,96},{80,112},{96,64},{112,80},{1... | collective-permute-start | bytes 98312 | tf_op jit(solution)/shard_map/ppermute | solution.py:22
  32.2 4.3 collective-permute-start.7
  32.3 5.4 %collective-permute-start.4 = (bf16[256,64]{0,1:T(8,128)(2,1)S(1)}, bf16[256,64]{0,1:T(8,128)(2,1)S(1)}, u32[]{:S(2)}, u32[]{:S(2)}) collective-permute-start(bf16[256,64]{0,1:T(8,128)(2,1)S(1)} %collective-permute-done.3), channel_id=1, source_target_pairs={{0,64},{16,80},{32,96},{48,112},{64,0},{80,16},{96,32},{112,48},{1... | collective-permute-start | bytes 98312 | tf_op jit(solution)/shard_map/ppermute | solution.py:22
  36.5 61.6 %collective-permute-start.8 = (bf16[256,64]{0,1:T(8,128)(2,1)S(1)}, bf16[256,64]{0,1:T(8,128)(2,1)S(1)}, u32[]{:S(2)}, u32[]{:S(2)}) collective-permute-start(bf16[256,64]{0,1:T(8,128)(2,1)S(1)} %collective-permute-done.7), channel_id=1, source_target_pairs={{0,64},{16,80},{32,96},{48,112},{64,0},{80,16},{96,32},{112,48},{1... | collective-permute-start | bytes 98312 | tf_op jit(solution)/shard_map/ppermute | solution.py:22
  98.1 5.7 %collective-permute-start.9 = (bf16[256,64]{0,1:T(8,128)(2,1)S(1)}, bf16[256,64]{0,1:T(8,128)(2,1)S(1)}, u32[]{:S(2)}, u32[]{:S(2)}) collective-permute-start(bf16[256,64]{0,1:T(8,128)(2,1)S(1)} %dynamic-slice_bitcast_fusion), channel_id=1, source_target_pairs={{0,16},{16,0},{32,48},{48,32},{64,80},{80,64},{96,112},{112,96},{1... | collective-permute-start | bytes 98312 | tf_op jit(solution)/shard_map/ppermute | solution.py:22
  103.8 5.2 %collective-permute-start.10 = (bf16[256,64]{0,1:T(8,128)(2,1)S(1)}, bf16[256,64]{0,1:T(8,128)(2,1)S(1)}, u32[]{:S(2)}, u32[]{:S(2)}) collective-permute-start(bf16[256,64]{0,1:T(8,128)(2,1)S(1)} %collective-permute-done.9), channel_id=1, source_target_pairs={{0,32},{16,48},{32,0},{48,16},{64,96},{80,112},{96,64},{112,80},{1... | collective-permute-start | bytes 98312 | tf_op jit(solution)/shard_map/ppermute | solution.py:22
  108.9 337.1 %all-reduce.5.cloned.1.call-start = ((), (), s32[]{:S(2)}) async-start(), calls=%async_computation | async-start | bytes 4194304 | tf_op jit(solution)/shard_map/psum | solution.py:64
  109.0 4.0 collective-permute-start.11
  249.1 16.3 %collective-permute-start = (bf16[256,1024]{1,0:T(8,128)(2,1)S(1)}, bf16[256,1024]{1,0:T(8,128)(2,1)S(1)}, u32[]{:S(2)}, u32[]{:S(2)}) collective-permute-start(bf16[256,1024]{1,0:T(8,128)(2,1)S(1)} %fusion.181), channel_id=1, source_target_pairs={{0,16},{16,32},{32,48},{48,64},{64,80},{80,96},{96,112},{1,17},{17... | collective-permute-start | bytes 1572872 | tf_op jit(solution)/shard_map/ppermute | solution.py:16
  252.3 13.1 %copy-start.37 = (bf16[2,256,1024]{2,1,0:T(8,128)(2,1)S(1)}, bf16[2,256,1024]{2,1,0:T(8,128)(2,1)}, u32[]{:S(2)}) copy-start(bf16[2,256,1024]{2,1,0:T(8,128)(2,1)} %param.13) | copy-start | bytes 3145732
  252.8 12.9 %copy-start.9 = (bf16[1,1024,1024]{2,1,0:T(8,128)(2,1)S(1)}, bf16[1,1024,1024]{2,1,0:T(8,128)(2,1)}, u32[]{:S(2)}) copy-start(bf16[1,1024,1024]{2,1,0:T(8,128)(2,1)} %param.16) | copy-start | bytes 6291460
  253.2 17.2 %collective-permute-start.5 = (bf16[256,1024]{1,0:T(8,128)(2,1)S(1)}, bf16[256,1024]{1,0:T(8,128)(2,1)S(1)}, u32[]{:S(2)}, u32[]{:S(2)}) collective-permute-start(bf16[256,1024]{1,0:T(8,128)(2,1)S(1)} %fusion.169), channel_id=1, source_target_pairs={{16,0},{32,16},{48,32},{64,48},{80,64},{96,80},{112,96},{17,1},{33... | collective-permute-start | bytes 1572872 | tf_op jit(solution)/shard_map/ppermute | solution.py:16
  312.6 5.0 %collective-permute-start.13 = (bf16[256,64]{1,0:T(8,128)(2,1)S(1)}, bf16[256,64]{1,0:T(8,128)(2,1)S(1)}, u32[]{:S(2)}, u32[]{:S(2)}) collective-permute-start(bf16[256,64]{1,0:T(8,128)(2,1)S(1)} %constant_dynamic-slice_fusion), channel_id=1, source_target_pairs={{0,16},{16,0},{32,48},{48,32},{64,80},{80,64},{96,112},{112,96},{1... | collective-permute-start | bytes 98312 | tf_op jit(solution)/shard_map/ppermute | solution.py:22
  317.6 4.6 collective-permute-start.14
  321.1 127.9 %copy-start.16 = (bf16[256,1024]{1,0:T(8,128)(2,1)S(1)}, bf16[256,1024]{1,0:T(8,128)(2,1)}, u32[]{:S(2)}) copy-start(bf16[256,1024]{1,0:T(8,128)(2,1)} %copy-done.15) | copy-start | bytes 1572868
  322.2 137.4 %collective-permute-start.15 = (bf16[256,64]{1,0:T(8,128)(2,1)S(1)}, bf16[256,64]{1,0:T(8,128)(2,1)S(1)}, u32[]{:S(2)}, u32[]{:S(2)}) collective-permute-start(bf16[256,64]{1,0:T(8,128)(2,1)S(1)} %collective-permute-done.14), channel_id=1, source_target_pairs={{0,64},{16,80},{32,96},{48,112},{64,0},{80,16},{96,32},{112,48},{1... | collective-permute-start | bytes 98312 | tf_op jit(solution)/shard_map/ppermute | solution.py:22
  446.1 11.4 %copy-start.39 = (bf16[8,128,256]{2,1,0:T(8,128)(2,1)S(1)}, bf16[8,128,256]{2,1,0:T(8,128)(2,1)}, u32[]{:S(2)}) copy-start(bf16[8,128,256]{2,1,0:T(8,128)(2,1)} %convolution_convert_fusion) | copy-start | bytes 1572868
  450.1 15.7 %collective-permute-start.12 = (bf16[256,1024]{1,0:T(8,128)(2,1)}, bf16[256,1024]{1,0:T(8,128)(2,1)}, u32[]{:S(2)}, u32[]{:S(2)}) collective-permute-start(bf16[256,1024]{1,0:T(8,128)(2,1)} %fusion.177), channel_id=1, source_target_pairs={{16,0},{32,16},{48,32},{64,48},{80,64},{96,80},{112,96},{17,1},{33... | collective-permute-start | bytes 1572872 | tf_op jit(solution)/shard_map/ppermute | solution.py:16
  455.6 16.1 %collective-permute-start.1 = (bf16[256,1024]{1,0:T(8,128)(2,1)}, bf16[256,1024]{1,0:T(8,128)(2,1)S(1)}, u32[]{:S(2)}, u32[]{:S(2)}) collective-permute-start(bf16[256,1024]{1,0:T(8,128)(2,1)} %fusion.187), channel_id=1, source_target_pairs={{0,16},{16,32},{32,48},{48,64},{64,80},{80,96},{96,112},{1,17},{17... | collective-permute-start | bytes 1572872 | tf_op jit(solution)/shard_map/ppermute | solution.py:16
  459.7 13.9 %copy-start.41 = (bf16[1,4,256,64]{2,3,1,0:T(8,128)(2,1)}, bf16[1,4,256,64]{2,3,1,0:T(8,128)(2,1)S(1)}, u32[]{:S(2)}) copy-start(bf16[1,4,256,64]{2,3,1,0:T(8,128)(2,1)S(1)} %constant_dynamic-update-slice_fusion) | copy-start | bytes 393220
  (39 other events, 126.0 us)
Sparse Core Ops, SparseCore 0:
  109.1 138.3 all-reduce.6
  304.3 141.7 all-reduce.4
where the time goes:
time: 489 us; the launch traced here: 481 us
  waiting for transfers between devices  224 us (46%)
  matrix products  106 us (22%)
  blocking collectives  61.7 us (13%)
  starting transfers between devices  29 us (6%)
  local copies, waits for them, and re-layouts  28.2 us (6%)
  between operations  18.7 us (4%)
  other arithmetic  13 us (3%)
    psum x2, waiting for transfers between devices, ahead(): total = lax.psum(partial_value, 'head')  205 us
    all_gather x2, blocking collectives, per_device(): restored = lax.all_gather(reloaded, 'head', axis=1, tiled=True)  61.7 us
    reshape x10, local copies, waits for them, and re-layouts, split_heads(): return rows.reshape(rows.shape[0], -1, DK)  17.7 us
    ppermute x4, waiting for transfers between devices, passed_along(): return lax.ppermute(value, axis, pairs)  17.2 us
    ppermute x4, starting transfers between devices, passed_along(): return lax.ppermute(value, axis, pairs)  14.9 us
    ppermute x12, starting transfers between devices, swapped(): return lax.ppermute(value, axis, pairs)  14.1 us
    sub x4, matrix products, attend(): exponent = jnp.exp(scores - highest)  13.3 us
    dot_general x2, matrix products, behind(): jnp.einsum('hqk,khd->qhd', score_grad, split_heads(key_rows), preferred_e...  10.5 us
  transfers between devices with their start and end apart: 18, of which 7 were waited for; matrix products, arithmetic and copies ran while one was open for 22% of the time, Pallas kernels for 0%

commit v1 on v0

v1 whole, which is shorter than its diff:
```python
import jax
import jax.numpy as jnp
from jax import lax
from jax.experimental import pallas as pl
from jax.experimental.pallas import tpu as pltpu
from jax.sharding import PartitionSpec as P

DK = 128
TICKS = 2
SCALE = DK ** (-0.5)
EPSILON = 1e-06
BF16 = jnp.bfloat16
F32 = jnp.float32
NT = (((1,), (1,)), ((), ()))
TN = (((0,), (0,)), ((), ()))
PAIR = 2 * DK
MIB = 1024 * 1024


def dot(a, b):
    return jnp.dot(a, b, preferred_element_type=F32)


def dot_nt(a, b):
    return lax.dot_general(a, b, NT, preferred_element_type=F32)


def dot_tn(a, b):
    return lax.dot_general(a, b, TN, preferred_element_type=F32)


def normalize(rows, gain_row):
    floats = rows.astype(F32)
    inverse = lax.rsqrt(jnp.mean(floats * floats, axis=-1, keepdims=True) + EPSILON)
    unit_rows = floats * inverse
    return unit_rows * gain_row, unit_rows, inverse


def softmax(queries, key_rows):
    scores = dot_nt(queries, key_rows) * SCALE
    exponent = jnp.exp(scores - jnp.max(scores, axis=-1, keepdims=True))
    return exponent * (1.0 / jnp.sum(exponent, axis=-1, keepdims=True))


def split_out(core, total, keep_ref, send_ref):
    half = keep_ref.shape[0]
    keep_ref[...] = total[pl.ds(pl.multiple_of(core * half, half), half), :]
    send_ref[...] = total[pl.ds(pl.multiple_of((1 - core) * half, half), half), :].astype(BF16)


def forward_kernel(core_ref, rows_ref, gain_ref, wq, wk, wv, wo, keep_ref, send_ref, normed, total):
    step = pl.program_id(0)

    @pl.when(step == 0)
    def _():
        normed[...] = normalize(rows_ref[...], gain_ref[...])[0].astype(BF16)
        total[...] = jnp.zeros_like(total)

    n = normed[...]
    queries = dot(n, wq[...]).astype(BF16)
    key_rows = dot(n, wk[...]).astype(BF16)
    value_rows = dot(n, wv[...]).astype(BF16)
    parts = []
    for i in range(2):
        at = slice(i * DK, (i + 1) * DK)
        low = softmax(queries[:, at], key_rows[:, at]).astype(BF16)
        parts.append(dot(low, value_rows[:, at]).astype(BF16))
    total[...] += dot(jnp.concatenate(parts, axis=1), wo[...])

    @pl.when(step == pl.num_programs(0) - 1)
    def _():
        split_out(core_ref[0], total, keep_ref, send_ref)


def whole(shape):
    return pl.BlockSpec(shape, lambda i: (0,) * len(shape))


def columns(rows):
    return pl.BlockSpec((rows, PAIR), lambda i: (0, i))


def rows_of(cols):
    return pl.BlockSpec((PAIR, cols), lambda i: (i, 0))


SMEM = pl.BlockSpec(memory_space=pltpu.SMEM)


def params(limit):
    return pltpu.CompilerParams(
        dimension_semantics=("arbitrary",), vmem_limit_bytes=limit * MIB
    )


def forward_partial(core, rows, gain, wq, wk, wv, wo):
    tokens, width = rows.shape
    inner = wq.shape[1]
    return pl.pallas_call(
        forward_kernel,
        grid=(inner // PAIR,),
        in_specs=[SMEM, whole((tokens, width)), whole((1, width))]
        + [columns(width)] * 3
        + [rows_of(width)],
        out_specs=[whole((tokens // 2, width))] * 2,
        out_shape=[
            jax.ShapeDtypeStruct((tokens // 2, width), F32),
            jax.ShapeDtypeStruct((tokens // 2, width), BF16),
        ],
        scratch_shapes=[pltpu.VMEM((tokens, width), BF16), pltpu.VMEM((tokens, width), F32)],
        compiler_params=params(24),
        cost_estimate=pl.CostEstimate(
            flops=8 * tokens * width * inner, bytes_accessed=8 * width * inner, transcendentals=0
        ),
        name="forward_part",
    )(core, rows, gain, wq, wk, wv, wo)


def recompute_kernel(
    place_ref, mine_ref, other_ref, gain_ref, wq, wk, wv,
    block_ref, normed_t_ref, q_ref, k_ref, v_ref, soft_ref, context_ref, block_t, normed,
):
    step = pl.program_id(0)

    @pl.when(step == 0)
    def _():
        core, high, column = place_ref[0], place_ref[1], place_ref[2]
        share = mine_ref.shape[1]
        for j in range(4):
            for i in range(2):
                head = (column ^ j) * 4 + (high ^ i) * 2
                for ref, c in ((mine_ref, core), (other_ref, 1 - core)):
                    at = pl.multiple_of((head + c) * share, share)
                    block_t[pl.ds(at, share), :] = ref[2 * j + i]
        block = block_t[...].T
        block_ref[...] = block
        n = normalize(block, gain_ref[...])[0].astype(BF16)
        normed[...] = n
        normed_t_ref[...] = n.T

    n = normed[...]
    queries = dot(n, wq[...]).astype(BF16)
    key_rows = dot(n, wk[...]).astype(BF16)
    value_rows = dot(n, wv[...]).astype(BF16)
    q_ref[...] = queries
    k_ref[...] = key_rows
    v_ref[...] = value_rows
    for i in range(2):
        at = slice(i * DK, (i + 1) * DK)
        rows = softmax(queries[:, at], key_rows[:, at])
        soft_ref[i] = rows
        context_ref[:, at] = dot(rows.astype(BF16), value_rows[:, at]).astype(BF16)


def recompute(place, mine, other, gain, wq, wk, wv):
    pieces, share, tokens = mine.shape
    width, inner = wq.shape
    heads = inner // DK
    flat = jax.ShapeDtypeStruct((tokens, inner), BF16)
    return pl.pallas_call(
        recompute_kernel,
        grid=(inner // PAIR,),
        in_specs=[SMEM, whole(mine.shape), whole(mine.shape), whole((1, width))]
        + [columns(width)] * 3,
        out_specs=[
            whole((tokens, width)),
            whole((width, tokens)),
            columns(tokens),
            columns(tokens),
            columns(tokens),
            pl.BlockSpec((2, tokens, tokens), lambda i: (i, 0, 0)),
            columns(tokens),
        ],
        out_shape=[
            jax.ShapeDtypeStruct((tokens, width), BF16),
            jax.ShapeDtypeStruct((width, tokens), BF16),
            flat,
            flat,
            flat,
            jax.ShapeDtypeStruct((heads, tokens, tokens), F32),
            flat,
        ],
        scratch_shapes=[pltpu.VMEM((width, tokens), BF16), pltpu.VMEM((tokens, width), BF16)],
        compiler_params=params(24),
        cost_estimate=pl.CostEstimate(
            flops=7 * tokens * width * inner, bytes_accessed=6 * width * inner, transcendentals=0
        ),
        name="recompute_part",
    )(place, mine, other, gain, wq, wk, wv)


def backward_kernel(
    core_ref, g_ref, q_ref, k_ref, v_ref, soft_ref, wq, wk, wv, wo,
    keep_ref, send_ref, qg_ref, kg_ref, vg_ref, total,
):
    step = pl.program_id(0)

    @pl.when(step == 0)
    def _():
        total[...] = jnp.zeros_like(total)

    grads = dot_nt(g_ref[...], wo[...]).astype(BF16)
    for i in range(2):
        at = slice(i * DK, (i + 1) * DK)
        rows = soft_ref[i]
        grad = grads[:, at]
        soft_grad = dot_nt(grad, v_ref[:, at])
        vg_ref[:, at] = dot_tn(rows.astype(BF16), grad).astype(BF16)
        along = jnp.sum(rows * soft_grad, axis=-1, keepdims=True)
        score_grad = (rows * (soft_grad - along) * SCALE).astype(BF16)
        qg_ref[:, at] = dot(score_grad, k_ref[:, at]).astype(BF16)
        kg_ref[:, at] = dot_tn(score_grad, q_ref[:, at]).astype(BF16)
    total[...] += (
        dot_nt(qg_ref[...], wq[...]) + dot_nt(kg_ref[...], wk[...]) + dot_nt(vg_ref[...], wv[...])
    )

    @pl.when(step == pl.num_programs(0) - 1)
    def _():
        split_out(core_ref[0], total, keep_ref, send_ref)


def backward_partial(core, g, q, k, v, soft, wq, wk, wv, wo):
    tokens, width = g.shape
    inner = wq.shape[1]
    flat = jax.ShapeDtypeStruct((tokens, inner), BF16)
    return pl.pallas_call(
        backward_kernel,
        grid=(inner // PAIR,),
        in_specs=[SMEM, whole((tokens, width))]
        + [columns(tokens)] * 3
        + [pl.BlockSpec((2, tokens, tokens), lambda i: (i, 0, 0))]
        + [columns(width)] * 3
        + [rows_of(width)],
        out_specs=[whole((tokens // 2, width))] * 2 + [columns(tokens)] * 3,
        out_shape=[
            jax.ShapeDtypeStruct((tokens // 2, width), F32),
            jax.ShapeDtypeStruct((tokens // 2, width), BF16),
            flat,
            flat,
            flat,
        ],
        scratch_shapes=[pltpu.VMEM((tokens, width), F32)],
        compiler_params=params(24),
        cost_estimate=pl.CostEstimate(
            flops=9 * tokens * width * inner, bytes_accessed=10 * width * inner, transcendentals=0
        ),
        name="backward_part",
    )(core, g, q, k, v, soft, wq, wk, wv, wo)


def weight_kernel(n0, n1, q0, q1, k0, k1, v0, v1, c0, c1, g0, g1, dq, dk, dv, do):
    for a0, a1, out in ((q0, q1, dq), (k0, k1, dk), (v0, v1, dv)):
        out[...] = (dot(n0[...], a0[...]) + dot(n1[...], a1[...])).astype(BF16)
    do[...] = (dot_tn(c0[...], g0[...]) + dot_tn(c1[...], g1[...])).astype(BF16)


def weight_grads(normed_t, q, k, v, context, g):
    width, tokens = normed_t[0].shape
    inner = q[0].shape[1]
    flat = jax.ShapeDtypeStruct((width, inner), BF16)
    return pl.pallas_call(
        weight_kernel,
        grid=(inner // PAIR,),
        in_specs=[whole((width, tokens))] * 2 + [columns(tokens)] * 8 + [whole((tokens, width))] * 2,
        out_specs=[columns(width)] * 3 + [rows_of(width)],
        out_shape=[flat, flat, flat, jax.ShapeDtypeStruct((inner, width), BF16)],
        compiler_params=params(24),
        cost_estimate=pl.CostEstimate(
            flops=16 * tokens * width * inner, bytes_accessed=8 * width * inner, transcendentals=0
        ),
        name="weight_part",
    )(*normed_t, *q, *k, *v, *context, *g)


class Moves:
    def __init__(self, sections, heads):
        self.sections, self.heads = sections, heads

    def send(self, value, to):
        pairs = []
        for s in range(self.sections):
            for h in range(self.heads):
                t, k = to(s, h)
                if 0 <= t < self.sections:
                    pairs.append((s * self.heads + h, t * self.heads + k))
        return lax.ppermute(value, ("section", "head"), pairs)

    def flip(self, value, mask):
        return self.send(value, lambda s, h: (s, h ^ mask))

    def shift(self, value, by, mask):
        return self.send(value, lambda s, h: (s + by, h ^ mask))

    def mirror(self, value, mask):
        return self.send(value, lambda s, h: (self.sections - 1 - s, h ^ mask))


def ordered(pieces, column):
    p = list(pieces)
    low, high = (column & 1) == 1, (column & 2) == 2
    p = [jnp.where(low, p[j ^ 1], p[j]) for j in range(4)]
    p = [jnp.where(high, p[j ^ 2], p[j]) for j in range(4)]
    return jnp.concatenate(p, axis=0)


def per_device(
    section_inputs, section_cotangents, fresh_tokens, fresh_cotangents, norm_gain,
    query_weight, key_weight, value_weight, out_weight, saved_inputs, reload_slot,
):
    sections, heads = lax.axis_size("section"), lax.axis_size("head")
    section, head = lax.axis_index("section"), lax.axis_index("head")
    moves = Moves(sections, heads)
    core, high, column = head & 1, (head >> 1) & 1, head >> 2
    mirror = sections - 1 - section
    share = saved_inputs.shape[3]
    core_at = core.astype(jnp.int32)[None]
    place = jnp.stack([core, high, column]).astype(jnp.int32)
    gain = norm_gain
    wq, wk, wv, wo = query_weight[0], key_weight[0], value_weight[0], out_weight[0]
    store = jnp.swapaxes(saved_inputs[0], 1, 2)
    tokens, width = section_inputs.shape[1:]
    rows = tokens // 8
    row_at = core * (tokens // 2) + column * rows

    def share_of(block):
        return lax.dynamic_slice_in_dim(block, head * share, share, 1).T

    def take_rows(block):
        return lax.dynamic_slice_in_dim(block, row_at, rows, 0)

    def scatter_sum(keep, send):
        got = moves.flip(send, 1)
        mine = keep + got.astype(F32)
        low = mine.astype(BF16)
        parts = []
        for j in (1, 2, 3):
            piece = lax.dynamic_slice_in_dim(low, (column ^ j) * rows, rows, 0)
            parts.append(moves.flip(piece, 4 * j))
        own = lax.dynamic_slice_in_dim(mine, column * rows, rows, 0)
        return own + (parts[0].astype(F32) + (parts[1].astype(F32) + parts[2].astype(F32)))

    def pass_on(value, by):
        low = value.astype(BF16)
        first = moves.shift(low, by, 0)
        second = moves.shift(low, by, 2)
        return (first.astype(F32) + second.astype(F32)).astype(BF16)

    def gather_rows(piece):
        pieces = [piece] + [moves.flip(piece, 4 * j) for j in (1, 2, 3)]
        mine = ordered(pieces, column)
        other = moves.flip(mine, 1)
        return jnp.concatenate(
            [jnp.where(core == 0, mine, other), jnp.where(core == 0, other, mine)], axis=0
        )

    def gather_shares(mine, far):
        both = jnp.stack([mine, far])
        pieces = [both] + [moves.flip(both, 4 * j) for j in (1, 2, 3)]
        mine = jnp.concatenate(pieces, axis=0)
        return mine, moves.flip(mine, 1)

    slot_here = [lax.dynamic_index_in_dim(reload_slot[t], section, 0, keepdims=False) for t in range(TICKS)]
    slot_there = [lax.dynamic_index_in_dim(reload_slot[t], mirror, 0, keepdims=False) for t in range(TICKS)]
    current, upstream = section_inputs[0], section_cotangents[0]

    held = [lax.dynamic_index_in_dim(store, slot_there[t], 0, keepdims=False) for t in range(TICKS)]
    same = slot_here[0] == slot_here[1]
    own_first = share_of(current)
    going = jnp.stack([held[0], held[1], own_first])
    near = moves.mirror(going, 0)
    far_first = moves.mirror(going[:2], 2)
    pair_first = moves.flip(own_first, 2)
    store = lax.dynamic_update_index_in_dim(store, near[2], slot_there[0], 0)
    reload = [
        gather_shares(near[0], far_first[0]),
        gather_shares(
            jnp.where(same, own_first, near[1]), jnp.where(same, pair_first, far_first[1])
        ),
    ]

    contexts, normed_ts, qgs, kgs, vgs, gs = [], [], [], [], [], []
    gain_sum = 0.0
    for t in range(TICKS):
        keep, send = forward_partial(core_at, current, gain, wq, wk, wv, wo)
        block, normed_t, q, k, v, soft, context = recompute(place, *reload[t], gain, wq, wk, wv)
        back_keep, back_send, qg, kg, vg = backward_partial(
            core_at, upstream, q, k, v, soft, wq, wk, wv, wo
        )
        contexts.append(context)
        normed_ts.append(normed_t)
        qgs.append(qg)
        kgs.append(kg)
        vgs.append(vg)
        gs.append(upstream)

        ahead = scatter_sum(keep, send)
        ahead = ahead + jnp.where(high == 0, take_rows(current).astype(F32), 0.0)
        ahead = pass_on(ahead, 1)
        ahead = jnp.where(section == 0, take_rows(fresh_tokens[t]), ahead)
        current = gather_rows(ahead)

        normed_grad = scatter_sum(back_keep, back_send)
        _, unit, inverse = normalize(take_rows(block), gain)
        gain_sum = gain_sum + jnp.sum(normed_grad * unit, axis=0)
        unit_grad = normed_grad * gain
        along = jnp.mean(unit_grad * unit, axis=-1, keepdims=True)
        back = jnp.where(high == 0, take_rows(upstream).astype(F32), 0.0)
        back = back + inverse * (unit_grad - unit * along)
        back = pass_on(back, -1)
        back = jnp.where(section == sections - 1, take_rows(fresh_cotangents[t]), back)
        upstream = gather_rows(back)
        if t == 0:
            arrived = moves.mirror(share_of(current), 0)
            store = lax.dynamic_update_index_in_dim(store, arrived, slot_there[1], 0)

    grads = weight_grads(normed_ts, qgs, kgs, vgs, contexts, gs)
    gain_grad = jnp.sum(lax.all_to_all(gain_sum.reshape(heads, share), "head", 0, 0), axis=0)
    return (
        current[None],
        upstream[None],
        jnp.swapaxes(store, 1, 2)[None],
        grads[0][None],
        grads[1][None],
        grads[2][None],
        grads[3][None],
        gain_grad[None],
    )


def solution(mesh):
    placed = (
        P("section", None, None),
        P("section", None, None),
        P(),
        P(),
        P("section", None),
        P("section", None, "head"),
        P("section", None, "head"),
        P("section", None, "head"),
        P("section", "head", None),
        P("section", None, None, "head"),
        P(),
    )
    return jax.shard_map(
        per_device,
        mesh=mesh,
        in_specs=placed,
        out_specs=(
            P("section", None, None),
            P("section", None, None),
            P("section", None, None, "head"),
            P("section", None, "head"),
            P("section", None, "head"),
            P("section", None, "head"),
            P("section", "head", None),
            P("section", "head"),
        ),
        check_vma=False,
    )
```

time: 489 us -> 232 us (0.47); the launches traced: 481 us -> 229 us
  waiting for transfers between devices: 224 us -> 22.9 us
  matrix products: 106 us -> 0 us
  starting transfers between devices: 29 us -> 104 us
  blocking collectives: 61.7 us -> 0 us
  Pallas kernels: 0 us -> 53.9 us
  between operations: 18.7 us -> 6.69 us
    psum x2 -> x0, waiting for transfers between devices: 205 us -> none  [ahead(): total = lax.psum(partial_value, 'head')]
    dot_general x42 -> x0, matrix products: 92.9 us -> none  [the longest x2 10.5 us: behind(): jnp.einsum('hqk,khd->qhd', score_grad, split_heads(key_rows), preferred_e...]
    ppermute x16 -> x52, starting transfers between devices: 28.9 us -> 99.4 us  [send(): return lax.ppermute(value, ('section', 'head'), pairs)]
    all_gather x2 -> x0, blocking collectives: 61.7 us -> none  [per_device(): restored = lax.all_gather(reloaded, 'head', axis=1, tiled=True)]
    pallas_call x0 -> x7, Pallas kernels: none -> 53.9 us  [the longest x2 17.3 us: backward_partial(): pl.pallas_call(backward_kernel, grid=(inner // PAIR,), in_specs=[SMEM, wh...]
    reshape x10 -> x0, local copies, waits for them, and re-layouts: 17.7 us -> none  [split_heads(): return rows.reshape(rows.shape[0], -1, DK)]
    sub x4 -> x0, matrix products: 13.3 us -> none  [attend(): exponent = jnp.exp(scores - highest)]
    unnamed x91 -> x93, local copies, waits for them, and re-layouts: 5.19 us -> 16.6 us
  transfers between devices with their start and end apart: 18 -> 53, of which waited for: 7 -> 12; matrix products, arithmetic and copies ran while one was open for 22% -> 10% of each run, Pallas kernels for 0% -> 23%
where the time goes in v1:
time: 232 us; the launch traced here: 229 us
  starting transfers between devices  104 us (45%)
  Pallas kernels  53.9 us (23%)
  local copies, waits for them, and re-layouts  24.5 us (11%)
  waiting for transfers between devices  22.9 us (10%)
  other arithmetic  17 us (7%)
  between operations  6.69 us (3%)
    ppermute x52, starting transfers between devices, send(): return lax.ppermute(value, ('section', 'head'), pairs)  99.4 us
    pallas_call x2, Pallas kernels, backward_partial(): pl.pallas_call(backward_kernel, grid=(inner // PAIR,), in_specs=[SMEM, wh...  17.3 us
    ppermute x52, waiting for transfers between devices, send(): return lax.ppermute(value, ('section', 'head'), pairs)  16.9 us
    unnamed x93, local copies, waits for them, and re-layouts  16.6 us
    pallas_call x2, Pallas kernels, recompute(): pl.pallas_call(recompute_kernel, grid=(inner // PAIR,), in_specs=[SMEM, w...  14.9 us
    pallas_call x2, Pallas kernels, forward_partial(): pl.pallas_call(forward_kernel, grid=(inner // PAIR,), in_specs=[SMEM, who...  14.8 us
    pallas_call x1, Pallas kernels, weight_grads(): pl.pallas_call(weight_kernel, grid=(inner // PAIR,), in_specs=[whole((wid...  6.81 us
    all_to_all x1, waiting for transfers between devices, per_device(): lax.all_to_all(gain_sum.reshape(heads, share), 'head', 0, 0)  6.09 us
  transfers between devices with their start and end apart: 53, of which 12 were waited for; matrix products, arithmetic and copies ran while one was open for 10% of the time, Pallas kernels for 23%

profile of v1, /device:TPU:9, one launch (start us, length us, event | category | flops | bytes accessed | tf_op | source)
XLA Modules:
  0.0 229.3 jit_solution(2851472590899937849)
XLA Ops:
  10.6 2.8 %collective-permute-start.21 = (bf16[2,64,256]{2,1,0:T(8,128)(2,1)}, bf16[2,64,256]{2,1,0:T(8,128)(2,1)}, u32[]{:S(2)}, u32[]{:S(2)}) collective-permute-start(bf16[2,64,256]{2,1,0:T(8,128)(2,1)} %pad_maximum_fusion.7), channel_id=1, source_target_pairs={{0,114},{1,115},{2,112},{3,113},{4,118},{5,119},{6,116},{7,117},{8... | collective-permute-start | bytes 196616 | tf_op jit(solution)/shard_map/ppermute | solution.py:286
  23.3 7.4 %forward_part.2 = (f32[128,1024]{1,0:T(8,128)S(1)}, bf16[128,1024]{1,0:T(8,128)(2,1)S(1)}) custom-call(s32[1]{0:T(128)} %bitcast.1.core_ref, bf16[256,1024]{1,0:T(8,128)(2,1)S(1)} %bitcast.103, f32[1,1024]{1,0:T(1,128)S(1)} %copy-done.20, bf16[1024,1024]{1,0:T(8,128)(2,1)S(1)} %bitcast.81, bf16[1024,1024]{1,0:T(8,128)(2,1)S(1)} %bitcast.87, ...), custom_call_target="tpu_custom_call" | custom-call | flops 2147483648 | bytes 8388608 | tf_op jit(solution)/shard_map/forward_part/pallas_call | solution.py:99
  44.9 3.3 %collective-permute-done.23 = bf16[2,64,256]{2,1,0:T(8,128)(2,1)S(1)} collective-permute-done((bf16[2,64,256]{2,1,0:T(8,128)(2,1)S(1)}, bf16[2,64,256]{2,1,0:T(8,128)(2,1)S(1)}, u32[]{:S(2)}, u32[]{:S(2)}) %collective-permute-start.23) | collective-permute-done | bytes 65568 | tf_op jit(solution)/shard_map/ppermute | solution.py:286
  49.4 3.1 %collective-permute-done.24 = bf16[2,64,256]{2,1,0:T(8,128)(2,1)S(1)} collective-permute-done((bf16[2,64,256]{2,1,0:T(8,128)(2,1)S(1)}, bf16[2,64,256]{2,1,0:T(8,128)(2,1)S(1)}, u32[]{:S(2)}, u32[]{:S(2)}) %collective-permute-start.24) | collective-permute-done | bytes 65568 | tf_op jit(solution)/shard_map/ppermute | solution.py:286
  52.5 3.0 %collective-permute-start.25 = (bf16[8,64,256]{2,1,0:T(8,128)(2,1)S(1)}, bf16[8,64,256]{2,1,0:T(8,128)(2,1)S(1)}, u32[]{:S(2)}, u32[]{:S(2)}) collective-permute-start(bf16[8,64,256]{2,1,0:T(8,128)(2,1)S(1)} %constant_dynamic-update-slice_fusion.mine_ref), channel_id=1, source_target_pairs={{0,1},{1,0},{2,3},{3,2},{4,5},{5,4},{6,7},{7,6},{8,9},{9,8},{10,11... | collective-permute-start | bytes 786440 | tf_op jit(solution)/shard_map/ppermute | solution.py:286
  63.9 3.0 %collective-permute-start.5 = (bf16[32,1024]{1,0:T(8,128)(2,1)S(1)}, bf16[32,1024]{1,0:T(8,128)(2,1)S(1)}, u32[]{:S(2)}, u32[]{:S(2)}) collective-permute-start(bf16[32,1024]{1,0:T(8,128)(2,1)S(1)} %fusion.20), channel_id=1, source_target_pairs={{0,18},{1,19},{2,16},{3,17},{4,22},{5,23},{6,20},{7,21},{8,26},{9,... | collective-permute-start | bytes 196616 | tf_op jit(solution)/shard_map/ppermute | solution.py:286
  66.8 3.1 %collective-permute-start.4 = (bf16[32,1024]{1,0:T(8,128)(2,1)S(1)}, bf16[32,1024]{1,0:T(8,128)(2,1)S(1)}, u32[]{:S(2)}, u32[]{:S(2)}) collective-permute-start(bf16[32,1024]{1,0:T(8,128)(2,1)S(1)} %fusion.20), channel_id=1, source_target_pairs={{0,16},{1,17},{2,18},{3,19},{4,20},{5,21},{6,22},{7,23},{8,24},{9,... | collective-permute-start | bytes 196616 | tf_op jit(solution)/shard_map/ppermute | solution.py:286
  79.8 7.5 %recompute_part.2 = (bf16[256,1024]{1,0:T(8,128)(2,1)S(1)}, bf16[1024,256]{1,0:T(8,128)(2,1)S(1)}, bf16[256,1024]{1,0:T(8,128)(2,1)S(1)}, bf16[256,1024]{1,0:T(8...) custom-call(s32[3]{0:T(128)S(1)} %pad_add_fusion.place_ref, ...), custom_call_target="tpu_custom_call" | custom-call | flops 1879048192 | bytes 6291456 | tf_op jit(solution)/shard_map/recompute_part/pallas_call | solution.py:160
  87.3 8.6 %backward_part.2 = (f32[128,1024]{1,0:T(8,128)S(1)}, bf16[128,1024]{1,0:T(8,128)(2,1)S(1)}, bf16[256,1024]{1,0:T(8,128)(2,1)S(1)}, bf16[256,1024]{1,0:T(8,128)(2,1)S(1)}, bf16[256,1024]{1,0:T(8,128)(2,1)S(1)}) custom-call(s32[1]{0:T(128)} %bitcast.1.core_ref, bf16[256,1024]{1,0:T(8,128)(2,1)S(1)} %bitcast.104, ...), custom_call_target="tpu_custom_call" | custom-call | flops 2415919104 | bytes 10485760 | tf_op jit(solution)/shard_map/backward_part/pallas_call | solution.py:226
  96.0 3.7 %collective-permute-start.26 = (bf16[128,1024]{1,0:T(8,128)(2,1)S(1)}, bf16[128,1024]{1,0:T(8,128)(2,1)S(1)}, u32[]{:S(2)}, u32[]{:S(2)}) collective-permute-start(bf16[128,1024]{1,0:T(8,128)(2,1)S(1)} %get-tuple-element.50), channel_id=1, source_target_pairs={{0,1},{1,0},{2,3},{3,2},{4,5},{5,4},{6,7},{7,6},{8,9},{9,8},{10,11... | collective-permute-start | bytes 786440 | tf_op jit(solution)/shard_map/ppermute | solution.py:286
  99.9 7.5 %recompute_part.3 = (bf16[256,1024]{1,0:T(8,128)(2,1)S(1)}, bf16[1024,256]{1,0:T(8,128)(2,1)S(1)}, bf16[256,1024]{1,0:T(8,128)(2,1)S(1)}, bf16[256,1024]{1,0:T(8...) custom-call(s32[3]{0:T(128)S(1)} %pad_add_fusion.place_ref, ...), custom_call_target="tpu_custom_call" | custom-call | flops 1879048192 | bytes 6291456 | tf_op jit(solution)/shard_map/recompute_part/pallas_call | solution.py:160
  114.5 3.5 %collective-permute-start.31 = (bf16[32,1024]{1,0:T(8,128)(2,1)S(1)}, bf16[32,1024]{1,0:T(8,128)(2,1)S(1)}, u32[]{:S(2)}, u32[]{:S(2)}) collective-permute-start(bf16[32,1024]{1,0:T(8,128)(2,1)S(1)} %fusion.10), channel_id=1, source_target_pairs={{16,2},{17,3},{18,0},{19,1},{20,6},{21,7},{22,4},{23,5},{24,10},{2... | collective-permute-start | bytes 196616 | tf_op jit(solution)/shard_map/ppermute | solution.py:286
  118.0 2.9 %collective-permute-start.30 = (bf16[32,1024]{1,0:T(8,128)(2,1)S(1)}, bf16[32,1024]{1,0:T(8,128)(2,1)S(1)}, u32[]{:S(2)}, u32[]{:S(2)}) collective-permute-start(bf16[32,1024]{1,0:T(8,128)(2,1)S(1)} %fusion.10), channel_id=1, source_target_pairs={{16,0},{17,1},{18,2},{19,3},{20,4},{21,5},{22,6},{23,7},{24,8},{25... | collective-permute-start | bytes 196616 | tf_op jit(solution)/shard_map/ppermute | solution.py:286
  127.8 7.4 %forward_part.3 = (f32[128,1024]{1,0:T(8,128)S(1)}, bf16[128,1024]{1,0:T(8,128)(2,1)S(1)}) custom-call(s32[1]{0:T(128)} %bitcast.1.core_ref, bf16[256,1024]{1,0:T(8,128)(2,1)S(1)} %pad_maximum_fusion.rows_ref, f32[1,1024]{1,0:T(1,128)S(1)} %copy-done.21, bf16[1024,1024]{1,0:T(8,128)(2,1)S(1)} %bitcast.85, bf16[1024,1024]{1,0:T(8,128)(2,1)S(1)} %bitcast.91, ...), custom_call_target="tpu_custom_call" | custom-call | flops 2147483648 | bytes 8388608 | tf_op jit(solution)/shard_map/forward_part/pallas_call | solution.py:99
  135.2 4.1 %collective-permute-start.10 = (bf16[128,1024]{1,0:T(8,128)(2,1)S(1)}, bf16[128,1024]{1,0:T(8,128)(2,1)S(1)}, u32[]{:S(2)}, u32[]{:S(2)}) collective-permute-start(bf16[128,1024]{1,0:T(8,128)(2,1)S(1)} %get-tuple-element.43), channel_id=1, source_target_pairs={{0,1},{1,0},{2,3},{3,2},{4,5},{5,4},{6,7},{7,6},{8,9},{9,8},{10,11... | collective-permute-start | bytes 786440 | tf_op jit(solution)/shard_map/ppermute | solution.py:286
  149.6 4.0 %collective-permute-start.15 = (bf16[32,1024]{1,0:T(8,128)(2,1)S(1)}, bf16[32,1024]{1,0:T(8,128)(2,1)S(1)}, u32[]{:S(2)}, u32[]{:S(2)}) collective-permute-start(bf16[32,1024]{1,0:T(8,128)(2,1)S(1)} %add_convert_fusion.3), channel_id=1, source_target_pairs={{0,18},{1,19},{2,16},{3,17},{4,22},{5,23},{6,20},{7,21},{8,26},{9,... | collective-permute-start | bytes 196616 | tf_op jit(solution)/shard_map/ppermute | solution.py:286
  163.4 8.6 %backward_part.3 = (f32[128,1024]{1,0:T(8,128)S(1)}, bf16[128,1024]{1,0:T(8,128)(2,1)S(1)}, bf16[256,1024]{1,0:T(8,128)(2,1)S(1)}, bf16[256,1024]{1,0:T(8,128)(2,1)S(1)}, bf16[256,1024]{1,0:T(8,128)(2,1)S(1)}) custom-call(s32[1]{0:T(128)} %bitcast.1.core_ref, bf16[256,1024]{1,0:T(8,128)(2,1)S(1)} %pad_maximum_fusion.1.g_ref.g1, ...), custom_call_target="tpu_custom_call" | custom-call | flops 2415919104 | bytes 10485760 | tf_op jit(solution)/shard_map/backward_part/pallas_call | solution.py:226
  182.2 6.8 %weight_part.1 = (bf16[1024,1024]{1,0:T(8,128)(2,1)}, bf16[1024,1024]{1,0:T(8,128)(2,1)}, bf16[1024,1024]{1,0:T(8,128)(2,1)}, bf16[1024,1024]{1,0:T(8,128)(2,1)}) custom-call(bf16[1024,256]{1,0:T(8,128)(2,1)S(1)} %copy-done.30, bf16[1024,256]{1,0:T(8,128)(2,1)S(1)} %copy-done.34, bf16[256,1024]{1,0:T(8,128)(2,1)S(1)} %copy-done.24, ...), custom_call_target="tpu_custom_call" | custom-call | flops 4294967296 | bytes 8388608 | tf_op jit(solution)/shard_map/weight_part/pallas_call | solution.py:261
  192.2 5.4 %collective-permute-start.46 = (bf16[32,1024]{1,0:T(8,128)(2,1)S(1)}, bf16[32,1024]{1,0:T(8,128)(2,1)S(1)}, u32[]{:S(2)}, u32[]{:S(2)}) collective-permute-start(bf16[32,1024]{1,0:T(8,128)(2,1)S(1)} %fusion.17), channel_id=1, source_target_pairs={{16,2},{17,3},{18,0},{19,1},{20,6},{21,7},{22,4},{23,5},{24,10},{2... | collective-permute-start | bytes 196616 | tf_op jit(solution)/shard_map/ppermute | solution.py:286
  197.6 3.9 %collective-permute-start.45 = (bf16[32,1024]{1,0:T(8,128)(2,1)S(1)}, bf16[32,1024]{1,0:T(8,128)(2,1)S(1)}, u32[]{:S(2)}, u32[]{:S(2)}) collective-permute-start(bf16[32,1024]{1,0:T(8,128)(2,1)S(1)} %fusion.17), channel_id=1, source_target_pairs={{16,0},{17,1},{18,2},{19,3},{20,4},{21,5},{22,6},{23,7},{24,8},{25... | collective-permute-start | bytes 196616 | tf_op jit(solution)/shard_map/ppermute | solution.py:286
  207.7 3.9 %collective-permute-start.19 = (bf16[128,1024]{1,0:T(8,128)(2,1)S(1)}, bf16[128,1024]{1,0:T(8,128)(2,1)S(1)}, u32[]{:S(2)}, u32[]{:S(2)}) collective-permute-start(bf16[128,1024]{1,0:T(8,128)(2,1)S(1)} %pad_maximum_fusion.3), channel_id=1, source_target_pairs={{0,1},{1,0},{2,3},{3,2},{4,5},{5,4},{6,7},{7,6},{8,9},{9,8},{10,11... | collective-permute-start | bytes 786440 | tf_op jit(solution)/shard_map/ppermute | solution.py:286
  211.6 3.6 %collective-permute-start.50 = (bf16[128,1024]{1,0:T(8,128)(2,1)S(1)}, bf16[128,1024]{1,0:T(8,128)(2,1)S(1)}, u32[]{:S(2)}, u32[]{:S(2)}) collective-permute-start(bf16[128,1024]{1,0:T(8,128)(2,1)S(1)} %pad_maximum_fusion.5), channel_id=1, source_target_pairs={{0,1},{1,0},{2,3},{3,2},{4,5},{5,4},{6,7},{7,6},{8,9},{9,8},{10,11... | collective-permute-start | bytes 786440 | tf_op jit(solution)/shard_map/ppermute | solution.py:286
  216.0 4.9 %all-to-all-start = ((f32[16,1,64]{2,1,0:T(1,128)}), f32[16,1,64]{2,1,0:T(1,128)S(1)}, u32[]{:S(2)}, u32[]{:S(2)}) async-start(f32[16,1,64]{2,1,0:T(1,128)} %add.203), calls=%async_computation | async-start | bytes 16384 | tf_op jit(solution)/shard_map/all_to_all | solution.py:417
  221.8 6.1 %all-to-all-done = f32[16,1,64]{2,1,0:T(1,128)S(1)} async-done(((f32[16,1,64]{2,1,0:T(1,128)}), f32[16,1,64]{2,1,0:T(1,128)S(1)}, u32[]{:S(2)}, u32[]{:S(2)}) %all-to-all-start) | async-done | bytes 4128 | tf_op jit(solution)/shard_map/all_to_all | solution.py:417
  (244 shorter events, 104.5 us)
Async XLA Ops:
  2.6 34.4 %collective-permute-start.36 = (bf16[64,256]{1,0:T(8,128)(2,1)S(1)}, bf16[64,256]{1,0:T(8,128)(2,1)}, u32[]{:S(2)}, u32[]{:S(2)}) collective-permute-start(bf16[64,256]{1,0:T(8,128)(2,1)S(1)} %bitcast.110), channel_id=1, source_target_pairs={{0,2},{1,3},{2,0},{3,1},{4,6},{5,7},{6,4},{7,5},{8,10},{9,11},{10,... | collective-permute-start | bytes 98312 | tf_op jit(solution)/shard_map/ppermute | solution.py:286
  10.6 26.4 %collective-permute-start.21 = (bf16[2,64,256]{2,1,0:T(8,128)(2,1)}, bf16[2,64,256]{2,1,0:T(8,128)(2,1)}, u32[]{:S(2)}, u32[]{:S(2)}) collective-permute-start(bf16[2,64,256]{2,1,0:T(8,128)(2,1)} %pad_maximum_fusion.7), channel_id=1, source_target_pairs={{0,114},{1,115},{2,112},{3,113},{4,118},{5,119},{6,116},{7,117},{8... | collective-permute-start | bytes 196616 | tf_op jit(solution)/shard_map/ppermute | solution.py:286
  13.4 22.0 %collective-permute-start.20 = (bf16[3,64,256]{2,1,0:T(8,128)(2,1)S(1)}, bf16[3,64,256]{2,1,0:T(8,128)(2,1)}, u32[]{:S(2)}, u32[]{:S(2)}) collective-permute-start(bf16[3,64,256]{2,1,0:T(8,128)(2,1)S(1)} %pad_maximum_fusion.6), channel_id=1, source_target_pairs={{0,112},{1,113},{2,114},{3,115},{4,116},{5,117},{6,118},{7,119},{8... | collective-permute-start | bytes 294920 | tf_op jit(solution)/shard_map/ppermute | solution.py:286
  30.8 24.7 %collective-permute-start = (bf16[128,1024]{1,0:T(8,128)(2,1)S(1)}, bf16[128,1024]{1,0:T(8,128)(2,1)}, u32[]{:S(2)}, u32[]{:S(2)}) collective-permute-start(bf16[128,1024]{1,0:T(8,128)(2,1)S(1)} %get-tuple-element.41), channel_id=1, source_target_pairs={{0,1},{1,0},{2,3},{3,2},{4,5},{5,4},{6,7},{7,6},{8,9},{9,8},{10,11... | collective-permute-start | bytes 786440 | tf_op jit(solution)/shard_map/ppermute | solution.py:286
  39.1 30.9 %collective-permute-start.39 = (bf16[2,64,256]{2,1,0:T(8,128)(2,1)S(1)}, bf16[2,64,256]{2,1,0:T(8,128)(2,1)S(1)}, u32[]{:S(2)}, u32[]{:S(2)}) collective-permute-start(bf16[2,64,256]{2,1,0:T(8,128)(2,1)S(1)} %pad_maximum_fusion.9), channel_id=1, source_target_pairs={{0,12},{1,13},{2,14},{3,15},{4,8},{5,9},{6,10},{7,11},{8,4},{9,5},... | collective-permute-start | bytes 196616 | tf_op jit(solution)/shard_map/ppermute | solution.py:286
  41.0 17.4 %collective-permute-start.38 = (bf16[2,64,256]{2,1,0:T(8,128)(2,1)S(1)}, bf16[2,64,256]{2,1,0:T(8,128)(2,1)S(1)}, u32[]{:S(2)}, u32[]{:S(2)}) collective-permute-start(bf16[2,64,256]{2,1,0:T(8,128)(2,1)S(1)} %pad_maximum_fusion.9), channel_id=1, source_target_pairs={{0,8},{1,9},{2,10},{3,11},{4,12},{5,13},{6,14},{7,15},{8,0},{9,1},... | collective-permute-start | bytes 196616 | tf_op jit(solution)/shard_map/ppermute | solution.py:286
  41.7 13.8 %collective-permute-start.37 = (bf16[2,64,256]{2,1,0:T(8,128)(2,1)S(1)}, bf16[2,64,256]{2,1,0:T(8,128)(2,1)S(1)}, u32[]{:S(2)}, u32[]{:S(2)}) collective-permute-start(bf16[2,64,256]{2,1,0:T(8,128)(2,1)S(1)} %pad_maximum_fusion.9), channel_id=1, source_target_pairs={{0,4},{1,5},{2,6},{3,7},{4,0},{5,1},{6,2},{7,3},{8,12},{9,13},{10,... | collective-permute-start | bytes 196616 | tf_op jit(solution)/shard_map/ppermute | solution.py:286
  52.5 25.7 %collective-permute-start.25 = (bf16[8,64,256]{2,1,0:T(8,128)(2,1)S(1)}, bf16[8,64,256]{2,1,0:T(8,128)(2,1)S(1)}, u32[]{:S(2)}, u32[]{:S(2)}) collective-permute-start(bf16[8,64,256]{2,1,0:T(8,128)(2,1)S(1)} %constant_dynamic-update-slice_fusion.mine_ref), channel_id=1, source_target_pairs={{0,1},{1,0},{2,3},{3,2},{4,5},{5,4},{6,7},{7,6},{8,9},{9,8},{10,11... | collective-permute-start | bytes 786440 | tf_op jit(solution)/shard_map/ppermute | solution.py:286
  70.0 29.9 %collective-permute-start.40 = (bf16[8,64,256]{2,1,0:T(8,128)(2,1)S(1)}, bf16[8,64,256]{2,1,0:T(8,128)(2,1)S(1)}, u32[]{:S(2)}, u32[]{:S(2)}) collective-permute-start(bf16[8,64,256]{2,1,0:T(8,128)(2,1)S(1)} %constant_dynamic-update-slice_fusion.5.mine_ref), channel_id=1, source_target_pairs={{0,1},{1,0},{2,3},{3,2},{4,5},{5,4},{6,7},{7,6},{8,9},{9,8},{10,11... | collective-permute-start | bytes 786440 | tf_op jit(solution)/shard_map/ppermute | solution.py:286
  74.3 33.3 %collective-permute-start.8 = (bf16[32,1024]{1,0:T(8,128)(2,1)S(1)}, bf16[32,1024]{1,0:T(8,128)(2,1)S(1)}, u32[]{:S(2)}, u32[]{:S(2)}) collective-permute-start(bf16[32,1024]{1,0:T(8,128)(2,1)S(1)} %fusion.24), channel_id=1, source_target_pairs={{0,4},{1,5},{2,6},{3,7},{4,0},{5,1},{6,2},{7,3},{8,12},{9,13},{10,... | collective-permute-start | bytes 196616 | tf_op jit(solution)/shard_map/ppermute | solution.py:286
  75.4 32.2 %collective-permute-start.7 = (bf16[32,1024]{1,0:T(8,128)(2,1)S(1)}, bf16[32,1024]{1,0:T(8,128)(2,1)S(1)}, u32[]{:S(2)}, u32[]{:S(2)}) collective-permute-start(bf16[32,1024]{1,0:T(8,128)(2,1)S(1)} %fusion.24), channel_id=1, source_target_pairs={{0,8},{1,9},{2,10},{3,11},{4,12},{5,13},{6,14},{7,15},{8,0},{9,1},... | collective-permute-start | bytes 196616 | tf_op jit(solution)/shard_map/ppermute | solution.py:286
  76.6 31.0 %collective-permute-start.6 = (bf16[32,1024]{1,0:T(8,128)(2,1)S(1)}, bf16[32,1024]{1,0:T(8,128)(2,1)S(1)}, u32[]{:S(2)}, u32[]{:S(2)}) collective-permute-start(bf16[32,1024]{1,0:T(8,128)(2,1)S(1)} %fusion.24), channel_id=1, source_target_pairs={{0,12},{1,13},{2,14},{3,15},{4,8},{5,9},{6,10},{7,11},{8,4},{9,5},... | collective-permute-start | bytes 196616 | tf_op jit(solution)/shard_map/ppermute | solution.py:286
  111.5 33.8 %collective-permute-start.51 = (bf16[64,256]{0,1:T(8,128)(2,1)S(1)}, bf16[64,256]{0,1:T(8,128)(2,1)}, u32[]{:S(2)}, u32[]{:S(2)}) collective-permute-start(bf16[64,256]{0,1:T(8,128)(2,1)S(1)} %fusion.28), channel_id=1, source_target_pairs={{0,112},{1,113},{2,114},{3,115},{4,116},{5,117},{6,118},{7,119},{8... | collective-permute-start | bytes 98312 | tf_op jit(solution)/shard_map/ppermute | solution.py:286
  123.9 15.4 %collective-permute-start.34 = (bf16[32,1024]{1,0:T(8,128)(2,1)S(1)}, bf16[32,1024]{1,0:T(8,128)(2,1)S(1)}, u32[]{:S(2)}, u32[]{:S(2)}) collective-permute-start(bf16[32,1024]{1,0:T(8,128)(2,1)S(1)} %fusion.26), channel_id=1, source_target_pairs={{0,4},{1,5},{2,6},{3,7},{4,0},{5,1},{6,2},{7,3},{8,12},{9,13},{10,... | collective-permute-start | bytes 196616 | tf_op jit(solution)/shard_map/ppermute | solution.py:286
  124.5 14.8 %collective-permute-start.33 = (bf16[32,1024]{1,0:T(8,128)(2,1)S(1)}, bf16[32,1024]{1,0:T(8,128)(2,1)S(1)}, u32[]{:S(2)}, u32[]{:S(2)}) collective-permute-start(bf16[32,1024]{1,0:T(8,128)(2,1)S(1)} %fusion.26), channel_id=1, source_target_pairs={{0,8},{1,9},{2,10},{3,11},{4,12},{5,13},{6,14},{7,15},{8,0},{9,1},... | collective-permute-start | bytes 196616 | tf_op jit(solution)/shard_map/ppermute | solution.py:286
  126.5 12.8 %collective-permute-start.32 = (bf16[32,1024]{1,0:T(8,128)(2,1)S(1)}, bf16[32,1024]{1,0:T(8,128)(2,1)S(1)}, u32[]{:S(2)}, u32[]{:S(2)}) collective-permute-start(bf16[32,1024]{1,0:T(8,128)(2,1)S(1)} %fusion.26), channel_id=1, source_target_pairs={{0,12},{1,13},{2,14},{3,15},{4,8},{5,9},{6,10},{7,11},{8,4},{9,5},... | collective-permute-start | bytes 196616 | tf_op jit(solution)/shard_map/ppermute | solution.py:286
  140.1 16.3 %collective-permute-start.35 = (bf16[128,1024]{1,0:T(8,128)(2,1)}, bf16[128,1024]{1,0:T(8,128)(2,1)}, u32[]{:S(2)}, u32[]{:S(2)}) collective-permute-start(bf16[128,1024]{1,0:T(8,128)(2,1)} %pad_maximum_fusion.4), channel_id=1, source_target_pairs={{0,1},{1,0},{2,3},{3,2},{4,5},{5,4},{6,7},{7,6},{8,9},{9,8},{10,11... | collective-permute-start | bytes 786440 | tf_op jit(solution)/shard_map/ppermute | solution.py:286
  149.6 25.4 %collective-permute-start.15 = (bf16[32,1024]{1,0:T(8,128)(2,1)S(1)}, bf16[32,1024]{1,0:T(8,128)(2,1)S(1)}, u32[]{:S(2)}, u32[]{:S(2)}) collective-permute-start(bf16[32,1024]{1,0:T(8,128)(2,1)S(1)} %add_convert_fusion.3), channel_id=1, source_target_pairs={{0,18},{1,19},{2,16},{3,17},{4,22},{5,23},{6,20},{7,21},{8,26},{9,... | collective-permute-start | bytes 196616 | tf_op jit(solution)/shard_map/ppermute | solution.py:286
  153.7 21.3 %collective-permute-start.14 = (bf16[32,1024]{1,0:T(8,128)(2,1)S(1)}, bf16[32,1024]{1,0:T(8,128)(2,1)S(1)}, u32[]{:S(2)}, u32[]{:S(2)}) collective-permute-start(bf16[32,1024]{1,0:T(8,128)(2,1)S(1)} %add_convert_fusion.3), channel_id=1, source_target_pairs={{0,16},{1,17},{2,18},{3,19},{4,20},{5,21},{6,22},{7,23},{8,24},{9,... | collective-permute-start | bytes 196616 | tf_op jit(solution)/shard_map/ppermute | solution.py:286
  175.9 25.6 %collective-permute-start.18 = (bf16[32,1024]{1,0:T(8,128)(2,1)S(1)}, bf16[32,1024]{1,0:T(8,128)(2,1)S(1)}, u32[]{:S(2)}, u32[]{:S(2)}) collective-permute-start(bf16[32,1024]{1,0:T(8,128)(2,1)S(1)} %fusion.25), channel_id=1, source_target_pairs={{0,4},{1,5},{2,6},{3,7},{4,0},{5,1},{6,2},{7,3},{8,12},{9,13},{10,... | collective-permute-start | bytes 196616 | tf_op jit(solution)/shard_map/ppermute | solution.py:286
  177.1 24.4 %collective-permute-start.17 = (bf16[32,1024]{1,0:T(8,128)(2,1)S(1)}, bf16[32,1024]{1,0:T(8,128)(2,1)S(1)}, u32[]{:S(2)}, u32[]{:S(2)}) collective-permute-start(bf16[32,1024]{1,0:T(8,128)(2,1)S(1)} %fusion.25), channel_id=1, source_target_pairs={{0,8},{1,9},{2,10},{3,11},{4,12},{5,13},{6,14},{7,15},{8,0},{9,1},... | collective-permute-start | bytes 196616 | tf_op jit(solution)/shard_map/ppermute | solution.py:286
  189.0 12.5 %collective-permute-start.16 = (bf16[32,1024]{1,0:T(8,128)(2,1)S(1)}, bf16[32,1024]{1,0:T(8,128)(2,1)S(1)}, u32[]{:S(2)}, u32[]{:S(2)}) collective-permute-start(bf16[32,1024]{1,0:T(8,128)(2,1)S(1)} %fusion.25), channel_id=1, source_target_pairs={{0,12},{1,13},{2,14},{3,15},{4,8},{5,9},{6,10},{7,11},{8,4},{9,5},... | collective-permute-start | bytes 196616 | tf_op jit(solution)/shard_map/ppermute | solution.py:286
  211.6 16.8 %collective-permute-start.50 = (bf16[128,1024]{1,0:T(8,128)(2,1)S(1)}, bf16[128,1024]{1,0:T(8,128)(2,1)S(1)}, u32[]{:S(2)}, u32[]{:S(2)}) collective-permute-start(bf16[128,1024]{1,0:T(8,128)(2,1)S(1)} %pad_maximum_fusion.5), channel_id=1, source_target_pairs={{0,1},{1,0},{2,3},{3,2},{4,5},{5,4},{6,7},{7,6},{8,9},{9,8},{10,11... | collective-permute-start | bytes 786440 | tf_op jit(solution)/shard_map/ppermute | solution.py:286
  216.0 11.8 %all-to-all-start = ((f32[16,1,64]{2,1,0:T(1,128)}), f32[16,1,64]{2,1,0:T(1,128)S(1)}, u32[]{:S(2)}, u32[]{:S(2)}) async-start(f32[16,1,64]{2,1,0:T(1,128)} %add.203), calls=%async_computation | async-start | bytes 16384 | tf_op jit(solution)/shard_map/all_to_all | solution.py:417
  (73 other events, 604.3 us)

commit v2 on v0

v2 whole, which is shorter than its diff:
```python
import jax
import jax.numpy as jnp
from jax import lax
from jax.experimental import pallas as pl
from jax.experimental.pallas import tpu as pltpu
from jax.sharding import PartitionSpec as P

DK = 128
TICKS = 2
SCALE = DK ** (-0.5)
EPSILON = 1e-06
BF16 = jnp.bfloat16
F32 = jnp.float32
NT = (((1,), (1,)), ((), ()))
TN = (((0,), (0,)), ((), ()))
MIB = 1024 * 1024


def dot(a, b):
    return jnp.dot(a, b, preferred_element_type=F32)


def dot_nt(a, b):
    return lax.dot_general(a, b, NT, preferred_element_type=F32)


def dot_tn(a, b):
    return lax.dot_general(a, b, TN, preferred_element_type=F32)


def normalize(rows, gain_row):
    floats = rows.astype(F32)
    inverse = lax.rsqrt(jnp.mean(floats * floats, axis=-1, keepdims=True) + EPSILON)
    unit_rows = floats * inverse
    return unit_rows * gain_row, unit_rows, inverse


def softmax(queries, key_rows):
    scores = dot_nt(queries, key_rows) * SCALE
    exponent = jnp.exp(scores - jnp.max(scores, axis=-1, keepdims=True))
    return exponent * (1.0 / jnp.sum(exponent, axis=-1, keepdims=True))


VMEM = pl.BlockSpec(memory_space=pltpu.VMEM)
SMEM = pl.BlockSpec(memory_space=pltpu.SMEM)
ANYWHERE = pl.BlockSpec(memory_space=pltpu.HBM)


def shape(dtype, *dims):
    return jax.ShapeDtypeStruct(dims, dtype)


def kept(dtype, *dims):
    return pltpu.VMEM(dims, dtype)


def in_hbm(dtype, *dims):
    return pltpu.HBM(dims, dtype)


def from_hbm(value):
    return pltpu.with_memory_space_constraint(value, pltpu.HBM)


def where_am_i():
    head = lax.axis_index("head")
    return head & 1, (head >> 1) & 1, head >> 2, lax.axis_index("section")


def kernel_call(body, name, args, outs, scratch=(), scalars=0, loose=0, flops=0, limit=16):
    moved = sum(a.size * a.dtype.itemsize for a in args)
    return pl.pallas_call(
        body,
        in_specs=[SMEM] * scalars + [VMEM] * (len(args) - scalars - loose) + [ANYWHERE] * loose,
        out_specs=[ANYWHERE if getattr(o, "memory_space", None) is pltpu.HBM else VMEM for o in outs],
        out_shape=list(outs),
        scratch_shapes=list(scratch),
        compiler_params=pltpu.CompilerParams(vmem_limit_bytes=limit * MIB),
        cost_estimate=pl.CostEstimate(flops=flops, bytes_accessed=moved, transcendentals=0),
        name=name,
    )(*args)


def lanes(i):
    return slice(i * DK, (i + 1) * DK)


def at_rows(start, count):
    return pl.ds(pl.multiple_of(start, count), count)


def run_copies(pairs, sems):
    copies = [pltpu.make_async_copy(src, dst, sems.at[i]) for i, (src, dst) in enumerate(pairs)]
    for copy in copies:
        copy.start()
    for copy in copies:
        copy.wait()


def pick_held(slots, store, out, sems):
    mirror = lax.axis_size("section") - 1 - lax.axis_index("section")
    run_copies([(store.at[slots[t, mirror]], out.at[t]) for t in range(TICKS)], sems)


def pick_rows(current, upstream, tokens, cotangents, z, *refs):
    *fresh, sems = refs
    core, _, column, _ = where_am_i()
    rows = z.shape[0] // 2
    at = at_rows(core * (current.shape[0] // 2) + column * rows, rows)
    pairs = [(current.at[at, :], z.at[:rows, :]), (upstream.at[at, :], z.at[rows:, :])]
    for t in range(TICKS):
        pairs.append((tokens.at[t, at, :], fresh[t].at[:rows, :]))
        pairs.append((cotangents.at[t, at, :], fresh[t].at[rows:, :]))
    run_copies(pairs, sems)


def turn_first(slots, current, shares, flag, turned):
    section, head = lax.axis_index("section"), lax.axis_index("head")
    share = shares.shape[1]
    turned[...] = current[...].T
    shares[0] = turned[at_rows(head * share, share), :]
    shares[1] = turned[at_rows((head ^ 2) * share, share), :]
    same = jnp.where(slots[0, section] == slots[1, section], 1.0, 0.0)
    flag[...] = jnp.full(flag.shape, same, F32)


def pick_reload(near, far, shares, flag, both):
    both[0] = near[0]
    both[1] = far[0]
    same = flag[0:1, :] > 0.5
    for y, ref in enumerate((near, far)):
        both[2 + y] = jnp.where(same, shares[y].astype(F32), ref[1].astype(F32)).astype(BF16)


def part_reload(own, got1, got2, got3, after, first, second):
    for j, ref in enumerate((own, got1, got2, got3)):
        first[2 * j : 2 * j + 2] = ref[0:2]
        second[2 * j : 2 * j + 2] = ref[2:4]


def pick_share(first_shares, current, after, out, turned):
    share = first_shares.shape[1]
    turned[...] = current[...].T
    out[0] = first_shares[0]
    out[1] = turned[at_rows(lax.axis_index("head") * share, share), :]


def put_store(slots, store, arrived, out):
    mirror = lax.axis_size("section") - 1 - lax.axis_index("section")
    out[...] = store[...]
    for t in range(TICKS):
        out[slots[t, mirror]] = arrived[t]


def attend_and_project(n, total, keep_ref, send_ref, wq, wk, wv, wo, q, k, v, context, ready):
    ready(0)
    q[...] = dot(n, wq[...]).astype(BF16)
    ready(1)
    k[...] = dot(n, wk[...]).astype(BF16)
    ready(2)
    v[...] = dot(n, wv[...]).astype(BF16)
    for i in range(q.shape[1] // DK):
        at = lanes(i)
        low = softmax(q[:, at], k[:, at]).astype(BF16)
        context[:, at] = dot(low, v[:, at]).astype(BF16)
    ready(3)
    total[...] = dot(context[...], wo[...])
    core = where_am_i()[0]
    half = keep_ref.shape[0]
    keep_ref[...] = total[at_rows(core * half, half), :]
    send_ref[...] = total[at_rows((1 - core) * half, half), :].astype(BF16)


def forward_first(rows, gain, hq, hk, hv, ho, wq, wk, wv, wo, keep, send, q, k, v, context, total, sems):
    copies = [
        pltpu.make_async_copy(src, dst, sems.at[i])
        for i, (src, dst) in enumerate(((hq, wq), (hk, wk), (hv, wv), (ho, wo)))
    ]
    for copy in copies:
        copy.start()
    n = normalize(rows[...], gain[...])[0].astype(BF16)
    attend_and_project(
        n, total, keep, send, wq, wk, wv, wo, q, k, v, context, lambda i: copies[i].wait()
    )


def put_pieces(pieces, first, second):
    core, _, column, _ = where_am_i()
    rows = pieces[0].shape[0] // 2
    half = first.shape[0] // 2
    for i, ref in enumerate(pieces):
        c = core if i < 4 else 1 - core
        at = at_rows(c * half + (column ^ (i % 4)) * rows, rows)
        first[at, :] = ref[:rows, :]
        second[at, :] = ref[rows:, :]


def forward_next(gain, wq, wk, wv, wo, *refs):
    pieces, (rows, g, keep, send), (q, k, v, context, total) = refs[:8], refs[8:12], refs[12:]
    put_pieces(pieces, rows, g)
    n = normalize(rows[...], gain[...])[0].astype(BF16)
    attend_and_project(n, total, keep, send, wq, wk, wv, wo, q, k, v, context, lambda i: None)


def put_last(gain_rows, gain_other, *refs):
    pieces, (rows, g, gain_out) = refs[:8], refs[8:]
    put_pieces(pieces, rows, g)
    value = get_gain(gain_rows, 0) + get_gain(gain_other, 0)
    share = gain_out.shape[1]
    for h in range(value.shape[1] // share):

        @pl.when(lax.axis_index("head") == h)
        def _():
            gain_out[...] = value[:, h * share : (h + 1) * share]


def recompute_kernel(gain, wq, wk, wv, *refs):
    mine, other, block_ref, normed_out, q, k, v, soft, context_out = refs[:9]
    block_t, normed_t, context, sems = refs[-4:]
    core, high, column, _ = where_am_i()
    share = mine.shape[1]
    for ref, c in ((mine, core), (other, 1 - core)):
        for i in range(8):
            head = (column ^ (i // 2)) * 4 + (high ^ (i % 2)) * 2 + c
            block_t[at_rows(head * share, share), :] = ref[i]
    block = block_t[...].T
    block_ref[...] = block
    n = normalize(block, gain[...])[0].astype(BF16)
    normed_t[...] = n.T
    first = pltpu.make_async_copy(normed_t, normed_out, sems.at[0])
    first.start()
    q[...] = dot(n, wq[...]).astype(BF16)
    k[...] = dot(n, wk[...]).astype(BF16)
    v[...] = dot(n, wv[...]).astype(BF16)
    for i in range(q.shape[1] // DK):
        at = lanes(i)
        rows = softmax(q[:, at], k[:, at])
        soft[i] = rows
        context[:, at] = dot(rows.astype(BF16), v[:, at]).astype(BF16)
    second = pltpu.make_async_copy(context, context_out, sems.at[1])
    second.start()
    first.wait()
    second.wait()


def backward_kernel(
    g, block, gain, q, k, v, soft, wq, wk, wv, wo, ahead_keep, ahead_send, gain_before,
    *refs,
):
    keep, send, qg_out, kg_out, vg_out, gain_part, qg, kg, vg, grads, total, sems = refs[-12:]
    grads[...] = dot_nt(g[...], wo[...]).astype(BF16)
    for i in range(q.shape[1] // DK):
        at = lanes(i)
        rows = soft[i]
        grad = grads[:, at]
        soft_grad = dot_nt(grad, v[:, at])
        vg[:, at] = dot_tn(rows.astype(BF16), grad).astype(BF16)
        along = jnp.sum(rows * soft_grad, axis=-1, keepdims=True)
        score_grad = (rows * (soft_grad - along) * SCALE).astype(BF16)
        qg[:, at] = dot(score_grad, k[:, at]).astype(BF16)
        kg[:, at] = dot_tn(score_grad, q[:, at]).astype(BF16)
    copies = [
        pltpu.make_async_copy(src, dst, sems.at[i])
        for i, (src, dst) in enumerate(((qg, qg_out), (kg, kg_out), (vg, vg_out)))
    ]
    for copy in copies:
        copy.start()
    total[...] = dot_nt(qg[...], wq[...])
    total[...] += dot_nt(kg[...], wk[...])
    total[...] += dot_nt(vg[...], wv[...])
    half = ahead_keep.shape[0]
    core = where_am_i()[0]
    keep[:half, :] = ahead_keep[...]
    keep[half:, :] = total[at_rows(core * half, half), :]
    send[:half, :] = ahead_send[...]
    send[half : 2 * half, :] = total[at_rows((1 - core) * half, half), :].astype(BF16)
    unit = normalize(block[...], gain[...])[1]
    part = gain_before[...] + jnp.sum(total[...] * unit, axis=0, keepdims=True)
    gain_part[...] = part
    if send.shape[0] > 2 * half:
        put_gain(send, 2 * half, part)
    for copy in copies:
        copy.wait()


def put_gain(ref, row, value):
    value = jnp.broadcast_to(value, (16, value.shape[1]))
    high = value.astype(BF16)
    low = (value - high.astype(F32)).astype(BF16)
    is_first = lax.broadcasted_iota(jnp.int32, value.shape, 0) == 0
    ref[row : row + 16, :] = jnp.where(is_first, high.astype(F32), low.astype(F32)).astype(BF16)


def get_gain(ref, row):
    tile = ref[row : row + 16, :].astype(F32)
    return tile[0:1] + tile[1:2]


def after_core(keep, got, gain_part, *refs):
    own, to1, to2, to3, gain_out, mine = refs[-6:]
    column = where_am_i()[2]
    half = keep.shape[0] // 2
    rows = half // 4
    mine[...] = keep[...] + got[: 2 * half, :].astype(F32)
    for j, ref in ((0, own), (1, to1), (2, to2), (3, to3)):
        for part in range(2):
            at = at_rows(part * half + (column ^ j) * rows, rows)
            ref[part * rows : (part + 1) * rows, :] = mine[at, :].astype(ref.dtype)
    if got.shape[0] > 2 * half:
        value = gain_part[...] + get_gain(got, 2 * half)
        gain_out[...] = value
        for ref in (to1, to2, to3):
            put_gain(ref, 2 * rows, value)
    else:
        gain_out[...] = gain_part[...]


def after_column(own, z, block, gain, gain_part, got1, got2, got3, *refs):
    even, odd, gain_out = refs[-3:]
    core, high, column, section = where_am_i()
    rows = z.shape[0] // 2
    tokens = block.shape[0]
    total = [None, None]
    for part in range(2):
        at = slice(part * rows, (part + 1) * rows)
        total[part] = own[at, :] + (
            got1[at, :].astype(F32) + (got2[at, :].astype(F32) + got3[at, :].astype(F32))
        )
    here = jnp.where(high == 0, 1.0, 0.0).astype(F32)
    ahead = (here * z[:rows, :].astype(F32) + total[0]).astype(BF16)
    at = at_rows(core * (tokens // 2) + column * rows, rows)
    _, unit, inverse = normalize(block[at, :], gain[...])
    unit_grad = total[1] * gain[...]
    along = jnp.mean(unit_grad * unit, axis=-1, keepdims=True)
    back = here * z[rows:, :].astype(F32) + inverse * (unit_grad - unit * along)
    back = back.astype(BF16)

    @pl.when((section & 1) == 0)
    def _():
        even[...] = ahead
        odd[...] = back

    @pl.when((section & 1) == 1)
    def _():
        even[...] = back
        odd[...] = ahead

    if got1.shape[0] > 2 * rows:
        value = get_gain(got1, 2 * rows) + get_gain(got2, 2 * rows) + get_gain(got3, 2 * rows)
        put_gain(gain_out, 0, gain_part[...] + value)
    else:
        put_gain(gain_out, 0, gain_part[...])


def after_shift(even0, even1, odd0, odd1, fresh, z):
    section = where_am_i()[3]
    rows = even0.shape[0]
    even = (even0[...].astype(F32) + even1[...].astype(F32)).astype(BF16)
    odd = (odd0[...].astype(F32) + odd1[...].astype(F32)).astype(BF16)

    @pl.when((section & 1) == 0)
    def _():
        z[:rows, :] = odd
        z[rows:, :] = even

    @pl.when((section & 1) == 1)
    def _():
        z[:rows, :] = even
        z[rows:, :] = odd

    @pl.when(section == 0)
    def _():
        z[:rows, :] = fresh[:rows, :]

    @pl.when(section == lax.axis_size("section") - 1)
    def _():
        z[rows:, :] = fresh[rows:, :]


def query_key_kernel(after, n0, n1, q0, q1, k0, k1, dq, dk):
    dq[...] = (dot(n0[...], q0[...]) + dot(n1[...], q1[...])).astype(BF16)
    dk[...] = (dot(n0[...], k0[...]) + dot(n1[...], k1[...])).astype(BF16)


def value_out_kernel(after, n0, n1, v0, v1, c0, c1, g0, g1, dv, do):
    dv[...] = (dot(n0[...], v0[...]) + dot(n1[...], v1[...])).astype(BF16)
    do[...] = (dot_tn(c0[...], g0[...]) + dot_tn(c1[...], g1[...])).astype(BF16)


def weight_grads(body, name, after, normed_t, blocked, fixed, by_rows):
    steps = 4
    width, tokens = normed_t[0].shape
    inner = blocked[0].shape[1]
    block = inner // steps
    args = [after, *normed_t, *blocked, *fixed]
    outs = [pl.BlockSpec((width, block), lambda i: (0, i))] * 2
    shapes = [shape(BF16, width, inner)] * 2
    if by_rows:
        outs[1] = pl.BlockSpec((block, width), lambda i: (i, 0))
        shapes[1] = shape(BF16, inner, width)
    return pl.pallas_call(
        body,
        grid=(steps,),
        in_specs=[pl.BlockSpec(memory_space=pl.ANY)]
        + [pl.BlockSpec((width, tokens), lambda i: (0, 0))] * 2
        + [pl.BlockSpec((tokens, block), lambda i: (0, i))] * len(blocked)
        + [pl.BlockSpec((tokens, width), lambda i: (0, 0))] * len(fixed),
        out_specs=outs,
        out_shape=shapes,
        compiler_params=pltpu.CompilerParams(
            dimension_semantics=("arbitrary",), vmem_limit_bytes=16 * MIB
        ),
        cost_estimate=pl.CostEstimate(
            flops=8 * tokens * width * inner, bytes_accessed=4 * width * inner, transcendentals=0
        ),
        name=name,
    )(*args)


class Moves:
    def __init__(self, sections, heads):
        self.sections, self.heads = sections, heads

    def send(self, value, to, mask):
        pairs = []
        for s in range(self.sections):
            t = to(s)
            if 0 <= t < self.sections:
                pairs += [(s * self.heads + h, t * self.heads + (h ^ mask)) for h in range(self.heads)]
        return lax.ppermute(value, ("section", "head"), pairs)

    def flip(self, value, mask):
        return self.send(value, lambda s: s, mask)

    def even(self, value, mask):
        return self.send(value, lambda s: s ^ 1, mask)

    def odd(self, value, mask):
        return self.send(value, lambda s: ((s - 1) ^ 1) + 1, mask)

    def mirror(self, value, mask):
        return self.send(value, lambda s: self.sections - 1 - s, mask)


def per_device(
    section_inputs, section_cotangents, fresh_tokens, fresh_cotangents, norm_gain,
    query_weight, key_weight, value_weight, out_weight, saved_inputs, reload_slot,
):
    sections, heads = lax.axis_size("section"), lax.axis_size("head")
    section, head = lax.axis_index("section"), lax.axis_index("head")
    moves = Moves(sections, heads)
    share = saved_inputs.shape[3]
    gain = norm_gain
    store = jnp.swapaxes(saved_inputs[0], 1, 2)
    tokens, width = section_inputs.shape[1:]
    inner = query_weight.shape[2]
    half, rows = tokens // 2, tokens // 8
    unit_flops = 2 * tokens * width * inner
    current, upstream = section_inputs[0], section_cotangents[0]

    (going,) = kernel_call(
        pick_held, "pick_held", (reload_slot, from_hbm(store)), [kept(BF16, TICKS, share, tokens)],
        [pltpu.SemaphoreType.DMA((TICKS,))], 1, 1,
    )
    near, far = moves.mirror(going, 0), moves.mirror(going, 2)
    z, *fresh = kernel_call(
        pick_rows, "pick_rows",
        [from_hbm(a) for a in (current, upstream, fresh_tokens, fresh_cotangents)],
        [kept(BF16, 2 * rows, width)] * (1 + TICKS),
        [pltpu.SemaphoreType.DMA((2 + 2 * TICKS,))], 0, 4,
    )
    first_shares, flag = kernel_call(
        turn_first, "turn_first", (reload_slot, current),
        [kept(BF16, 2, share, tokens), kept(F32, 8, tokens)],
        [pltpu.VMEM((width, tokens), BF16)], 1,
    )
    (both,) = kernel_call(
        pick_reload, "pick_reload", (near, far, first_shares, flag),
        [kept(BF16, 2 * TICKS, share, tokens)],
    )
    arriving = [both] + [moves.flip(both, 4 * j) for j in (1, 2, 3)]

    flat = kept(BF16, tokens, inner)
    whole = kept(BF16, tokens, width)
    half_outs = [kept(F32, half, width), kept(BF16, half, width)]
    work = [pltpu.VMEM((tokens, inner), BF16)] * 4 + [pltpu.VMEM((tokens, width), F32)]
    gain_part = jnp.zeros((1, width), F32)
    left, context, grads_of, cotangents = [], [], [], []
    pieces = None

    def recompute(u):
        return kernel_call(
            recompute_kernel, "recompute", (gain, wq, wk, wv, *reload[u]),
            [
                whole, kept(BF16, width, tokens), flat, flat, flat,
                kept(F32, inner // DK, tokens, tokens), flat,
            ],
            [
                pltpu.VMEM((width, tokens), BF16), pltpu.VMEM((width, tokens), BF16),
                pltpu.VMEM((tokens, inner), BF16), pltpu.SemaphoreType.DMA((2,)),
            ], 0, 0, 5 * unit_flops,
        )

    for t in range(TICKS):
        if t == 0:
            raw = [
                from_hbm(w[0]) for w in (query_weight, key_weight, value_weight, out_weight)
            ]
            *weights, keep, send = kernel_call(
                forward_first, "forward_first", (current, gain, *raw),
                [kept(BF16, *w.shape) for w in raw] + half_outs,
                work + [pltpu.SemaphoreType.DMA((4,))], 0, 4, 5 * unit_flops,
            )
            wq, wk, wv, wo = weights
            own_shares = kernel_call(
                part_reload, "part_reload", (*arriving, send),
                [kept(BF16, 8, share, tokens)] * TICKS, (), 0, 1,
            )
            reload = [(a, moves.flip(a, 1)) for a in own_shares]
        else:
            current, upstream, keep, send = kernel_call(
                forward_next, "forward_next", (gain, wq, wk, wv, wo, *pieces),
                [whole] * 2 + half_outs, work, 0, 0, 5 * unit_flops,
            )
        if t == 0:
            read = [recompute(u) for u in range(1)]
        block, normed_t, q, k, v, soft, ctx = read[t]
        extra = 16 if t == TICKS - 1 else 0
        keep, send, qg, kg, vg, gain_part = kernel_call(
            backward_kernel, "backward",
            (upstream, block, gain, q, k, v, soft, wq, wk, wv, wo, keep, send, gain_part),
            [kept(F32, tokens, width), kept(BF16, tokens + extra, width)]
            + [flat] * 3 + [kept(F32, 1, width)],
            [pltpu.VMEM((tokens, inner), BF16)] * 4
            + [pltpu.VMEM((tokens, width), F32), pltpu.SemaphoreType.DMA((3,))],
            0, 0, 6 * unit_flops,
        )
        left.append(normed_t)
        context.append(ctx)
        grads_of.append((qg, kg, vg))
        cotangents.append(upstream)

        got = moves.flip(send, 1)
        own, to1, to2, to3, gain_sum = kernel_call(
            after_core, "after_core", (keep, got, gain_part),
            [kept(F32, 2 * rows, width)] + [kept(BF16, 2 * rows + extra, width)] * 3 + [kept(F32, 1, width)],
            [pltpu.VMEM((tokens, width), F32)],
        )
        got1, got2, got3 = moves.flip(to1, 4), moves.flip(to2, 8), moves.flip(to3, 12)
        if t == 0:
            read.append(recompute(1))
            beside = [read[1][5]]
        else:
            query_grad, key_grad = weight_grads(
                query_key_kernel, "query_key_grad", own, left,
                [grads_of[u][i] for i in range(2) for u in range(TICKS)], [], False,
            )
            value_grad, out_grad = weight_grads(
                value_out_kernel, "value_out_grad", own, left,
                [grads_of[u][2] for u in range(TICKS)] + context, cotangents, True,
            )
            beside = [from_hbm(query_grad), from_hbm(value_grad)]
        even, odd, gain_rows = kernel_call(
            after_column, "after_column",
            (own, z, block, gain, gain_sum, got1, got2, got3, *beside),
            [kept(BF16, rows, width)] * 2 + [kept(BF16, 16, width)], (), 0, len(beside),
        )
        even0, odd0 = moves.even(even, 0), moves.odd(odd, 0)
        even1, odd1 = moves.even(even, 2), moves.odd(odd, 2)
        (z,) = kernel_call(
            after_shift, "after_shift",
            (even0, even1, odd0, odd1, fresh[t]),
            [kept(BF16, 2 * rows, width)],
        )
        pieces = [z] + [moves.flip(z, 4 * j) for j in (1, 2, 3)]
        pieces = pieces + [moves.flip(p, 1) for p in pieces]
    last_inputs, last_cotangents, gain_grad = kernel_call(
        put_last, "put_last", (gain_rows, moves.flip(gain_rows, 2), *pieces),
        [shape(BF16, tokens, width)] * 2 + [shape(F32, 1, share)],
    )

    (shares,) = kernel_call(
        pick_share, "pick_share", (first_shares, current, to1), [kept(BF16, 2, share, tokens)],
        [pltpu.VMEM((width, tokens), BF16)], 0, 1,
    )
    (stored,) = kernel_call(
        put_store, "put_store", (reload_slot, store, moves.mirror(shares, 0)),
        [shape(BF16, *store.shape)], (), 1,
    )

    return (
        last_inputs[None],
        last_cotangents[None],
        jnp.swapaxes(stored, 1, 2)[None],
        query_grad[None],
        key_grad[None],
        value_grad[None],
        out_grad[None],
        gain_grad,
    )


def solution(mesh):
    placed = (
        P("section", None, None),
        P("section", None, None),
        P(),
        P(),
        P("section", None),
        P("section", None, "head"),
        P("section", None, "head"),
        P("section", None, "head"),
        P("section", "head", None),
        P("section", None, None, "head"),
        P(),
    )
    return jax.shard_map(
        per_device,
        mesh=mesh,
        in_specs=placed,
        out_specs=(
            P("section", None, None),
            P("section", None, None),
            P("section", None, None, "head"),
            P("section", None, "head"),
            P("section", None, "head"),
            P("section", None, "head"),
            P("section", "head", None),
            P("section", "head"),
        ),
        check_vma=False,
    )
```

time: 489 us -> 147 us (0.30); the launches traced: 481 us -> 144 us
  waiting for transfers between devices: 224 us -> 21.5 us
  matrix products: 106 us -> 0 us
  blocking collectives: 61.7 us -> 0 us
  Pallas kernels: 0 us -> 44.6 us
  starting transfers between devices: 29 us -> 72.9 us
  local copies, waits for them, and re-layouts: 28.2 us -> 4.15 us
  between operations: 18.7 us -> 0.97 us
  other arithmetic: 13 us -> 0 us
    psum x2 -> x0, waiting for transfers between devices: 205 us -> none  [ahead(): total = lax.psum(partial_value, 'head')]
    dot_general x42 -> x0, matrix products: 92.9 us -> none  [the longest x2 10.5 us: behind(): jnp.einsum('hqk,khd->qhd', score_grad, split_heads(key_rows), preferred_e...]
    all_gather x2 -> x0, blocking collectives: 61.7 us -> none  [per_device(): restored = lax.all_gather(reloaded, 'head', axis=1, tiled=True)]
    pallas_call x0 -> x22, Pallas kernels: none -> 44.6 us  [the longest x20 36 us: kernel_call(): pl.pallas_call(body, in_specs=[SMEM] * scalars + [VMEM] * (len(args) - sc...]
    ppermute x16 -> x39, starting transfers between devices: 28.9 us -> 72.9 us  [send(): return lax.ppermute(value, ('section', 'head'), pairs)]
    reshape x10 -> x0, local copies, waits for them, and re-layouts: 17.7 us -> none  [split_heads(): return rows.reshape(rows.shape[0], -1, DK)]
    sub x4 -> x0, matrix products: 13.3 us -> none  [attend(): exponent = jnp.exp(scores - highest)]
    convert_element_type x4 -> x0, other arithmetic: 5.57 us -> none  [the longest x2 4.04 us: ahead(): output_rows = (rows.astype(jnp.float32) + total).astype(jnp.bfloat16)]
  transfers between devices with their start and end apart: 18 -> 39, of which waited for: 7 -> 13; matrix products, arithmetic and copies ran while one was open for 22% -> 0% of each run, Pallas kernels for 0% -> 15%
where the time goes in v2:
time: 147 us; the launch traced here: 144 us
  starting transfers between devices  72.9 us (50%)
  Pallas kernels  44.6 us (30%)
  waiting for transfers between devices  21.5 us (15%)
  local copies, waits for them, and re-layouts  4.15 us (3%)
    ppermute x39, starting transfers between devices, send(): return lax.ppermute(value, ('section', 'head'), pairs)  72.9 us
    pallas_call x20, Pallas kernels, kernel_call(): pl.pallas_call(body, in_specs=[SMEM] * scalars + [VMEM] * (len(args) - sc...  36 us
    ppermute x39, waiting for transfers between devices, send(): return lax.ppermute(value, ('section', 'head'), pairs)  21.5 us
    pallas_call x2, Pallas kernels, weight_grads(): pl.pallas_call(body, grid=(steps,), in_specs=[pl.BlockSpec(memory_space=p...  8.67 us
    unnamed x20, local copies, waits for them, and re-layouts  4.14 us
  transfers between devices with their start and end apart: 39, of which 13 were waited for; matrix products, arithmetic and copies ran while one was open for 0% of the time, Pallas kernels for 15%

profile of v2, /device:TPU:9, one launch (start us, length us, event | category | flops | bytes accessed | tf_op | source)
XLA Modules:
  0.0 144.2 jit_solution(11421603841706872010)
XLA Ops:
  2.7 3.8 %collective-permute-start = (bf16[2,64,256]{2,1,0:T(8,128)(2,1)S(1)}, bf16[2,64,256]{2,1,0:T(8,128)(2,1)S(1)}, u32[]{:S(2)}, u32[]{:S(2)}) collective-permute-start(bf16[2,64,256]{2,1,0:T(8,128)(2,1)S(1)} %pick_held.1), channel_id=1, source_target_pairs={{0,112},{1,113},{2,114},{3,115},{4,116},{5,117},{6,118},{7,119},{8... | collective-permute-start | bytes 196616 | tf_op jit(solution)/shard_map/ppermute | solution.py:430
  17.4 6.0 %forward_first.1 = (bf16[1024,1024]{1,0:T(8,128)(2,1)S(1)}, bf16[1024,1024]{1,0:T(8,128)(2,1)S(1)}, bf16[1024,1024]{1,0:T(8,128)(2,1)S(1)}, bf16[1024,1024]{1,0:...) custom-call(bf16[256,1024]{1,0:T(8,128)(2,1)S(1)} %bitcast.23, f32[1,1024]{1,0:T(1,128)S(1)} %copy-done.5, ...), custom_call_target="tpu_custom_call" | custom-call | flops 2684354560 | bytes 8916992 | tf_op jit(solution)/shard_map/forward_first/pallas_call | solution.py:72
  23.4 3.2 %collective-permute-start.5 = (bf16[8,64,256]{2,1,0:T(8,128)(2,1)S(1)}, bf16[8,64,256]{2,1,0:T(8,128)(2,1)S(1)}, u32[]{:S(2)}, u32[]{:S(2)}) collective-permute-start(bf16[8,64,256]{2,1,0:T(8,128)(2,1)S(1)} %get-tuple-element.80.refs_0_), channel_id=1, source_target_pairs={{0,1},{1,0},{2,3},{3,2},{4,5},{5,4},{6,7},{7,6},{8,9},{9,8},{10,11... | collective-permute-start | bytes 786440 | tf_op jit(solution)/shard_map/ppermute | solution.py:430
  27.8 3.8 %recompute.2 = (bf16[256,1024]{1,0:T(8,128)(2,1)S(1)}, bf16[1024,256]{1,0:T(8,128)(2,1)S(1)}, bf16[256,1024]{1,0:T(8,128)(2,1)S(1)}, bf16[256,1024]{1,0:T(8,128)...) custom-call(f32[1,1024]{1,0:T(1,128)S(1)} %copy-done.5, ...), custom_call_target="tpu_custom_call" | custom-call | flops 2684354560 | bytes 6819840 | tf_op jit(solution)/shard_map/recompute/pallas_call | solution.py:72
  31.6 5.5 %backward.2 = (f32[256,1024]{1,0:T(8,128)S(1)}, bf16[256,1024]{1,0:T(8,128)(2,1)S(1)}, bf16[256,1024]{1,0:T(8,128)(2,1)S(1)}, bf16[256,1024]{1,0:T(8,128)(2,1)S(...) custom-call(bf16[256,1024]{1,0:T(8,128)(2,1)S(1)} %bitcast.19, bf16[256,1024]{1,0:T(8,128)(2,1)S(1)} %get-tuple-element.81.block, ...), custom_call_target="tpu_custom_call" | custom-call | flops 3221225472 | bytes 13901824 | tf_op jit(solution)/shard_map/backward/pallas_call | solution.py:72
  39.4 3.6 %collective-permute-start.8 = (bf16[64,1024]{1,0:T(8,128)(2,1)S(1)}, bf16[64,1024]{1,0:T(8,128)(2,1)S(1)}, u32[]{:S(2)}, u32[]{:S(2)}) collective-permute-start(bf16[64,1024]{1,0:T(8,128)(2,1)S(1)} %get-tuple-element.94), channel_id=1, source_target_pairs={{0,8},{1,9},{2,10},{3,11},{4,12},{5,13},{6,14},{7,15},{8,0},{9,1},... | collective-permute-start | bytes 393224 | tf_op jit(solution)/shard_map/ppermute | solution.py:430
  43.3 3.8 %recompute.3 = (bf16[256,1024]{1,0:T(8,128)(2,1)S(1)}, bf16[1024,256]{1,0:T(8,128)(2,1)S(1)}, bf16[256,1024]{1,0:T(8,128)(2,1)S(1)}, bf16[256,1024]{1,0:T(8,128)...) custom-call(f32[1,1024]{1,0:T(1,128)S(1)} %copy-done.5, ...), custom_call_target="tpu_custom_call" | custom-call | flops 2684354560 | bytes 6819840 | tf_op jit(solution)/shard_map/recompute/pallas_call | solution.py:72
  52.5 4.7 %collective-permute-start.12 = (bf16[32,1024]{1,0:T(8,128)(2,1)S(1)}, bf16[32,1024]{1,0:T(8,128)(2,1)S(1)}, u32[]{:S(2)}, u32[]{:S(2)}) collective-permute-start(bf16[32,1024]{1,0:T(8,128)(2,1)S(1)} %get-tuple-element.98), channel_id=1, source_target_pairs={{0,18},{1,19},{2,16},{3,17},{4,22},{5,23},{6,20},{7,21},{8,26},{9,... | collective-permute-start | bytes 196616 | tf_op jit(solution)/shard_map/ppermute | solution.py:430
  59.2 3.7 %collective-permute-start.14 = (bf16[32,1024]{1,0:T(8,128)(2,1)S(1)}, bf16[32,1024]{1,0:T(8,128)(2,1)S(1)}, u32[]{:S(2)}, u32[]{:S(2)}) collective-permute-start(bf16[32,1024]{1,0:T(8,128)(2,1)S(1)} %get-tuple-element.99), channel_id=1, source_target_pairs={{16,34},{17,35},{18,32},{19,33},{20,38},{21,39},{22,36},{23,37},{2... | collective-permute-start | bytes 196616 | tf_op jit(solution)/shard_map/ppermute | solution.py:430
  64.3 2.6 %collective-permute-done.14.odd1 = bf16[32,1024]{1,0:T(8,128)(2,1)S(1)} collective-permute-done((bf16[32,1024]{1,0:T(8,128)(2,1)S(1)}, bf16[32,1024]{1,0:T(8,128)(2,1)S(1)}, u32[]{:S(2)}, u32[]{:S(2)}) %collective-permute-start.14) | collective-permute-done | bytes 65568 | tf_op jit(solution)/shard_map/ppermute | solution.py:430
  71.0 3.2 %collective-permute-start.18 = (bf16[64,1024]{1,0:T(8,128)(2,1)S(1)}, bf16[64,1024]{1,0:T(8,128)(2,1)S(1)}, u32[]{:S(2)}, u32[]{:S(2)}) collective-permute-start(bf16[64,1024]{1,0:T(8,128)(2,1)S(1)} %after_shift.2.refs_0_.z), channel_id=1, source_target_pairs={{0,1},{1,0},{2,3},{3,2},{4,5},{5,4},{6,7},{7,6},{8,9},{9,8},{10,11... | collective-permute-start | bytes 393224 | tf_op jit(solution)/shard_map/ppermute | solution.py:430
  78.6 4.0 %forward_next.1 = (bf16[256,1024]{1,0:T(8,128)(2,1)S(1)}, bf16[256,1024]{1,0:T(8,128)(2,1)S(1)}, f32[128,1024]{1,0:T(8,128)S(1)}, bf16[128,1024]{1,0:T(8,128)(2,1)S(1)}) custom-call(f32[1,1024]{1,0:T(1,128)S(1)} %copy-done.5, bf16[1024,1024]{1,0:T(8,128)(2,1)S(1)} %get-tuple-element.73.wq, bf16[1024,1024]{1,0:T(8,128)(2,1)S(1)} %get-tuple-element.74.wk, ...), custom_call_target="tpu_custom_call" | custom-call | flops 2684354560 | bytes 9441280 | tf_op jit(solution)/shard_map/forward_next/pallas_call | solution.py:72
  82.6 5.5 %backward.3 = (f32[256,1024]{1,0:T(8,128)S(1)}, bf16[272,1024]{1,0:T(8,128)(2,1)S(1)}, bf16[256,1024]{1,0:T(8,128)(2,1)S(1)}, bf16[256,1024]{1,0:T(8,128)(2,1)S(...) custom-call(bf16[256,1024]{1,0:T(8,128)(2,1)S(1)} %get-tuple-element.101.g.g1, ...), custom_call_target="tpu_custom_call" | custom-call | flops 3221225472 | bytes 13901824 | tf_op jit(solution)/shard_map/backward/pallas_call | solution.py:72
  91.0 3.2 %collective-permute-start.24 = (bf16[80,1024]{1,0:T(8,128)(2,1)S(1)}, bf16[80,1024]{1,0:T(8,128)(2,1)S(1)}, u32[]{:S(2)}, u32[]{:S(2)}) collective-permute-start(bf16[80,1024]{1,0:T(8,128)(2,1)S(1)} %get-tuple-element.114), channel_id=1, source_target_pairs={{0,8},{1,9},{2,10},{3,11},{4,12},{5,13},{6,14},{7,15},{8,0},{9,1},... | collective-permute-start | bytes 491528 | tf_op jit(solution)/shard_map/ppermute | solution.py:430
  94.4 4.3 %value_out_grad.1 = (bf16[1024,1024]{1,0:T(8,128)(2,1)}, bf16[1024,1024]{1,0:T(8,128)(2,1)}) custom-call(f32[64,1024]{1,0:T(8,128)S(1)} %get-tuple-element.111.after.own, bf16[1024,256]{1,0:T(8,128)(2,1)S(1)} %get-tuple-element.116.n0, bf16[1024,256]{1,0:T(8,128)(2,1)S(1)} %get-tuple-element.117.n1, bf16[256,1024]{1,0:T(8,128)(2,1)S(1)} %get-tuple-element.123.v0, ...), custom_call_target="tpu_custom_call" | custom-call | flops 2147483648 | bytes 4194304 | tf_op jit(solution)/shard_map/value_out_grad/pallas_call | solution.py:401
  98.7 4.3 %query_key_grad.1 = (bf16[1024,1024]{1,0:T(8,128)(2,1)}, bf16[1024,1024]{1,0:T(8,128)(2,1)}) custom-call(f32[64,1024]{1,0:T(8,128)S(1)} %get-tuple-element.111.after.own, bf16[1024,256]{1,0:T(8,128)(2,1)S(1)} %get-tuple-element.116.n0, bf16[1024,256]{1,0:T(8,128)(2,1)S(1)} %get-tuple-element.117.n1, bf16[256,1024]{1,0:T(8,128)(2,1)S(1)} %get-tuple-element.118.q0, ...), custom_call_target="tpu_custom_call" | custom-call | flops 2147483648 | bytes 4194304 | tf_op jit(solution)/shard_map/query_key_grad/pallas_call | solution.py:401
  104.7 2.8 %collective-permute-start.28 = (bf16[32,1024]{1,0:T(8,128)(2,1)S(1)}, bf16[32,1024]{1,0:T(8,128)(2,1)S(1)}, u32[]{:S(2)}, u32[]{:S(2)}) collective-permute-start(bf16[32,1024]{1,0:T(8,128)(2,1)S(1)} %get-tuple-element.129), channel_id=1, source_target_pairs={{0,18},{1,19},{2,16},{3,17},{4,22},{5,23},{6,20},{7,21},{8,26},{9,... | collective-permute-start | bytes 196616 | tf_op jit(solution)/shard_map/ppermute | solution.py:430
  107.5 3.9 %collective-permute-start.29 = (bf16[32,1024]{1,0:T(8,128)(2,1)S(1)}, bf16[32,1024]{1,0:T(8,128)(2,1)S(1)}, u32[]{:S(2)}, u32[]{:S(2)}) collective-permute-start(bf16[32,1024]{1,0:T(8,128)(2,1)S(1)} %get-tuple-element.130), channel_id=1, source_target_pairs={{16,32},{17,33},{18,34},{19,35},{20,36},{21,37},{22,38},{23,39},{2... | collective-permute-start | bytes 196616 | tf_op jit(solution)/shard_map/ppermute | solution.py:430
  111.4 4.2 %collective-permute-start.30 = (bf16[32,1024]{1,0:T(8,128)(2,1)S(1)}, bf16[32,1024]{1,0:T(8,128)(2,1)S(1)}, u32[]{:S(2)}, u32[]{:S(2)}) collective-permute-start(bf16[32,1024]{1,0:T(8,128)(2,1)S(1)} %get-tuple-element.130), channel_id=1, source_target_pairs={{16,34},{17,35},{18,32},{19,33},{20,38},{21,39},{22,36},{23,37},{2... | collective-permute-start | bytes 196616 | tf_op jit(solution)/shard_map/ppermute | solution.py:430
  115.6 2.9 %collective-permute-done.30.odd1 = bf16[32,1024]{1,0:T(8,128)(2,1)S(1)} collective-permute-done((bf16[32,1024]{1,0:T(8,128)(2,1)S(1)}, bf16[32,1024]{1,0:T(8,128)(2,1)S(1)}, u32[]{:S(2)}, u32[]{:S(2)}) %collective-permute-start.30) | collective-permute-done | bytes 65568 | tf_op jit(solution)/shard_map/ppermute | solution.py:430
  122.5 3.9 %collective-permute-start.34 = (bf16[64,1024]{1,0:T(8,128)(2,1)S(1)}, bf16[64,1024]{1,0:T(8,128)(2,1)S(1)}, u32[]{:S(2)}, u32[]{:S(2)}) collective-permute-start(bf16[64,1024]{1,0:T(8,128)(2,1)S(1)} %after_shift.3.refs_0_), channel_id=1, source_target_pairs={{0,1},{1,0},{2,3},{3,2},{4,5},{5,4},{6,7},{7,6},{8,9},{9,8},{10,11... | collective-permute-start | bytes 393224 | tf_op jit(solution)/shard_map/ppermute | solution.py:430
  131.1 3.0 %collective-permute-start.38 = (bf16[2,64,256]{2,1,0:T(8,128)(2,1)S(1)}, bf16[2,64,256]{2,1,0:T(8,128)(2,1)S(1)}, u32[]{:S(2)}, u32[]{:S(2)}) collective-permute-start(bf16[2,64,256]{2,1,0:T(8,128)(2,1)S(1)} %pick_share.1), channel_id=1, source_target_pairs={{0,112},{1,113},{2,114},{3,115},{4,116},{5,117},{6,118},{7,119},{8... | collective-permute-start | bytes 196616 | tf_op jit(solution)/shard_map/ppermute | solution.py:430
  134.1 2.9 %collective-permute-done.38.arrived = bf16[2,64,256]{2,1,0:T(8,128)(2,1)S(1)} collective-permute-done((bf16[2,64,256]{2,1,0:T(8,128)(2,1)S(1)}, bf16[2,64,256]{2,1,0:T(8,128)(2,1)S(1)}, u32[]{:S(2)}, u32[]{:S(2)}) %collective-permute-start.38) | collective-permute-done | bytes 65568 | tf_op jit(solution)/shard_map/ppermute | solution.py:430
  137.0 4.7 %collective-permute-start.26 = (bf16[16,1024]{1,0:T(8,128)(2,1)S(1)}, bf16[16,1024]{1,0:T(8,128)(2,1)S(1)}, u32[]{:S(2)}, u32[]{:S(2)}) collective-permute-start(bf16[16,1024]{1,0:T(8,128)(2,1)S(1)} %get-tuple-element.128.gain_rows), channel_id=1, source_target_pairs={{0,2},{1,3},{2,0},{3,1},{4,6},{5,7},{6,4},{7,5},{8,10},{9,11},{10,... | collective-permute-start | bytes 98312 | tf_op jit(solution)/shard_map/ppermute | solution.py:430
  (97 shorter events, 49.6 us)
Async XLA Ops:
  2.7 7.5 %collective-permute-start = (bf16[2,64,256]{2,1,0:T(8,128)(2,1)S(1)}, bf16[2,64,256]{2,1,0:T(8,128)(2,1)S(1)}, u32[]{:S(2)}, u32[]{:S(2)}) collective-permute-start(bf16[2,64,256]{2,1,0:T(8,128)(2,1)S(1)} %pick_held.1), channel_id=1, source_target_pairs={{0,112},{1,113},{2,114},{3,115},{4,116},{5,117},{6,118},{7,119},{8... | collective-permute-start | bytes 196616 | tf_op jit(solution)/shard_map/ppermute | solution.py:430
  11.7 11.6 %collective-permute-start.2 = (bf16[4,64,256]{2,1,0:T(8,128)(2,1)S(1)}, bf16[4,64,256]{2,1,0:T(8,128)(2,1)S(1)}, u32[]{:S(2)}, u32[]{:S(2)}) collective-permute-start(bf16[4,64,256]{2,1,0:T(8,128)(2,1)S(1)} %pick_reload.1.own), channel_id=1, source_target_pairs={{0,4},{1,5},{2,6},{3,7},{4,0},{5,1},{6,2},{7,3},{8,12},{9,13},{10,... | collective-permute-start | bytes 393224 | tf_op jit(solution)/shard_map/ppermute | solution.py:430
  13.0 10.4 %collective-permute-start.3 = (bf16[4,64,256]{2,1,0:T(8,128)(2,1)S(1)}, bf16[4,64,256]{2,1,0:T(8,128)(2,1)S(1)}, u32[]{:S(2)}, u32[]{:S(2)}) collective-permute-start(bf16[4,64,256]{2,1,0:T(8,128)(2,1)S(1)} %pick_reload.1.own), channel_id=1, source_target_pairs={{0,8},{1,9},{2,10},{3,11},{4,12},{5,13},{6,14},{7,15},{8,0},{9,1},... | collective-permute-start | bytes 393224 | tf_op jit(solution)/shard_map/ppermute | solution.py:430
  15.5 7.9 %collective-permute-start.4 = (bf16[4,64,256]{2,1,0:T(8,128)(2,1)S(1)}, bf16[4,64,256]{2,1,0:T(8,128)(2,1)S(1)}, u32[]{:S(2)}, u32[]{:S(2)}) collective-permute-start(bf16[4,64,256]{2,1,0:T(8,128)(2,1)S(1)} %pick_reload.1.own), channel_id=1, source_target_pairs={{0,12},{1,13},{2,14},{3,15},{4,8},{5,9},{6,10},{7,11},{8,4},{9,5},... | collective-permute-start | bytes 393224 | tf_op jit(solution)/shard_map/ppermute | solution.py:430
  39.4 7.7 %collective-permute-start.7 = (bf16[64,1024]{1,0:T(8,128)(2,1)S(1)}, bf16[64,1024]{1,0:T(8,128)(2,1)S(1)}, u32[]{:S(2)}, u32[]{:S(2)}) collective-permute-start(bf16[64,1024]{1,0:T(8,128)(2,1)S(1)} %get-tuple-element.93), channel_id=1, source_target_pairs={{0,4},{1,5},{2,6},{3,7},{4,0},{5,1},{6,2},{7,3},{8,12},{9,13},{10,... | collective-permute-start | bytes 393224 | tf_op jit(solution)/shard_map/ppermute | solution.py:430
  39.4 9.7 %collective-permute-start.8 = (bf16[64,1024]{1,0:T(8,128)(2,1)S(1)}, bf16[64,1024]{1,0:T(8,128)(2,1)S(1)}, u32[]{:S(2)}, u32[]{:S(2)}) collective-permute-start(bf16[64,1024]{1,0:T(8,128)(2,1)S(1)} %get-tuple-element.94), channel_id=1, source_target_pairs={{0,8},{1,9},{2,10},{3,11},{4,12},{5,13},{6,14},{7,15},{8,0},{9,1},... | collective-permute-start | bytes 393224 | tf_op jit(solution)/shard_map/ppermute | solution.py:430
  43.1 8.6 %collective-permute-start.9 = (bf16[64,1024]{1,0:T(8,128)(2,1)S(1)}, bf16[64,1024]{1,0:T(8,128)(2,1)S(1)}, u32[]{:S(2)}, u32[]{:S(2)}) collective-permute-start(bf16[64,1024]{1,0:T(8,128)(2,1)S(1)} %get-tuple-element.95), channel_id=1, source_target_pairs={{0,12},{1,13},{2,14},{3,15},{4,8},{5,9},{6,10},{7,11},{8,4},{9,5},... | collective-permute-start | bytes 393224 | tf_op jit(solution)/shard_map/ppermute | solution.py:430
  52.5 10.4 %collective-permute-start.11 = (bf16[32,1024]{1,0:T(8,128)(2,1)S(1)}, bf16[32,1024]{1,0:T(8,128)(2,1)S(1)}, u32[]{:S(2)}, u32[]{:S(2)}) collective-permute-start(bf16[32,1024]{1,0:T(8,128)(2,1)S(1)} %get-tuple-element.98), channel_id=1, source_target_pairs={{0,16},{1,17},{2,18},{3,19},{4,20},{5,21},{6,22},{7,23},{8,24},{9,... | collective-permute-start | bytes 196616 | tf_op jit(solution)/shard_map/ppermute | solution.py:430
  52.5 10.4 %collective-permute-start.12 = (bf16[32,1024]{1,0:T(8,128)(2,1)S(1)}, bf16[32,1024]{1,0:T(8,128)(2,1)S(1)}, u32[]{:S(2)}, u32[]{:S(2)}) collective-permute-start(bf16[32,1024]{1,0:T(8,128)(2,1)S(1)} %get-tuple-element.98), channel_id=1, source_target_pairs={{0,18},{1,19},{2,16},{3,17},{4,22},{5,23},{6,20},{7,21},{8,26},{9,... | collective-permute-start | bytes 196616 | tf_op jit(solution)/shard_map/ppermute | solution.py:430
  59.2 7.8 %collective-permute-start.14 = (bf16[32,1024]{1,0:T(8,128)(2,1)S(1)}, bf16[32,1024]{1,0:T(8,128)(2,1)S(1)}, u32[]{:S(2)}, u32[]{:S(2)}) collective-permute-start(bf16[32,1024]{1,0:T(8,128)(2,1)S(1)} %get-tuple-element.99), channel_id=1, source_target_pairs={{16,34},{17,35},{18,32},{19,33},{20,38},{21,39},{22,36},{23,37},{2... | collective-permute-start | bytes 196616 | tf_op jit(solution)/shard_map/ppermute | solution.py:430
  68.5 7.5 %collective-permute-start.17 = (bf16[64,1024]{1,0:T(8,128)(2,1)S(1)}, bf16[64,1024]{1,0:T(8,128)(2,1)S(1)}, u32[]{:S(2)}, u32[]{:S(2)}) collective-permute-start(bf16[64,1024]{1,0:T(8,128)(2,1)S(1)} %after_shift.2.refs_0_.z), channel_id=1, source_target_pairs={{0,12},{1,13},{2,14},{3,15},{4,8},{5,9},{6,10},{7,11},{8,4},{9,5},... | collective-permute-start | bytes 393224 | tf_op jit(solution)/shard_map/ppermute | solution.py:430
  90.4 12.6 %collective-permute-start.23 = (bf16[80,1024]{1,0:T(8,128)(2,1)S(1)}, bf16[80,1024]{1,0:T(8,128)(2,1)S(1)}, u32[]{:S(2)}, u32[]{:S(2)}) collective-permute-start(bf16[80,1024]{1,0:T(8,128)(2,1)S(1)} %get-tuple-element.113.after), channel_id=1, source_target_pairs={{0,4},{1,5},{2,6},{3,7},{4,0},{5,1},{6,2},{7,3},{8,12},{9,13},{10,... | collective-permute-start | bytes 491528 | tf_op jit(solution)/shard_map/ppermute | solution.py:430
  91.0 12.1 %collective-permute-start.24 = (bf16[80,1024]{1,0:T(8,128)(2,1)S(1)}, bf16[80,1024]{1,0:T(8,128)(2,1)S(1)}, u32[]{:S(2)}, u32[]{:S(2)}) collective-permute-start(bf16[80,1024]{1,0:T(8,128)(2,1)S(1)} %get-tuple-element.114), channel_id=1, source_target_pairs={{0,8},{1,9},{2,10},{3,11},{4,12},{5,13},{6,14},{7,15},{8,0},{9,1},... | collective-permute-start | bytes 491528 | tf_op jit(solution)/shard_map/ppermute | solution.py:430
  94.2 10.2 %collective-permute-start.25 = (bf16[80,1024]{1,0:T(8,128)(2,1)S(1)}, bf16[80,1024]{1,0:T(8,128)(2,1)S(1)}, u32[]{:S(2)}, u32[]{:S(2)}) collective-permute-start(bf16[80,1024]{1,0:T(8,128)(2,1)S(1)} %get-tuple-element.115), channel_id=1, source_target_pairs={{0,12},{1,13},{2,14},{3,15},{4,8},{5,9},{6,10},{7,11},{8,4},{9,5},... | collective-permute-start | bytes 491528 | tf_op jit(solution)/shard_map/ppermute | solution.py:430
  104.6 11.0 %collective-permute-start.27 = (bf16[32,1024]{1,0:T(8,128)(2,1)S(1)}, bf16[32,1024]{1,0:T(8,128)(2,1)S(1)}, u32[]{:S(2)}, u32[]{:S(2)}) collective-permute-start(bf16[32,1024]{1,0:T(8,128)(2,1)S(1)} %get-tuple-element.129), channel_id=1, source_target_pairs={{0,16},{1,17},{2,18},{3,19},{4,20},{5,21},{6,22},{7,23},{8,24},{9,... | collective-permute-start | bytes 196616 | tf_op jit(solution)/shard_map/ppermute | solution.py:430
  104.7 10.9 %collective-permute-start.28 = (bf16[32,1024]{1,0:T(8,128)(2,1)S(1)}, bf16[32,1024]{1,0:T(8,128)(2,1)S(1)}, u32[]{:S(2)}, u32[]{:S(2)}) collective-permute-start(bf16[32,1024]{1,0:T(8,128)(2,1)S(1)} %get-tuple-element.129), channel_id=1, source_target_pairs={{0,18},{1,19},{2,16},{3,17},{4,22},{5,23},{6,20},{7,21},{8,26},{9,... | collective-permute-start | bytes 196616 | tf_op jit(solution)/shard_map/ppermute | solution.py:430
  107.5 8.1 %collective-permute-start.29 = (bf16[32,1024]{1,0:T(8,128)(2,1)S(1)}, bf16[32,1024]{1,0:T(8,128)(2,1)S(1)}, u32[]{:S(2)}, u32[]{:S(2)}) collective-permute-start(bf16[32,1024]{1,0:T(8,128)(2,1)S(1)} %get-tuple-element.130), channel_id=1, source_target_pairs={{16,32},{17,33},{18,34},{19,35},{20,36},{21,37},{22,38},{23,39},{2... | collective-permute-start | bytes 196616 | tf_op jit(solution)/shard_map/ppermute | solution.py:430
  118.6 7.8 %collective-permute-start.31 = (bf16[64,1024]{1,0:T(8,128)(2,1)S(1)}, bf16[64,1024]{1,0:T(8,128)(2,1)S(1)}, u32[]{:S(2)}, u32[]{:S(2)}) collective-permute-start(bf16[64,1024]{1,0:T(8,128)(2,1)S(1)} %after_shift.3.refs_0_), channel_id=1, source_target_pairs={{0,4},{1,5},{2,6},{3,7},{4,0},{5,1},{6,2},{7,3},{8,12},{9,13},{10,... | collective-permute-start | bytes 393224 | tf_op jit(solution)/shard_map/ppermute | solution.py:430
  118.7 8.0 %collective-permute-start.32 = (bf16[64,1024]{1,0:T(8,128)(2,1)S(1)}, bf16[64,1024]{1,0:T(8,128)(2,1)S(1)}, u32[]{:S(2)}, u32[]{:S(2)}) collective-permute-start(bf16[64,1024]{1,0:T(8,128)(2,1)S(1)} %after_shift.3.refs_0_), channel_id=1, source_target_pairs={{0,8},{1,9},{2,10},{3,11},{4,12},{5,13},{6,14},{7,15},{8,0},{9,1},... | collective-permute-start | bytes 393224 | tf_op jit(solution)/shard_map/ppermute | solution.py:430
  121.0 8.0 %collective-permute-start.33 = (bf16[64,1024]{1,0:T(8,128)(2,1)S(1)}, bf16[64,1024]{1,0:T(8,128)(2,1)S(1)}, u32[]{:S(2)}, u32[]{:S(2)}) collective-permute-start(bf16[64,1024]{1,0:T(8,128)(2,1)S(1)} %after_shift.3.refs_0_), channel_id=1, source_target_pairs={{0,12},{1,13},{2,14},{3,15},{4,8},{5,9},{6,10},{7,11},{8,4},{9,5},... | collective-permute-start | bytes 393224 | tf_op jit(solution)/shard_map/ppermute | solution.py:430
  122.5 20.5 %collective-permute-start.34 = (bf16[64,1024]{1,0:T(8,128)(2,1)S(1)}, bf16[64,1024]{1,0:T(8,128)(2,1)S(1)}, u32[]{:S(2)}, u32[]{:S(2)}) collective-permute-start(bf16[64,1024]{1,0:T(8,128)(2,1)S(1)} %after_shift.3.refs_0_), channel_id=1, source_target_pairs={{0,1},{1,0},{2,3},{3,2},{4,5},{5,4},{6,7},{7,6},{8,9},{9,8},{10,11... | collective-permute-start | bytes 393224 | tf_op jit(solution)/shard_map/ppermute | solution.py:430
  126.4 16.6 %collective-permute-start.35 = (bf16[64,1024]{1,0:T(8,128)(2,1)S(1)}, bf16[64,1024]{1,0:T(8,128)(2,1)S(1)}, u32[]{:S(2)}, u32[]{:S(2)}) collective-permute-start(bf16[64,1024]{1,0:T(8,128)(2,1)S(1)} %collective-permute-done.31.refs_1_), channel_id=1, source_target_pairs={{0,1},{1,0},{2,3},{3,2},{4,5},{5,4},{6,7},{7,6},{8,9},{9,8},{10,11... | collective-permute-start | bytes 393224 | tf_op jit(solution)/shard_map/ppermute | solution.py:430
  126.7 16.4 %collective-permute-start.36 = (bf16[64,1024]{1,0:T(8,128)(2,1)S(1)}, bf16[64,1024]{1,0:T(8,128)(2,1)S(1)}, u32[]{:S(2)}, u32[]{:S(2)}) collective-permute-start(bf16[64,1024]{1,0:T(8,128)(2,1)S(1)} %collective-permute-done.32.refs_2_), channel_id=1, source_target_pairs={{0,1},{1,0},{2,3},{3,2},{4,5},{5,4},{6,7},{7,6},{8,9},{9,8},{10,11... | collective-permute-start | bytes 393224 | tf_op jit(solution)/shard_map/ppermute | solution.py:430
  129.0 14.0 %collective-permute-start.37 = (bf16[64,1024]{1,0:T(8,128)(2,1)S(1)}, bf16[64,1024]{1,0:T(8,128)(2,1)S(1)}, u32[]{:S(2)}, u32[]{:S(2)}) collective-permute-start(bf16[64,1024]{1,0:T(8,128)(2,1)S(1)} %collective-permute-done.33.refs_3_), channel_id=1, source_target_pairs={{0,1},{1,0},{2,3},{3,2},{4,5},{5,4},{6,7},{7,6},{8,9},{9,8},{10,11... | collective-permute-start | bytes 393224 | tf_op jit(solution)/shard_map/ppermute | solution.py:430
  (25 other events, 175.7 us)

commit v3 on v2

--- a/solution.py
+++ b/solution.py
@@ -114,7 +114,7 @@
     run_copies(pairs, sems)
 
 
-def turn_first(slots, current, shares, flag, turned):
+def turn_first(slots, current, gain, shares, flag, current_out, gain_out, turned):
     section, head = lax.axis_index("section"), lax.axis_index("head")
     share = shares.shape[1]
     turned[...] = current[...].T
@@ -122,6 +122,8 @@
     shares[1] = turned[at_rows((head ^ 2) * share, share), :]
     same = jnp.where(slots[0, section] == slots[1, section], 1.0, 0.0)
     flag[...] = jnp.full(flag.shape, same, F32)
+    current_out[...] = current[...]
+    gain_out[...] = gain[...]
 
 
 def pick_reload(near, far, shares, flag, both):
@@ -132,7 +134,7 @@
         both[2 + y] = jnp.where(same, shares[y].astype(F32), ref[1].astype(F32)).astype(BF16)
 
 
-def part_reload(own, got1, got2, got3, after, first, second):
+def part_reload(own, got2, got1, got3, after, first, second):
     for j, ref in enumerate((own, got1, got2, got3)):
         first[2 * j : 2 * j + 2] = ref[0:2]
         second[2 * j : 2 * j + 2] = ref[2:4]
@@ -143,13 +145,6 @@
     turned[...] = current[...].T
     out[0] = first_shares[0]
     out[1] = turned[at_rows(lax.axis_index("head") * share, share), :]
-
-
-def put_store(slots, store, arrived, out):
-    mirror = lax.axis_size("section") - 1 - lax.axis_index("section")
-    out[...] = store[...]
-    for t in range(TICKS):
-        out[slots[t, mirror]] = arrived[t]
 
 
 def attend_and_project(n, total, keep_ref, send_ref, wq, wk, wv, wo, q, k, v, context, ready):
@@ -202,8 +197,12 @@
     attend_and_project(n, total, keep, send, wq, wk, wv, wo, q, k, v, context, lambda i: None)
 
 
-def put_last(gain_rows, gain_other, *refs):
-    pieces, (rows, g, gain_out) = refs[:8], refs[8:]
+def put_last(slots, store, arrived, gain_rows, gain_other, *refs):
+    pieces, (rows, g, stored, gain_out) = refs[:8], refs[8:]
+    mirror = lax.axis_size("section") - 1 - lax.axis_index("section")
+    stored[...] = store[...]
+    for t in range(TICKS):
+        stored[slots[t, mirror]] = arrived[t]
     put_pieces(pieces, rows, g)
     value = get_gain(gain_rows, 0) + get_gain(gain_other, 0)
     share = gain_out.shape[1]
@@ -215,8 +214,7 @@
 
 
 def recompute_kernel(gain, wq, wk, wv, *refs):
-    mine, other, block_ref, normed_out, q, k, v, soft, context_out = refs[:9]
-    block_t, normed_t, context, sems = refs[-4:]
+    mine, other, block_ref, normed_t, q, k, v, soft, context, block_t = refs
     core, high, column, _ = where_am_i()
     share = mine.shape[1]
     for ref, c in ((mine, core), (other, 1 - core)):
@@ -227,8 +225,6 @@
     block_ref[...] = block
     n = normalize(block, gain[...])[0].astype(BF16)
     normed_t[...] = n.T
-    first = pltpu.make_async_copy(normed_t, normed_out, sems.at[0])
-    first.start()
     q[...] = dot(n, wq[...]).astype(BF16)
     k[...] = dot(n, wk[...]).astype(BF16)
     v[...] = dot(n, wv[...]).astype(BF16)
@@ -237,17 +233,13 @@
         rows = softmax(q[:, at], k[:, at])
         soft[i] = rows
         context[:, at] = dot(rows.astype(BF16), v[:, at]).astype(BF16)
-    second = pltpu.make_async_copy(context, context_out, sems.at[1])
-    second.start()
-    first.wait()
-    second.wait()
 
 
 def backward_kernel(
     g, block, gain, q, k, v, soft, wq, wk, wv, wo, ahead_keep, ahead_send, gain_before,
     *refs,
 ):
-    keep, send, qg_out, kg_out, vg_out, gain_part, qg, kg, vg, grads, total, sems = refs[-12:]
+    keep, send, qg, kg, vg, gain_part, grads, total = refs
     grads[...] = dot_nt(g[...], wo[...]).astype(BF16)
     for i in range(q.shape[1] // DK):
         at = lanes(i)
@@ -259,12 +251,6 @@
         score_grad = (rows * (soft_grad - along) * SCALE).astype(BF16)
         qg[:, at] = dot(score_grad, k[:, at]).astype(BF16)
         kg[:, at] = dot_tn(score_grad, q[:, at]).astype(BF16)
-    copies = [
-        pltpu.make_async_copy(src, dst, sems.at[i])
-        for i, (src, dst) in enumerate(((qg, qg_out), (kg, kg_out), (vg, vg_out)))
-    ]
-    for copy in copies:
-        copy.start()
     total[...] = dot_nt(qg[...], wq[...])
     total[...] += dot_nt(kg[...], wk[...])
     total[...] += dot_nt(vg[...], wv[...])
@@ -279,8 +265,6 @@
     gain_part[...] = part
     if send.shape[0] > 2 * half:
         put_gain(send, 2 * half, part)
-    for copy in copies:
-        copy.wait()
 
 
 def put_gain(ref, row, value):
@@ -315,7 +299,7 @@
         gain_out[...] = gain_part[...]
 
 
-def after_column(own, z, block, gain, gain_part, got1, got2, got3, *refs):
+def after_column(own, z, block, gain, gain_part, got2, got1, got3, *refs):
     even, odd, gain_out = refs[-3:]
     core, high, column, section = where_am_i()
     rows = z.shape[0] // 2
@@ -352,7 +336,8 @@
         put_gain(gain_out, 0, gain_part[...])
 
 
-def after_shift(even0, even1, odd0, odd1, fresh, z):
+def after_shift(even0, odd0, even1, odd1, fresh, *refs):
+    z = refs[-1]
     section = where_am_i()[3]
     rows = even0.shape[0]
     even = (even0[...].astype(F32) + even1[...].astype(F32)).astype(BF16)
@@ -377,44 +362,41 @@
         z[rows:, :] = fresh[rows:, :]
 
 
-def query_key_kernel(after, n0, n1, q0, q1, k0, k1, dq, dk):
-    dq[...] = (dot(n0[...], q0[...]) + dot(n1[...], q1[...])).astype(BF16)
-    dk[...] = (dot(n0[...], k0[...]) + dot(n1[...], k1[...])).astype(BF16)
-
-
-def value_out_kernel(after, n0, n1, v0, v1, c0, c1, g0, g1, dv, do):
-    dv[...] = (dot(n0[...], v0[...]) + dot(n1[...], v1[...])).astype(BF16)
-    do[...] = (dot_tn(c0[...], g0[...]) + dot_tn(c1[...], g1[...])).astype(BF16)
-
-
-def weight_grads(body, name, after, normed_t, blocked, fixed, by_rows):
+def step_lanes(ref):
+    width = ref.shape[1] // pl.num_programs(0)
+    return ref[:, pl.ds(pl.multiple_of(pl.program_id(0) * width, width), width)]
+
+
+def weight_kernel(after, n0, n1, a0, a1, out):
+    out[...] = (dot(n0[...], step_lanes(a0)) + dot(n1[...], step_lanes(a1))).astype(BF16)
+
+
+def out_weight_kernel(after, c0, c1, g0, g1, out):
+    out[...] = (dot_tn(step_lanes(c0), g0[...]) + dot_tn(step_lanes(c1), g1[...])).astype(BF16)
+
+
+def weight_grad(name, after, left, right, by_rows=False):
     steps = 4
-    width, tokens = normed_t[0].shape
-    inner = blocked[0].shape[1]
-    block = inner // steps
-    args = [after, *normed_t, *blocked, *fixed]
-    outs = [pl.BlockSpec((width, block), lambda i: (0, i))] * 2
-    shapes = [shape(BF16, width, inner)] * 2
+    tokens, cols = right[0].shape
+    rows = left[0].shape[1] if by_rows else left[0].shape[0]
     if by_rows:
-        outs[1] = pl.BlockSpec((block, width), lambda i: (i, 0))
-        shapes[1] = shape(BF16, inner, width)
+        out = pl.BlockSpec((rows // steps, cols), lambda i: (i, 0))
+    else:
+        out = pl.BlockSpec((rows, cols // steps), lambda i: (0, i))
     return pl.pallas_call(
-        body,
+        out_weight_kernel if by_rows else weight_kernel,
         grid=(steps,),
-        in_specs=[pl.BlockSpec(memory_space=pl.ANY)]
-        + [pl.BlockSpec((width, tokens), lambda i: (0, 0))] * 2
-        + [pl.BlockSpec((tokens, block), lambda i: (0, i))] * len(blocked)
-        + [pl.BlockSpec((tokens, width), lambda i: (0, 0))] * len(fixed),
-        out_specs=outs,
-        out_shape=shapes,
+        in_specs=[pl.BlockSpec(memory_space=pl.ANY)] + [VMEM] * 4,
+        out_specs=out,
+        out_shape=shape(BF16, rows, cols),
         compiler_params=pltpu.CompilerParams(
             dimension_semantics=("arbitrary",), vmem_limit_bytes=16 * MIB
         ),
         cost_estimate=pl.CostEstimate(
-            flops=8 * tokens * width * inner, bytes_accessed=4 * width * inner, transcendentals=0
+            flops=4 * tokens * rows * cols, bytes_accessed=2 * rows * cols, transcendentals=0
         ),
         name=name,
-    )(*args)
+    )(after, *left, *right)
 
 
 class Moves:
@@ -469,16 +451,20 @@
         [kept(BF16, 2 * rows, width)] * (1 + TICKS),
         [pltpu.SemaphoreType.DMA((2 + 2 * TICKS,))], 0, 4,
     )
-    first_shares, flag = kernel_call(
-        turn_first, "turn_first", (reload_slot, current),
-        [kept(BF16, 2, share, tokens), kept(F32, 8, tokens)],
+    first_shares, flag, first_inputs, gain = kernel_call(
+        turn_first, "turn_first", (reload_slot, current, gain),
+        [
+            kept(BF16, 2, share, tokens), kept(F32, 8, tokens),
+            kept(BF16, tokens, width), kept(F32, 1, width),
+        ],
         [pltpu.VMEM((width, tokens), BF16)], 1,
     )
     (both,) = kernel_call(
         pick_reload, "pick_reload", (near, far, first_shares, flag),
         [kept(BF16, 2 * TICKS, share, tokens)],
     )
-    arriving = [both] + [moves.flip(both, 4 * j) for j in (1, 2, 3)]
+    far_shares = moves.flip(both, 8)
+    arriving = [both, far_shares, moves.flip(both, 4), moves.flip(both, 12)]
 
     flat = kept(BF16, tokens, inner)
     whole = kept(BF16, tokens, width)
@@ -495,10 +481,7 @@
                 whole, kept(BF16, width, tokens), flat, flat, flat,
                 kept(F32, inner // DK, tokens, tokens), flat,
             ],
-            [
-                pltpu.VMEM((width, tokens), BF16), pltpu.VMEM((width, tokens), BF16),
-                pltpu.VMEM((tokens, inner), BF16), pltpu.SemaphoreType.DMA((2,)),
-            ], 0, 0, 5 * unit_flops,
+            [pltpu.VMEM((width, tokens), BF16)], 0, 0, 5 * unit_flops,
         )
 
     for t in range(TICKS):
@@ -507,7 +490,7 @@
                 from_hbm(w[0]) for w in (query_weight, key_weight, value_weight, out_weight)
             ]
             *weights, keep, send = kernel_call(
-                forward_first, "forward_first", (current, gain, *raw),
+                forward_first, "forward_first", (first_inputs, gain, *raw),
                 [kept(BF16, *w.shape) for w in raw] + half_outs,
                 work + [pltpu.SemaphoreType.DMA((4,))], 0, 4, 5 * unit_flops,
             )
@@ -531,8 +514,7 @@
             (upstream, block, gain, q, k, v, soft, wq, wk, wv, wo, keep, send, gain_part),
             [kept(F32, tokens, width), kept(BF16, tokens + extra, width)]
             + [flat] * 3 + [kept(F32, 1, width)],
-            [pltpu.VMEM((tokens, inner), BF16)] * 4
-            + [pltpu.VMEM((tokens, width), F32), pltpu.SemaphoreType.DMA((3,))],
+            [pltpu.VMEM((tokens, inner), BF16), pltpu.VMEM((tokens, width), F32)],
             0, 0, 6 * unit_flops,
         )
         left.append(normed_t)
@@ -541,53 +523,53 @@
         cotangents.append(upstream)
 
         got = moves.flip(send, 1)
+        last = t == TICKS - 1
+        if last:
+            grads_of = [[grads_of[u][i] for u in range(TICKS)] for i in range(3)]
+            query_grad = weight_grad("query_grad", gain_part, left, grads_of[0])
+        beside = [from_hbm(query_grad)] if last else []
         own, to1, to2, to3, gain_sum = kernel_call(
-            after_core, "after_core", (keep, got, gain_part),
+            after_core, "after_core", (keep, got, gain_part, *beside),
             [kept(F32, 2 * rows, width)] + [kept(BF16, 2 * rows + extra, width)] * 3 + [kept(F32, 1, width)],
-            [pltpu.VMEM((tokens, width), F32)],
+            [pltpu.VMEM((tokens, width), F32)], 0, len(beside),
         )
-        got1, got2, got3 = moves.flip(to1, 4), moves.flip(to2, 8), moves.flip(to3, 12)
-        if t == 0:
+        got2 = moves.flip(to2, 8)
+        got1, got3 = moves.flip(to1, 4), moves.flip(to3, 12)
+        if last:
+            key_grad = weight_grad("key_grad", own, left, grads_of[1])
+            value_grad = weight_grad("value_grad", own, left, grads_of[2])
+            (shares,) = kernel_call(
+                pick_share, "pick_share", (first_shares, current, from_hbm(key_grad)), [kept(BF16, 2, share, tokens)],
+                [pltpu.VMEM((width, tokens), BF16)], 0, 1,
+            )
+            arrived = moves.mirror(shares, 0)
+            beside = [from_hbm(key_grad), from_hbm(value_grad), arrived]
+        else:
             read.append(recompute(1))
             beside = [read[1][5]]
-        else:
-            query_grad, key_grad = weight_grads(
-                query_key_kernel, "query_key_grad", own, left,
-                [grads_of[u][i] for i in range(2) for u in range(TICKS)], [], False,
-            )
-            value_grad, out_grad = weight_grads(
-                value_out_kernel, "value_out_grad", own, left,
-                [grads_of[u][2] for u in range(TICKS)] + context, cotangents, True,
-            )
-            beside = [from_hbm(query_grad), from_hbm(value_grad)]
         even, odd, gain_rows = kernel_call(
             after_column, "after_column",
-            (own, z, block, gain, gain_sum, got1, got2, got3, *beside),
+            (own, z, block, gain, gain_sum, got2, got1, got3, *beside),
             [kept(BF16, rows, width)] * 2 + [kept(BF16, 16, width)], (), 0, len(beside),
         )
         even0, odd0 = moves.even(even, 0), moves.odd(odd, 0)
         even1, odd1 = moves.even(even, 2), moves.odd(odd, 2)
+        if last:
+            out_grad = weight_grad("out_grad", even, context, cotangents, True)
+            gain_other = moves.flip(gain_rows, 2)
+            beside = [gain_other, from_hbm(out_grad)]
+        else:
+            beside = []
         (z,) = kernel_call(
-            after_shift, "after_shift",
-            (even0, even1, odd0, odd1, fresh[t]),
-            [kept(BF16, 2 * rows, width)],
+            after_shift, "after_shift", (even0, odd0, even1, odd1, fresh[t], *beside),
+            [kept(BF16, 2 * rows, width)], (), 0, len(beside),
         )
         pieces = [z] + [moves.flip(z, 4 * j) for j in (1, 2, 3)]
         pieces = pieces + [moves.flip(p, 1) for p in pieces]
-    last_inputs, last_cotangents, gain_grad = kernel_call(
-        put_last, "put_last", (gain_rows, moves.flip(gain_rows, 2), *pieces),
-        [shape(BF16, tokens, width)] * 2 + [shape(F32, 1, share)],
-    )
-
-    (shares,) = kernel_call(
-        pick_share, "pick_share", (first_shares, current, to1), [kept(BF16, 2, share, tokens)],
-        [pltpu.VMEM((width, tokens), BF16)], 0, 1,
-    )
-    (stored,) = kernel_call(
-        put_store, "put_store", (reload_slot, store, moves.mirror(shares, 0)),
-        [shape(BF16, *store.shape)], (), 1,
-    )
-
+    last_inputs, last_cotangents, stored, gain_grad = kernel_call(
+        put_last, "put_last", (reload_slot, store, arrived, gain_rows, gain_other, *pieces),
+        [shape(BF16, tokens, width)] * 2 + [shape(BF16, *store.shape), shape(F32, 1, share)], (), 1,
+    )
     return (
         last_inputs[None],
         last_cotangents[None],

time: 147 us -> 131 us (0.89); the launches traced: 144 us -> 130 us
  waiting for transfers between devices: 21.5 us -> 12 us
  starting transfers between devices: 72.9 us -> 69.7 us
  local copies, waits for them, and re-layouts: 4.15 us -> 2.42 us
    ppermute x39, waiting for transfers between devices: 21.5 us -> 12 us  [send(): return lax.ppermute(value, ('section', 'head'), pairs)]
    pallas_call x2 -> x4, Pallas kernels: 8.67 us -> 11.8 us  [weight_grad(): pl.pallas_call(out_weight_kernel if by_rows else weight_kernel, grid=(ste...]
    ppermute x39, starting transfers between devices: 72.9 us -> 69.7 us  [send(): return lax.ppermute(value, ('section', 'head'), pairs)]
    pallas_call x20 -> x19, Pallas kernels: 36 us -> 33.5 us  [kernel_call(): pl.pallas_call(body, in_specs=[SMEM] * scalars + [VMEM] * (len(args) - sc...]
    unnamed x20 -> x14, local copies, waits for them, and re-layouts: 4.14 us -> 2.42 us
  transfers between devices with their start and end apart: 39 -> 39, of which waited for: 13 -> 9; matrix products, arithmetic and copies ran while one was open for 0% -> 0% of each run, Pallas kernels for 15% -> 18%
where the time goes in v3:
time: 131 us; the launch traced here: 130 us
  starting transfers between devices  69.7 us (53%)
  Pallas kernels  45.4 us (35%)
  waiting for transfers between devices  12 us (9%)
  local copies, waits for them, and re-layouts  2.42 us (2%)
    ppermute x39, starting transfers between devices, send(): return lax.ppermute(value, ('section', 'head'), pairs)  69.7 us
    pallas_call x19, Pallas kernels, kernel_call(): pl.pallas_call(body, in_specs=[SMEM] * scalars + [VMEM] * (len(args) - sc...  33.5 us
    ppermute x39, waiting for transfers between devices, send(): return lax.ppermute(value, ('section', 'head'), pairs)  12 us
    pallas_call x4, Pallas kernels, weight_grad(): pl.pallas_call(out_weight_kernel if by_rows else weight_kernel, grid=(ste...  11.8 us
  transfers between devices with their start and end apart: 39, of which 9 were waited for; matrix products, arithmetic and copies ran while one was open for 0% of the time, Pallas kernels for 18%

profile of v3, /device:TPU:9, one launch (start us, length us, event | category | flops | bytes accessed | tf_op | source)
XLA Modules:
  0.0 130.4 jit_solution(3021610090117671643)
XLA Ops:
  2.7 3.8 %collective-permute-start = (bf16[2,64,256]{2,1,0:T(8,128)(2,1)S(1)}, bf16[2,64,256]{2,1,0:T(8,128)(2,1)S(1)}, u32[]{:S(2)}, u32[]{:S(2)}) collective-permute-start(bf16[2,64,256]{2,1,0:T(8,128)(2,1)S(1)} %pick_held.1), channel_id=1, source_target_pairs={{0,112},{1,113},{2,114},{3,115},{4,116},{5,117},{6,118},{7,119},{8... | collective-permute-start | bytes 196616 | tf_op jit(solution)/shard_map/ppermute | solution.py:412
  11.7 2.8 %collective-permute-start.2 = (bf16[4,64,256]{2,1,0:T(8,128)(2,1)S(1)}, bf16[4,64,256]{2,1,0:T(8,128)(2,1)S(1)}, u32[]{:S(2)}, u32[]{:S(2)}) collective-permute-start(bf16[4,64,256]{2,1,0:T(8,128)(2,1)S(1)} %pick_reload.1.own), channel_id=1, source_target_pairs={{0,8},{1,9},{2,10},{3,11},{4,12},{5,13},{6,14},{7,15},{8,0},{9,1},... | collective-permute-start | bytes 393224 | tf_op jit(solution)/shard_map/ppermute | solution.py:412
  15.4 6.0 %forward_first.1 = (bf16[1024,1024]{1,0:T(8,128)(2,1)S(1)}, bf16[1024,1024]{1,0:T(8,128)(2,1)S(1)}, bf16[1024,1024]{1,0:T(8,128)(2,1)S(1)}, bf16[1024,1024]{1,0:...) custom-call(bf16[256,1024]{1,0:T(8,128)(2,1)S(1)} %get-tuple-element.74.rows, ...), custom_call_target="tpu_custom_call" | custom-call | flops 2684354560 | bytes 8916992 | tf_op jit(solution)/shard_map/forward_first/pallas_call | solution.py:72
  21.5 2.9 %collective-permute-start.5 = (bf16[8,64,256]{2,1,0:T(8,128)(2,1)S(1)}, bf16[8,64,256]{2,1,0:T(8,128)(2,1)S(1)}, u32[]{:S(2)}, u32[]{:S(2)}) collective-permute-start(bf16[8,64,256]{2,1,0:T(8,128)(2,1)S(1)} %get-tuple-element.81.refs_0_), channel_id=1, source_target_pairs={{0,1},{1,0},{2,3},{3,2},{4,5},{5,4},{6,7},{7,6},{8,9},{9,8},{10,11... | collective-permute-start | bytes 786440 | tf_op jit(solution)/shard_map/ppermute | solution.py:412
  25.5 3.2 %recompute.2 = (bf16[256,1024]{1,0:T(8,128)(2,1)S(1)}, bf16[1024,256]{1,0:T(8,128)(2,1)S(1)}, bf16[256,1024]{1,0:T(8,128)(2,1)S(1)}, bf16[256,1024]{1,0:T(8,128)...) custom-call(f32[1,1024]{1,0:T(1,128)S(1)} %get-tuple-element.73.gain, ...), custom_call_target="tpu_custom_call" | custom-call | flops 2684354560 | bytes 6819840 | tf_op jit(solution)/shard_map/recompute/pallas_call | solution.py:72
  28.8 5.2 %backward.2 = (f32[256,1024]{1,0:T(8,128)S(1)}, bf16[256,1024]{1,0:T(8,128)(2,1)S(1)}, bf16[256,1024]{1,0:T(8,128)(2,1)S(1)}, bf16[256,1024]{1,0:T(8,128)(2,1)S(...) custom-call(bf16[256,1024]{1,0:T(8,128)(2,1)S(1)} %bitcast.19, bf16[256,1024]{1,0:T(8,128)(2,1)S(1)} %get-tuple-element.82.block, ...), custom_call_target="tpu_custom_call" | custom-call | flops 3221225472 | bytes 13901824 | tf_op jit(solution)/shard_map/backward/pallas_call | solution.py:72
  39.8 3.2 %recompute.3 = (bf16[256,1024]{1,0:T(8,128)(2,1)S(1)}, bf16[1024,256]{1,0:T(8,128)(2,1)S(1)}, bf16[256,1024]{1,0:T(8,128)(2,1)S(1)}, bf16[256,1024]{1,0:T(8,128)...) custom-call(f32[1,1024]{1,0:T(1,128)S(1)} %get-tuple-element.73.gain, ...), custom_call_target="tpu_custom_call" | custom-call | flops 2684354560 | bytes 6819840 | tf_op jit(solution)/shard_map/recompute/pallas_call | solution.py:72
  46.3 3.6 %collective-permute-start.12 = (bf16[32,1024]{1,0:T(8,128)(2,1)S(1)}, bf16[32,1024]{1,0:T(8,128)(2,1)S(1)}, u32[]{:S(2)}, u32[]{:S(2)}) collective-permute-start(bf16[32,1024]{1,0:T(8,128)(2,1)S(1)} %get-tuple-element.100), channel_id=1, source_target_pairs={{16,32},{17,33},{18,34},{19,35},{20,36},{21,37},{22,38},{23,39},{2... | collective-permute-start | bytes 196616 | tf_op jit(solution)/shard_map/ppermute | solution.py:412
  49.9 3.1 %collective-permute-start.13 = (bf16[32,1024]{1,0:T(8,128)(2,1)S(1)}, bf16[32,1024]{1,0:T(8,128)(2,1)S(1)}, u32[]{:S(2)}, u32[]{:S(2)}) collective-permute-start(bf16[32,1024]{1,0:T(8,128)(2,1)S(1)} %get-tuple-element.99), channel_id=1, source_target_pairs={{0,18},{1,19},{2,16},{3,17},{4,22},{5,23},{6,20},{7,21},{8,26},{9,... | collective-permute-start | bytes 196616 | tf_op jit(solution)/shard_map/ppermute | solution.py:412
  53.0 3.8 %collective-permute-start.14 = (bf16[32,1024]{1,0:T(8,128)(2,1)S(1)}, bf16[32,1024]{1,0:T(8,128)(2,1)S(1)}, u32[]{:S(2)}, u32[]{:S(2)}) collective-permute-start(bf16[32,1024]{1,0:T(8,128)(2,1)S(1)} %get-tuple-element.100), channel_id=1, source_target_pairs={{16,34},{17,35},{18,32},{19,33},{20,38},{21,39},{22,36},{23,37},{2... | collective-permute-start | bytes 196616 | tf_op jit(solution)/shard_map/ppermute | solution.py:412
  56.8 3.3 %collective-permute-done.14.odd1 = bf16[32,1024]{1,0:T(8,128)(2,1)S(1)} collective-permute-done((bf16[32,1024]{1,0:T(8,128)(2,1)S(1)}, bf16[32,1024]{1,0:T(8,128)(2,1)S(1)}, u32[]{:S(2)}, u32[]{:S(2)}) %collective-permute-start.14) | collective-permute-done | bytes 65568 | tf_op jit(solution)/shard_map/ppermute | solution.py:412
  61.5 2.8 %collective-permute-start.16 = (bf16[64,1024]{1,0:T(8,128)(2,1)S(1)}, bf16[64,1024]{1,0:T(8,128)(2,1)S(1)}, u32[]{:S(2)}, u32[]{:S(2)}) collective-permute-start(bf16[64,1024]{1,0:T(8,128)(2,1)S(1)} %after_shift.2.refs_0_.z), channel_id=1, source_target_pairs={{0,8},{1,9},{2,10},{3,11},{4,12},{5,13},{6,14},{7,15},{8,0},{9,1},... | collective-permute-start | bytes 393224 | tf_op jit(solution)/shard_map/ppermute | solution.py:412
  64.3 3.6 %collective-permute-start.18 = (bf16[64,1024]{1,0:T(8,128)(2,1)S(1)}, bf16[64,1024]{1,0:T(8,128)(2,1)S(1)}, u32[]{:S(2)}, u32[]{:S(2)}) collective-permute-start(bf16[64,1024]{1,0:T(8,128)(2,1)S(1)} %after_shift.2.refs_0_.z), channel_id=1, source_target_pairs={{0,1},{1,0},{2,3},{3,2},{4,5},{5,4},{6,7},{7,6},{8,9},{9,8},{10,11... | collective-permute-start | bytes 393224 | tf_op jit(solution)/shard_map/ppermute | solution.py:412
  68.7 2.9 %collective-permute-start.20 = (bf16[64,1024]{1,0:T(8,128)(2,1)S(1)}, bf16[64,1024]{1,0:T(8,128)(2,1)S(1)}, u32[]{:S(2)}, u32[]{:S(2)}) collective-permute-start(bf16[64,1024]{1,0:T(8,128)(2,1)S(1)} %collective-permute-done.16.refs_2_), channel_id=1, source_target_pairs={{0,1},{1,0},{2,3},{3,2},{4,5},{5,4},{6,7},{7,6},{8,9},{9,8},{10,11... | collective-permute-start | bytes 393224 | tf_op jit(solution)/shard_map/ppermute | solution.py:412
  74.3 4.0 %forward_next.1 = (bf16[256,1024]{1,0:T(8,128)(2,1)S(1)}, bf16[256,1024]{1,0:T(8,128)(2,1)S(1)}, f32[128,1024]{1,0:T(8,128)S(1)}, bf16[128,1024]{1,0:T(8,128)(2,1)S(1)}) custom-call(f32[1,1024]{1,0:T(1,128)S(1)} %get-tuple-element.73.gain, bf16[1024,1024]{1,0:T(8,128)(2,1)S(1)} %get-tuple-element.75.wq, bf16[1024,1024]{1,0:T(8,128)(2,1)S(1)} %get-tuple-element.76.wk, ...), custom_call_target="tpu_custom_call" | custom-call | flops 2684354560 | bytes 9441280 | tf_op jit(solution)/shard_map/forward_next/pallas_call | solution.py:72
  78.3 5.2 %backward.3 = (f32[256,1024]{1,0:T(8,128)S(1)}, bf16[272,1024]{1,0:T(8,128)(2,1)S(1)}, bf16[256,1024]{1,0:T(8,128)(2,1)S(1)}, bf16[256,1024]{1,0:T(8,128)(2,1)S(...) custom-call(bf16[256,1024]{1,0:T(8,128)(2,1)S(1)} %get-tuple-element.103.g.g1, ...), custom_call_target="tpu_custom_call" | custom-call | flops 3221225472 | bytes 13901824 | tf_op jit(solution)/shard_map/backward/pallas_call | solution.py:72
  83.9 2.9 %query_grad.1.refs_0_ = bf16[1024,1024]{1,0:T(8,128)(2,1)} custom-call(f32[1,1024]{1,0:T(1,128)S(1)} %get-tuple-element.112.after.gain_part, bf16[1024,256]{1,0:T(8,128)(2,1)S(1)} %get-tuple-element.113.n0, bf16[1024,256]{1,0:T(8,128)(2,1)S(1)} %get-tuple-element.114.n1, bf16[256,1024]{1,0:T(8,128)(2,1)S(1)} %get-tuple-element.115.a0, ...), custom_call_target="tpu_custom_call" | custom-call | flops 1073741824 | bytes 2097152 | tf_op jit(solution)/shard_map/query_grad/pallas_call | solution.py:386
  90.4 2.9 %key_grad.1.after.refs_0_ = bf16[1024,1024]{1,0:T(8,128)(2,1)} custom-call(f32[64,1024]{1,0:T(8,128)S(1)} %get-tuple-element.117.after.own, bf16[1024,256]{1,0:T(8,128)(2,1)S(1)} %get-tuple-element.113.n0, bf16[1024,256]{1,0:T(8,128)(2,1)S(1)} %get-tuple-element.114.n1, bf16[256,1024]{1,0:T(8,128)(2,1)S(1)} %get-tuple-element.118.a0, ...), custom_call_target="tpu_custom_call" | custom-call | flops 1073741824 | bytes 2097152 | tf_op jit(solution)/shard_map/key_grad/pallas_call | solution.py:386
  93.5 3.7 %collective-permute-start.23 = (bf16[2,64,256]{2,1,0:T(8,128)(2,1)S(1)}, bf16[2,64,256]{2,1,0:T(8,128)(2,1)S(1)}, u32[]{:S(2)}, u32[]{:S(2)}) collective-permute-start(bf16[2,64,256]{2,1,0:T(8,128)(2,1)S(1)} %pick_share.1), channel_id=1, source_target_pairs={{0,112},{1,113},{2,114},{3,115},{4,116},{5,117},{6,118},{7,119},{8... | collective-permute-start | bytes 196616 | tf_op jit(solution)/shard_map/ppermute | solution.py:412
  97.2 2.9 %value_grad.1.refs_1_ = bf16[1024,1024]{1,0:T(8,128)(2,1)} custom-call(f32[64,1024]{1,0:T(8,128)S(1)} %get-tuple-element.117.after.own, bf16[1024,256]{1,0:T(8,128)(2,1)S(1)} %get-tuple-element.113.n0, bf16[1024,256]{1,0:T(8,128)(2,1)S(1)} %get-tuple-element.114.n1, bf16[256,1024]{1,0:T(8,128)(2,1)S(1)} %get-tuple-element.124.a0, ...), custom_call_target="tpu_custom_call" | custom-call | flops 1073741824 | bytes 2097152 | tf_op jit(solution)/shard_map/value_grad/pallas_call | solution.py:386
  101.7 4.5 %collective-permute-start.29 = (bf16[32,1024]{1,0:T(8,128)(2,1)S(1)}, bf16[32,1024]{1,0:T(8,128)(2,1)S(1)}, u32[]{:S(2)}, u32[]{:S(2)}) collective-permute-start(bf16[32,1024]{1,0:T(8,128)(2,1)S(1)} %get-tuple-element.128), channel_id=1, source_target_pairs={{16,32},{17,33},{18,34},{19,35},{20,36},{21,37},{22,38},{23,39},{2... | collective-permute-start | bytes 196616 | tf_op jit(solution)/shard_map/ppermute | solution.py:412
  106.2 4.7 %collective-permute-start.31 = (bf16[32,1024]{1,0:T(8,128)(2,1)S(1)}, bf16[32,1024]{1,0:T(8,128)(2,1)S(1)}, u32[]{:S(2)}, u32[]{:S(2)}) collective-permute-start(bf16[32,1024]{1,0:T(8,128)(2,1)S(1)} %get-tuple-element.128), channel_id=1, source_target_pairs={{16,34},{17,35},{18,32},{19,33},{20,38},{21,39},{22,36},{23,37},{2... | collective-permute-start | bytes 196616 | tf_op jit(solution)/shard_map/ppermute | solution.py:412
  111.0 3.0 %out_grad.1.refs_1_ = bf16[1024,1024]{1,0:T(8,128)(2,1)} custom-call(bf16[32,1024]{1,0:T(8,128)(2,1)S(1)} %get-tuple-element.127.after, bf16[256,1024]{1,0:T(8,128)(2,1)S(1)} %get-tuple-element.130.c0, bf16[256,1024]{1,0:T(8,128)(2,1)S(1)} %get-tuple-element.131.c1, bf16[256,1024]{1,0:T(8,128)(2,1)S(1)} %bitcast.20, ...), custom_call_target="tpu_custom_call" | custom-call | flops 1073741824 | bytes 2097152 | tf_op jit(solution)/shard_map/out_grad/pallas_call | solution.py:386
  119.3 4.4 %collective-permute-start.35 = (bf16[64,1024]{1,0:T(8,128)(2,1)S(1)}, bf16[64,1024]{1,0:T(8,128)(2,1)S(1)}, u32[]{:S(2)}, u32[]{:S(2)}) collective-permute-start(bf16[64,1024]{1,0:T(8,128)(2,1)S(1)} %after_shift.3.refs_0_), channel_id=1, source_target_pairs={{0,1},{1,0},{2,3},{3,2},{4,5},{5,4},{6,7},{7,6},{8,9},{9,8},{10,11... | collective-permute-start | bytes 393224 | tf_op jit(solution)/shard_map/ppermute | solution.py:412
  (92 shorter events, 41.1 us)
Async XLA Ops:
  2.7 7.5 %collective-permute-start = (bf16[2,64,256]{2,1,0:T(8,128)(2,1)S(1)}, bf16[2,64,256]{2,1,0:T(8,128)(2,1)S(1)}, u32[]{:S(2)}, u32[]{:S(2)}) collective-permute-start(bf16[2,64,256]{2,1,0:T(8,128)(2,1)S(1)} %pick_held.1), channel_id=1, source_target_pairs={{0,112},{1,113},{2,114},{3,115},{4,116},{5,117},{6,118},{7,119},{8... | collective-permute-start | bytes 196616 | tf_op jit(solution)/shard_map/ppermute | solution.py:412
  11.7 9.7 %collective-permute-start.2 = (bf16[4,64,256]{2,1,0:T(8,128)(2,1)S(1)}, bf16[4,64,256]{2,1,0:T(8,128)(2,1)S(1)}, u32[]{:S(2)}, u32[]{:S(2)}) collective-permute-start(bf16[4,64,256]{2,1,0:T(8,128)(2,1)S(1)} %pick_reload.1.own), channel_id=1, source_target_pairs={{0,8},{1,9},{2,10},{3,11},{4,12},{5,13},{6,14},{7,15},{8,0},{9,1},... | collective-permute-start | bytes 393224 | tf_op jit(solution)/shard_map/ppermute | solution.py:412
  14.5 6.9 %collective-permute-start.3 = (bf16[4,64,256]{2,1,0:T(8,128)(2,1)S(1)}, bf16[4,64,256]{2,1,0:T(8,128)(2,1)S(1)}, u32[]{:S(2)}, u32[]{:S(2)}) collective-permute-start(bf16[4,64,256]{2,1,0:T(8,128)(2,1)S(1)} %pick_reload.1.own), channel_id=1, source_target_pairs={{0,4},{1,5},{2,6},{3,7},{4,0},{5,1},{6,2},{7,3},{8,12},{9,13},{10,... | collective-permute-start | bytes 393224 | tf_op jit(solution)/shard_map/ppermute | solution.py:412
  36.2 6.8 %collective-permute-start.7 = (bf16[64,1024]{1,0:T(8,128)(2,1)S(1)}, bf16[64,1024]{1,0:T(8,128)(2,1)S(1)}, u32[]{:S(2)}, u32[]{:S(2)}) collective-permute-start(bf16[64,1024]{1,0:T(8,128)(2,1)S(1)} %get-tuple-element.94), channel_id=1, source_target_pairs={{0,8},{1,9},{2,10},{3,11},{4,12},{5,13},{6,14},{7,15},{8,0},{9,1},... | collective-permute-start | bytes 393224 | tf_op jit(solution)/shard_map/ppermute | solution.py:412
  46.3 10.5 %collective-permute-start.11 = (bf16[32,1024]{1,0:T(8,128)(2,1)S(1)}, bf16[32,1024]{1,0:T(8,128)(2,1)S(1)}, u32[]{:S(2)}, u32[]{:S(2)}) collective-permute-start(bf16[32,1024]{1,0:T(8,128)(2,1)S(1)} %get-tuple-element.99), channel_id=1, source_target_pairs={{0,16},{1,17},{2,18},{3,19},{4,20},{5,21},{6,22},{7,23},{8,24},{9,... | collective-permute-start | bytes 196616 | tf_op jit(solution)/shard_map/ppermute | solution.py:412
  46.3 10.5 %collective-permute-start.12 = (bf16[32,1024]{1,0:T(8,128)(2,1)S(1)}, bf16[32,1024]{1,0:T(8,128)(2,1)S(1)}, u32[]{:S(2)}, u32[]{:S(2)}) collective-permute-start(bf16[32,1024]{1,0:T(8,128)(2,1)S(1)} %get-tuple-element.100), channel_id=1, source_target_pairs={{16,32},{17,33},{18,34},{19,35},{20,36},{21,37},{22,38},{23,39},{2... | collective-permute-start | bytes 196616 | tf_op jit(solution)/shard_map/ppermute | solution.py:412
  49.9 6.9 %collective-permute-start.13 = (bf16[32,1024]{1,0:T(8,128)(2,1)S(1)}, bf16[32,1024]{1,0:T(8,128)(2,1)S(1)}, u32[]{:S(2)}, u32[]{:S(2)}) collective-permute-start(bf16[32,1024]{1,0:T(8,128)(2,1)S(1)} %get-tuple-element.99), channel_id=1, source_target_pairs={{0,18},{1,19},{2,16},{3,17},{4,22},{5,23},{6,20},{7,21},{8,26},{9,... | collective-permute-start | bytes 196616 | tf_op jit(solution)/shard_map/ppermute | solution.py:412
  53.0 7.1 %collective-permute-start.14 = (bf16[32,1024]{1,0:T(8,128)(2,1)S(1)}, bf16[32,1024]{1,0:T(8,128)(2,1)S(1)}, u32[]{:S(2)}, u32[]{:S(2)}) collective-permute-start(bf16[32,1024]{1,0:T(8,128)(2,1)S(1)} %get-tuple-element.100), channel_id=1, source_target_pairs={{16,34},{17,35},{18,32},{19,33},{20,38},{21,39},{22,36},{23,37},{2... | collective-permute-start | bytes 196616 | tf_op jit(solution)/shard_map/ppermute | solution.py:412
  60.1 7.9 %collective-permute-start.15 = (bf16[64,1024]{1,0:T(8,128)(2,1)S(1)}, bf16[64,1024]{1,0:T(8,128)(2,1)S(1)}, u32[]{:S(2)}, u32[]{:S(2)}) collective-permute-start(bf16[64,1024]{1,0:T(8,128)(2,1)S(1)} %after_shift.2.refs_0_.z), channel_id=1, source_target_pairs={{0,4},{1,5},{2,6},{3,7},{4,0},{5,1},{6,2},{7,3},{8,12},{9,13},{10,... | collective-permute-start | bytes 393224 | tf_op jit(solution)/shard_map/ppermute | solution.py:412
  61.5 7.2 %collective-permute-start.16 = (bf16[64,1024]{1,0:T(8,128)(2,1)S(1)}, bf16[64,1024]{1,0:T(8,128)(2,1)S(1)}, u32[]{:S(2)}, u32[]{:S(2)}) collective-permute-start(bf16[64,1024]{1,0:T(8,128)(2,1)S(1)} %after_shift.2.refs_0_.z), channel_id=1, source_target_pairs={{0,8},{1,9},{2,10},{3,11},{4,12},{5,13},{6,14},{7,15},{8,0},{9,1},... | collective-permute-start | bytes 393224 | tf_op jit(solution)/shard_map/ppermute | solution.py:412
  64.3 7.3 %collective-permute-start.17 = (bf16[64,1024]{1,0:T(8,128)(2,1)S(1)}, bf16[64,1024]{1,0:T(8,128)(2,1)S(1)}, u32[]{:S(2)}, u32[]{:S(2)}) collective-permute-start(bf16[64,1024]{1,0:T(8,128)(2,1)S(1)} %after_shift.2.refs_0_.z), channel_id=1, source_target_pairs={{0,12},{1,13},{2,14},{3,15},{4,8},{5,9},{6,10},{7,11},{8,4},{9,5},... | collective-permute-start | bytes 393224 | tf_op jit(solution)/shard_map/ppermute | solution.py:412
  64.3 8.9 %collective-permute-start.18 = (bf16[64,1024]{1,0:T(8,128)(2,1)S(1)}, bf16[64,1024]{1,0:T(8,128)(2,1)S(1)}, u32[]{:S(2)}, u32[]{:S(2)}) collective-permute-start(bf16[64,1024]{1,0:T(8,128)(2,1)S(1)} %after_shift.2.refs_0_.z), channel_id=1, source_target_pairs={{0,1},{1,0},{2,3},{3,2},{4,5},{5,4},{6,7},{7,6},{8,9},{9,8},{10,11... | collective-permute-start | bytes 393224 | tf_op jit(solution)/shard_map/ppermute | solution.py:412
  87.1 13.1 %collective-permute-start.24 = (bf16[80,1024]{1,0:T(8,128)(2,1)S(1)}, bf16[80,1024]{1,0:T(8,128)(2,1)S(1)}, u32[]{:S(2)}, u32[]{:S(2)}) collective-permute-start(bf16[80,1024]{1,0:T(8,128)(2,1)S(1)} %get-tuple-element.121), channel_id=1, source_target_pairs={{0,8},{1,9},{2,10},{3,11},{4,12},{5,13},{6,14},{7,15},{8,0},{9,1},... | collective-permute-start | bytes 491528 | tf_op jit(solution)/shard_map/ppermute | solution.py:412
  88.0 12.1 %collective-permute-start.25 = (bf16[80,1024]{1,0:T(8,128)(2,1)S(1)}, bf16[80,1024]{1,0:T(8,128)(2,1)S(1)}, u32[]{:S(2)}, u32[]{:S(2)}) collective-permute-start(bf16[80,1024]{1,0:T(8,128)(2,1)S(1)} %get-tuple-element.122), channel_id=1, source_target_pairs={{0,4},{1,5},{2,6},{3,7},{4,0},{5,1},{6,2},{7,3},{8,12},{9,13},{10,... | collective-permute-start | bytes 491528 | tf_op jit(solution)/shard_map/ppermute | solution.py:412
  88.5 11.7 %collective-permute-start.26 = (bf16[80,1024]{1,0:T(8,128)(2,1)S(1)}, bf16[80,1024]{1,0:T(8,128)(2,1)S(1)}, u32[]{:S(2)}, u32[]{:S(2)}) collective-permute-start(bf16[80,1024]{1,0:T(8,128)(2,1)S(1)} %get-tuple-element.123), channel_id=1, source_target_pairs={{0,12},{1,13},{2,14},{3,15},{4,8},{5,9},{6,10},{7,11},{8,4},{9,5},... | collective-permute-start | bytes 491528 | tf_op jit(solution)/shard_map/ppermute | solution.py:412
  93.5 6.6 %collective-permute-start.23 = (bf16[2,64,256]{2,1,0:T(8,128)(2,1)S(1)}, bf16[2,64,256]{2,1,0:T(8,128)(2,1)S(1)}, u32[]{:S(2)}, u32[]{:S(2)}) collective-permute-start(bf16[2,64,256]{2,1,0:T(8,128)(2,1)S(1)} %pick_share.1), channel_id=1, source_target_pairs={{0,112},{1,113},{2,114},{3,115},{4,116},{5,117},{6,118},{7,119},{8... | collective-permute-start | bytes 196616 | tf_op jit(solution)/shard_map/ppermute | solution.py:412
  100.5 14.8 %collective-permute-start.28 = (bf16[32,1024]{1,0:T(8,128)(2,1)S(1)}, bf16[32,1024]{1,0:T(8,128)(2,1)S(1)}, u32[]{:S(2)}, u32[]{:S(2)}) collective-permute-start(bf16[32,1024]{1,0:T(8,128)(2,1)S(1)} %get-tuple-element.127.after), channel_id=1, source_target_pairs={{0,16},{1,17},{2,18},{3,19},{4,20},{5,21},{6,22},{7,23},{8,24},{9,... | collective-permute-start | bytes 196616 | tf_op jit(solution)/shard_map/ppermute | solution.py:412
  100.8 14.5 %collective-permute-start.30 = (bf16[32,1024]{1,0:T(8,128)(2,1)S(1)}, bf16[32,1024]{1,0:T(8,128)(2,1)S(1)}, u32[]{:S(2)}, u32[]{:S(2)}) collective-permute-start(bf16[32,1024]{1,0:T(8,128)(2,1)S(1)} %get-tuple-element.127.after), channel_id=1, source_target_pairs={{0,18},{1,19},{2,16},{3,17},{4,22},{5,23},{6,20},{7,21},{8,26},{9,... | collective-permute-start | bytes 196616 | tf_op jit(solution)/shard_map/ppermute | solution.py:412
  101.7 13.5 %collective-permute-start.29 = (bf16[32,1024]{1,0:T(8,128)(2,1)S(1)}, bf16[32,1024]{1,0:T(8,128)(2,1)S(1)}, u32[]{:S(2)}, u32[]{:S(2)}) collective-permute-start(bf16[32,1024]{1,0:T(8,128)(2,1)S(1)} %get-tuple-element.128), channel_id=1, source_target_pairs={{16,32},{17,33},{18,34},{19,35},{20,36},{21,37},{22,38},{23,39},{2... | collective-permute-start | bytes 196616 | tf_op jit(solution)/shard_map/ppermute | solution.py:412
  106.2 9.0 %collective-permute-start.31 = (bf16[32,1024]{1,0:T(8,128)(2,1)S(1)}, bf16[32,1024]{1,0:T(8,128)(2,1)S(1)}, u32[]{:S(2)}, u32[]{:S(2)}) collective-permute-start(bf16[32,1024]{1,0:T(8,128)(2,1)S(1)} %get-tuple-element.128), channel_id=1, source_target_pairs={{16,34},{17,35},{18,32},{19,33},{20,38},{21,39},{22,36},{23,37},{2... | collective-permute-start | bytes 196616 | tf_op jit(solution)/shard_map/ppermute | solution.py:412
  115.3 8.3 %collective-permute-start.32 = (bf16[64,1024]{1,0:T(8,128)(2,1)S(1)}, bf16[64,1024]{1,0:T(8,128)(2,1)S(1)}, u32[]{:S(2)}, u32[]{:S(2)}) collective-permute-start(bf16[64,1024]{1,0:T(8,128)(2,1)S(1)} %after_shift.3.refs_0_), channel_id=1, source_target_pairs={{0,4},{1,5},{2,6},{3,7},{4,0},{5,1},{6,2},{7,3},{8,12},{9,13},{10,... | collective-permute-start | bytes 393224 | tf_op jit(solution)/shard_map/ppermute | solution.py:412
  115.4 8.5 %collective-permute-start.33 = (bf16[64,1024]{1,0:T(8,128)(2,1)S(1)}, bf16[64,1024]{1,0:T(8,128)(2,1)S(1)}, u32[]{:S(2)}, u32[]{:S(2)}) collective-permute-start(bf16[64,1024]{1,0:T(8,128)(2,1)S(1)} %after_shift.3.refs_0_), channel_id=1, source_target_pairs={{0,8},{1,9},{2,10},{3,11},{4,12},{5,13},{6,14},{7,15},{8,0},{9,1},... | collective-permute-start | bytes 393224 | tf_op jit(solution)/shard_map/ppermute | solution.py:412
  117.4 8.5 %collective-permute-start.34 = (bf16[64,1024]{1,0:T(8,128)(2,1)S(1)}, bf16[64,1024]{1,0:T(8,128)(2,1)S(1)}, u32[]{:S(2)}, u32[]{:S(2)}) collective-permute-start(bf16[64,1024]{1,0:T(8,128)(2,1)S(1)} %after_shift.3.refs_0_), channel_id=1, source_target_pairs={{0,12},{1,13},{2,14},{3,15},{4,8},{5,9},{6,10},{7,11},{8,4},{9,5},... | collective-permute-start | bytes 393224 | tf_op jit(solution)/shard_map/ppermute | solution.py:412
  119.3 8.4 %collective-permute-start.35 = (bf16[64,1024]{1,0:T(8,128)(2,1)S(1)}, bf16[64,1024]{1,0:T(8,128)(2,1)S(1)}, u32[]{:S(2)}, u32[]{:S(2)}) collective-permute-start(bf16[64,1024]{1,0:T(8,128)(2,1)S(1)} %after_shift.3.refs_0_), channel_id=1, source_target_pairs={{0,1},{1,0},{2,3},{3,2},{4,5},{5,4},{6,7},{7,6},{8,9},{9,8},{10,11... | collective-permute-start | bytes 393224 | tf_op jit(solution)/shard_map/ppermute | solution.py:412
  (22 other events, 112.3 us)

commit v4 on v3

--- a/solution.py
+++ b/solution.py
@@ -140,7 +140,7 @@
         second[2 * j : 2 * j + 2] = ref[2:4]
 
 
-def pick_share(first_shares, current, after, out, turned):
+def pick_share(first_shares, current, out, turned):
     share = first_shares.shape[1]
     turned[...] = current[...].T
     out[0] = first_shares[0]
@@ -362,41 +362,39 @@
         z[rows:, :] = fresh[rows:, :]
 
 
-def step_lanes(ref):
-    width = ref.shape[1] // pl.num_programs(0)
-    return ref[:, pl.ds(pl.multiple_of(pl.program_id(0) * width, width), width)]
-
-
-def weight_kernel(after, n0, n1, a0, a1, out):
-    out[...] = (dot(n0[...], step_lanes(a0)) + dot(n1[...], step_lanes(a1))).astype(BF16)
+def step_block(ref, axis):
+    size = ref.shape[axis] // pl.num_programs(0)
+    at = pl.ds(pl.multiple_of(pl.program_id(0) * size, size), size)
+    return ref[at, :] if axis == 0 else ref[:, at]
+
+
+def in_weight_kernel(after, n0, n1, *refs):
+    left, right = step_block(n0, 0), step_block(n1, 0)
+    for i in range(3):
+        refs[6 + i][...] = (dot(left, refs[2 * i][...]) + dot(right, refs[2 * i + 1][...])).astype(BF16)
 
 
 def out_weight_kernel(after, c0, c1, g0, g1, out):
-    out[...] = (dot_tn(step_lanes(c0), g0[...]) + dot_tn(step_lanes(c1), g1[...])).astype(BF16)
-
-
-def weight_grad(name, after, left, right, by_rows=False):
+    out[...] = (dot_tn(step_block(c0, 1), g0[...]) + dot_tn(step_block(c1, 1), g1[...])).astype(BF16)
+
+
+def weight_grads(body, name, after, args, rows, count):
     steps = 4
-    tokens, cols = right[0].shape
-    rows = left[0].shape[1] if by_rows else left[0].shape[0]
-    if by_rows:
-        out = pl.BlockSpec((rows // steps, cols), lambda i: (i, 0))
-    else:
-        out = pl.BlockSpec((rows, cols // steps), lambda i: (0, i))
+    tokens, cols = args[-1].shape
     return pl.pallas_call(
-        out_weight_kernel if by_rows else weight_kernel,
+        body,
         grid=(steps,),
-        in_specs=[pl.BlockSpec(memory_space=pl.ANY)] + [VMEM] * 4,
-        out_specs=out,
-        out_shape=shape(BF16, rows, cols),
+        in_specs=[pl.BlockSpec(memory_space=pl.ANY)] + [VMEM] * len(args),
+        out_specs=[pl.BlockSpec((rows // steps, cols), lambda i: (i, 0))] * count,
+        out_shape=[shape(BF16, rows, cols)] * count,
         compiler_params=pltpu.CompilerParams(
             dimension_semantics=("arbitrary",), vmem_limit_bytes=16 * MIB
         ),
         cost_estimate=pl.CostEstimate(
-            flops=4 * tokens * rows * cols, bytes_accessed=2 * rows * cols, transcendentals=0
+            flops=4 * count * tokens * rows * cols, bytes_accessed=2 * count * rows * cols, transcendentals=0
         ),
         name=name,
-    )(after, *left, *right)
+    )(after, *args)
 
 
 class Moves:
@@ -525,9 +523,12 @@
         got = moves.flip(send, 1)
         last = t == TICKS - 1
         if last:
-            grads_of = [[grads_of[u][i] for u in range(TICKS)] for i in range(3)]
-            query_grad = weight_grad("query_grad", gain_part, left, grads_of[0])
-        beside = [from_hbm(query_grad)] if last else []
+            (shares,) = kernel_call(
+                pick_share, "pick_share", (first_shares, current), [kept(BF16, 2, share, tokens)],
+                [pltpu.VMEM((width, tokens), BF16)],
+            )
+            arrived = moves.mirror(shares, 0)
+        beside = [shares] if last else []
         own, to1, to2, to3, gain_sum = kernel_call(
             after_core, "after_core", (keep, got, gain_part, *beside),
             [kept(F32, 2 * rows, width)] + [kept(BF16, 2 * rows + extra, width)] * 3 + [kept(F32, 1, width)],
@@ -536,14 +537,11 @@
         got2 = moves.flip(to2, 8)
         got1, got3 = moves.flip(to1, 4), moves.flip(to3, 12)
         if last:
-            key_grad = weight_grad("key_grad", own, left, grads_of[1])
-            value_grad = weight_grad("value_grad", own, left, grads_of[2])
-            (shares,) = kernel_call(
-                pick_share, "pick_share", (first_shares, current, from_hbm(key_grad)), [kept(BF16, 2, share, tokens)],
-                [pltpu.VMEM((width, tokens), BF16)], 0, 1,
+            query_grad, key_grad, value_grad = weight_grads(
+                in_weight_kernel, "in_grads", own,
+                [*left, *[grads_of[u][i] for i in range(3) for u in range(TICKS)]], width, 3,
             )
-            arrived = moves.mirror(shares, 0)
-            beside = [from_hbm(key_grad), from_hbm(value_grad), arrived]
+            beside = [from_hbm(query_grad), arrived]
         else:
             read.append(recompute(1))
             beside = [read[1][5]]
@@ -555,7 +553,9 @@
         even0, odd0 = moves.even(even, 0), moves.odd(odd, 0)
         even1, odd1 = moves.even(even, 2), moves.odd(odd, 2)
         if last:
-            out_grad = weight_grad("out_grad", even, context, cotangents, True)
+            (out_grad,) = weight_grads(
+                out_weight_kernel, "out_grad", even, [*context, *cotangents], inner, 1
+            )
             gain_other = moves.flip(gain_rows, 2)
             beside = [gain_other, from_hbm(out_grad)]
         else:

time: 131 us -> 129 us (0.985)
  Pallas kernels: 45.4 us -> 41.4 us
  waiting for transfers between devices: 12 us -> 14.9 us
    pallas_call x4 -> x2, Pallas kernels: 11.8 us -> 7.96 us  [weight_grads(): pl.pallas_call(body, grid=(steps,), in_specs=[pl.BlockSpec(memory_space=p...]
    ppermute x39, waiting for transfers between devices: 12 us -> 14.9 us  [send(): return lax.ppermute(value, ('section', 'head'), pairs)]
  transfers between devices with their start and end apart: 39 -> 39, of which waited for: 9 -> 11; matrix products, arithmetic and copies ran while one was open for 0% -> 0% of each run, Pallas kernels for 18% -> 15%
where the time goes in v4:
time: 129 us
  starting transfers between devices  69 us (53%)
  Pallas kernels  41.4 us (32%)
  waiting for transfers between devices  14.9 us (12%)
  local copies, waits for them, and re-layouts  2.42 us (2%)
    ppermute x39, starting transfers between devices, send(): return lax.ppermute(value, ('section', 'head'), pairs)  69 us
    pallas_call x19, Pallas kernels, kernel_call(): pl.pallas_call(body, in_specs=[SMEM] * scalars + [VMEM] * (len(args) - sc...  33.5 us
    ppermute x39, waiting for transfers between devices, send(): return lax.ppermute(value, ('section', 'head'), pairs)  14.9 us
    pallas_call x2, Pallas kernels, weight_grads(): pl.pallas_call(body, grid=(steps,), in_specs=[pl.BlockSpec(memory_space=p...  7.96 us
  transfers between devices with their start and end apart: 39, of which 11 were waited for; matrix products, arithmetic and copies ran while one was open for 0% of the time, Pallas kernels for 15%

profile of v4, /device:TPU:9, one launch (start us, length us, event | category | flops | bytes accessed | tf_op | source)
XLA Modules:
  0.0 128.6 jit_solution(16582111073939961581)
XLA Ops:
  2.7 3.7 %collective-permute-start = (bf16[2,64,256]{2,1,0:T(8,128)(2,1)S(1)}, bf16[2,64,256]{2,1,0:T(8,128)(2,1)S(1)}, u32[]{:S(2)}, u32[]{:S(2)}) collective-permute-start(bf16[2,64,256]{2,1,0:T(8,128)(2,1)S(1)} %pick_held.1), channel_id=1, source_target_pairs={{0,112},{1,113},{2,114},{3,115},{4,116},{5,117},{6,118},{7,119},{8... | collective-permute-start | bytes 196616 | tf_op jit(solution)/shard_map/ppermute | solution.py:410
  11.7 2.8 %collective-permute-start.2 = (bf16[4,64,256]{2,1,0:T(8,128)(2,1)S(1)}, bf16[4,64,256]{2,1,0:T(8,128)(2,1)S(1)}, u32[]{:S(2)}, u32[]{:S(2)}) collective-permute-start(bf16[4,64,256]{2,1,0:T(8,128)(2,1)S(1)} %pick_reload.1.own), channel_id=1, source_target_pairs={{0,8},{1,9},{2,10},{3,11},{4,12},{5,13},{6,14},{7,15},{8,0},{9,1},... | collective-permute-start | bytes 393224 | tf_op jit(solution)/shard_map/ppermute | solution.py:410
  15.3 6.0 %forward_first.1 = (bf16[1024,1024]{1,0:T(8,128)(2,1)S(1)}, bf16[1024,1024]{1,0:T(8,128)(2,1)S(1)}, bf16[1024,1024]{1,0:T(8,128)(2,1)S(1)}, bf16[1024,1024]{1,0:...) custom-call(bf16[256,1024]{1,0:T(8,128)(2,1)S(1)} %get-tuple-element.77.rows, ...), custom_call_target="tpu_custom_call" | custom-call | flops 2684354560 | bytes 8916992 | tf_op jit(solution)/shard_map/forward_first/pallas_call | solution.py:72
  21.4 2.9 %collective-permute-start.5 = (bf16[8,64,256]{2,1,0:T(8,128)(2,1)S(1)}, bf16[8,64,256]{2,1,0:T(8,128)(2,1)S(1)}, u32[]{:S(2)}, u32[]{:S(2)}) collective-permute-start(bf16[8,64,256]{2,1,0:T(8,128)(2,1)S(1)} %get-tuple-element.84.refs_0_), channel_id=1, source_target_pairs={{0,1},{1,0},{2,3},{3,2},{4,5},{5,4},{6,7},{7,6},{8,9},{9,8},{10,11... | collective-permute-start | bytes 786440 | tf_op jit(solution)/shard_map/ppermute | solution.py:410
  25.5 3.2 %recompute.2 = (bf16[256,1024]{1,0:T(8,128)(2,1)S(1)}, bf16[1024,256]{1,0:T(8,128)(2,1)S(1)}, bf16[256,1024]{1,0:T(8,128)(2,1)S(1)}, bf16[256,1024]{1,0:T(8,128)...) custom-call(f32[1,1024]{1,0:T(1,128)S(1)} %get-tuple-element.76.gain, ...), custom_call_target="tpu_custom_call" | custom-call | flops 2684354560 | bytes 6819840 | tf_op jit(solution)/shard_map/recompute/pallas_call | solution.py:72
  28.7 5.2 %backward.2 = (f32[256,1024]{1,0:T(8,128)S(1)}, bf16[256,1024]{1,0:T(8,128)(2,1)S(1)}, bf16[256,1024]{1,0:T(8,128)(2,1)S(1)}, bf16[256,1024]{1,0:T(8,128)(2,1)S(...) custom-call(bf16[256,1024]{1,0:T(8,128)(2,1)S(1)} %bitcast.19, bf16[256,1024]{1,0:T(8,128)(2,1)S(1)} %get-tuple-element.85.block, ...), custom_call_target="tpu_custom_call" | custom-call | flops 3221225472 | bytes 13901824 | tf_op jit(solution)/shard_map/backward/pallas_call | solution.py:72
  36.1 2.7 %collective-permute-start.7 = (bf16[64,1024]{1,0:T(8,128)(2,1)S(1)}, bf16[64,1024]{1,0:T(8,128)(2,1)S(1)}, u32[]{:S(2)}, u32[]{:S(2)}) collective-permute-start(bf16[64,1024]{1,0:T(8,128)(2,1)S(1)} %get-tuple-element.97), channel_id=1, source_target_pairs={{0,8},{1,9},{2,10},{3,11},{4,12},{5,13},{6,14},{7,15},{8,0},{9,1},... | collective-permute-start | bytes 393224 | tf_op jit(solution)/shard_map/ppermute | solution.py:410
  39.7 3.2 %recompute.3 = (bf16[256,1024]{1,0:T(8,128)(2,1)S(1)}, bf16[1024,256]{1,0:T(8,128)(2,1)S(1)}, bf16[256,1024]{1,0:T(8,128)(2,1)S(1)}, bf16[256,1024]{1,0:T(8,128)...) custom-call(f32[1,1024]{1,0:T(1,128)S(1)} %get-tuple-element.76.gain, ...), custom_call_target="tpu_custom_call" | custom-call | flops 2684354560 | bytes 6819840 | tf_op jit(solution)/shard_map/recompute/pallas_call | solution.py:72
  46.2 3.6 %collective-permute-start.12 = (bf16[32,1024]{1,0:T(8,128)(2,1)S(1)}, bf16[32,1024]{1,0:T(8,128)(2,1)S(1)}, u32[]{:S(2)}, u32[]{:S(2)}) collective-permute-start(bf16[32,1024]{1,0:T(8,128)(2,1)S(1)} %get-tuple-element.103), channel_id=1, source_target_pairs={{16,32},{17,33},{18,34},{19,35},{20,36},{21,37},{22,38},{23,39},{2... | collective-permute-start | bytes 196616 | tf_op jit(solution)/shard_map/ppermute | solution.py:410
  49.8 3.1 %collective-permute-start.13 = (bf16[32,1024]{1,0:T(8,128)(2,1)S(1)}, bf16[32,1024]{1,0:T(8,128)(2,1)S(1)}, u32[]{:S(2)}, u32[]{:S(2)}) collective-permute-start(bf16[32,1024]{1,0:T(8,128)(2,1)S(1)} %get-tuple-element.102), channel_id=1, source_target_pairs={{0,18},{1,19},{2,16},{3,17},{4,22},{5,23},{6,20},{7,21},{8,26},{9,... | collective-permute-start | bytes 196616 | tf_op jit(solution)/shard_map/ppermute | solution.py:410
  52.9 3.8 %collective-permute-start.14 = (bf16[32,1024]{1,0:T(8,128)(2,1)S(1)}, bf16[32,1024]{1,0:T(8,128)(2,1)S(1)}, u32[]{:S(2)}, u32[]{:S(2)}) collective-permute-start(bf16[32,1024]{1,0:T(8,128)(2,1)S(1)} %get-tuple-element.103), channel_id=1, source_target_pairs={{16,34},{17,35},{18,32},{19,33},{20,38},{21,39},{22,36},{23,37},{2... | collective-permute-start | bytes 196616 | tf_op jit(solution)/shard_map/ppermute | solution.py:410
  56.7 3.2 %collective-permute-done.14.odd1 = bf16[32,1024]{1,0:T(8,128)(2,1)S(1)} collective-permute-done((bf16[32,1024]{1,0:T(8,128)(2,1)S(1)}, bf16[32,1024]{1,0:T(8,128)(2,1)S(1)}, u32[]{:S(2)}, u32[]{:S(2)}) %collective-permute-start.14) | collective-permute-done | bytes 65568 | tf_op jit(solution)/shard_map/ppermute | solution.py:410
  61.4 2.8 %collective-permute-start.16 = (bf16[64,1024]{1,0:T(8,128)(2,1)S(1)}, bf16[64,1024]{1,0:T(8,128)(2,1)S(1)}, u32[]{:S(2)}, u32[]{:S(2)}) collective-permute-start(bf16[64,1024]{1,0:T(8,128)(2,1)S(1)} %after_shift.2.refs_0_.z), channel_id=1, source_target_pairs={{0,8},{1,9},{2,10},{3,11},{4,12},{5,13},{6,14},{7,15},{8,0},{9,1},... | collective-permute-start | bytes 393224 | tf_op jit(solution)/shard_map/ppermute | solution.py:410
  64.2 3.7 %collective-permute-start.18 = (bf16[64,1024]{1,0:T(8,128)(2,1)S(1)}, bf16[64,1024]{1,0:T(8,128)(2,1)S(1)}, u32[]{:S(2)}, u32[]{:S(2)}) collective-permute-start(bf16[64,1024]{1,0:T(8,128)(2,1)S(1)} %after_shift.2.refs_0_.z), channel_id=1, source_target_pairs={{0,1},{1,0},{2,3},{3,2},{4,5},{5,4},{6,7},{7,6},{8,9},{9,8},{10,11... | collective-permute-start | bytes 393224 | tf_op jit(solution)/shard_map/ppermute | solution.py:410
  68.6 2.9 %collective-permute-start.20 = (bf16[64,1024]{1,0:T(8,128)(2,1)S(1)}, bf16[64,1024]{1,0:T(8,128)(2,1)S(1)}, u32[]{:S(2)}, u32[]{:S(2)}) collective-permute-start(bf16[64,1024]{1,0:T(8,128)(2,1)S(1)} %collective-permute-done.16.refs_2_), channel_id=1, source_target_pairs={{0,1},{1,0},{2,3},{3,2},{4,5},{5,4},{6,7},{7,6},{8,9},{9,8},{10,11... | collective-permute-start | bytes 393224 | tf_op jit(solution)/shard_map/ppermute | solution.py:410
  74.2 4.0 %forward_next.1 = (bf16[256,1024]{1,0:T(8,128)(2,1)S(1)}, bf16[256,1024]{1,0:T(8,128)(2,1)S(1)}, f32[128,1024]{1,0:T(8,128)S(1)}, bf16[128,1024]{1,0:T(8,128)(2,1)S(1)}) custom-call(f32[1,1024]{1,0:T(1,128)S(1)} %get-tuple-element.76.gain, bf16[1024,1024]{1,0:T(8,128)(2,1)S(1)} %get-tuple-element.78.wq, bf16[1024,1024]{1,0:T(8,128)(2,1)S(1)} %get-tuple-element.79.wk, ...), custom_call_target="tpu_custom_call" | custom-call | flops 2684354560 | bytes 9441280 | tf_op jit(solution)/shard_map/forward_next/pallas_call | solution.py:72
  78.2 5.2 %backward.3 = (f32[256,1024]{1,0:T(8,128)S(1)}, bf16[272,1024]{1,0:T(8,128)(2,1)S(1)}, bf16[256,1024]{1,0:T(8,128)(2,1)S(1)}, bf16[256,1024]{1,0:T(8,128)(2,1)S(...) custom-call(bf16[256,1024]{1,0:T(8,128)(2,1)S(1)} %get-tuple-element.106.g.g1, ...), custom_call_target="tpu_custom_call" | custom-call | flops 3221225472 | bytes 13901824 | tf_op jit(solution)/shard_map/backward/pallas_call | solution.py:72
  84.0 3.7 %collective-permute-start.22 = (bf16[2,64,256]{2,1,0:T(8,128)(2,1)S(1)}, bf16[2,64,256]{2,1,0:T(8,128)(2,1)S(1)}, u32[]{:S(2)}, u32[]{:S(2)}) collective-permute-start(bf16[2,64,256]{2,1,0:T(8,128)(2,1)S(1)} %pick_share.1.refs_0_), channel_id=1, source_target_pairs={{0,112},{1,113},{2,114},{3,115},{4,116},{5,117},{6,118},{7,119},{8... | collective-permute-start | bytes 196616 | tf_op jit(solution)/shard_map/ppermute | solution.py:410
  91.3 4.9 %in_grads.1 = (bf16[1024,1024]{1,0:T(8,128)(2,1)}, bf16[1024,1024]{1,0:T(8,128)(2,1)}, bf16[1024,1024]{1,0:T(8,128)(2,1)}) custom-call(f32[64,1024]{1,0:T(8,128)S(1)} %get-tuple-element.116.after.own, bf16[1024,256]{1,0:T(8,128)(2,1)S(1)} %get-tuple-element.121.n0, bf16[1024,256]{1,0:T(8,128)(2,1)S(1)} %get-tuple-element.122.n1, ...), custom_call_target="tpu_custom_call" | custom-call | flops 3221225472 | bytes 6291456 | tf_op jit(solution)/shard_map/in_grads/pallas_call | solution.py:384
  96.8 2.4 %collective-permute-done.26.got3 = bf16[80,1024]{1,0:T(8,128)(2,1)S(1)} collective-permute-done((bf16[80,1024]{1,0:T(8,128)(2,1)S(1)}, bf16[80,1024]{1,0:T(8,128)(2,1)S(1)}, u32[]{:S(2)}, u32[]{:S(2)}) %collective-permute-start.26) | collective-permute-done | bytes 163872 | tf_op jit(solution)/shard_map/ppermute | solution.py:410
  100.5 4.0 %collective-permute-start.29 = (bf16[32,1024]{1,0:T(8,128)(2,1)S(1)}, bf16[32,1024]{1,0:T(8,128)(2,1)S(1)}, u32[]{:S(2)}, u32[]{:S(2)}) collective-permute-start(bf16[32,1024]{1,0:T(8,128)(2,1)S(1)} %get-tuple-element.132), channel_id=1, source_target_pairs={{16,32},{17,33},{18,34},{19,35},{20,36},{21,37},{22,38},{23,39},{2... | collective-permute-start | bytes 196616 | tf_op jit(solution)/shard_map/ppermute | solution.py:410
  104.5 5.4 %collective-permute-start.31 = (bf16[32,1024]{1,0:T(8,128)(2,1)S(1)}, bf16[32,1024]{1,0:T(8,128)(2,1)S(1)}, u32[]{:S(2)}, u32[]{:S(2)}) collective-permute-start(bf16[32,1024]{1,0:T(8,128)(2,1)S(1)} %get-tuple-element.132), channel_id=1, source_target_pairs={{16,34},{17,35},{18,32},{19,33},{20,38},{21,39},{22,36},{23,37},{2... | collective-permute-start | bytes 196616 | tf_op jit(solution)/shard_map/ppermute | solution.py:410
  110.0 3.1 %out_grad.1.refs_1_ = bf16[1024,1024]{1,0:T(8,128)(2,1)} custom-call(bf16[32,1024]{1,0:T(8,128)(2,1)S(1)} %get-tuple-element.131.after, bf16[256,1024]{1,0:T(8,128)(2,1)S(1)} %get-tuple-element.134.c0, bf16[256,1024]{1,0:T(8,128)(2,1)S(1)} %get-tuple-element.135.c1, bf16[256,1024]{1,0:T(8,128)(2,1)S(1)} %bitcast.20, ...), custom_call_target="tpu_custom_call" | custom-call | flops 1073741824 | bytes 2097152 | tf_op jit(solution)/shard_map/out_grad/pallas_call | solution.py:384
  118.3 3.6 %collective-permute-start.35 = (bf16[64,1024]{1,0:T(8,128)(2,1)S(1)}, bf16[64,1024]{1,0:T(8,128)(2,1)S(1)}, u32[]{:S(2)}, u32[]{:S(2)}) collective-permute-start(bf16[64,1024]{1,0:T(8,128)(2,1)S(1)} %after_shift.3.refs_0_), channel_id=1, source_target_pairs={{0,1},{1,0},{2,3},{3,2},{4,5},{5,4},{6,7},{7,6},{8,9},{9,8},{10,11... | collective-permute-start | bytes 393224 | tf_op jit(solution)/shard_map/ppermute | solution.py:410
  (90 shorter events, 38.5 us)
Async XLA Ops:
  2.7 7.4 %collective-permute-start = (bf16[2,64,256]{2,1,0:T(8,128)(2,1)S(1)}, bf16[2,64,256]{2,1,0:T(8,128)(2,1)S(1)}, u32[]{:S(2)}, u32[]{:S(2)}) collective-permute-start(bf16[2,64,256]{2,1,0:T(8,128)(2,1)S(1)} %pick_held.1), channel_id=1, source_target_pairs={{0,112},{1,113},{2,114},{3,115},{4,116},{5,117},{6,118},{7,119},{8... | collective-permute-start | bytes 196616 | tf_op jit(solution)/shard_map/ppermute | solution.py:410
  11.7 9.7 %collective-permute-start.2 = (bf16[4,64,256]{2,1,0:T(8,128)(2,1)S(1)}, bf16[4,64,256]{2,1,0:T(8,128)(2,1)S(1)}, u32[]{:S(2)}, u32[]{:S(2)}) collective-permute-start(bf16[4,64,256]{2,1,0:T(8,128)(2,1)S(1)} %pick_reload.1.own), channel_id=1, source_target_pairs={{0,8},{1,9},{2,10},{3,11},{4,12},{5,13},{6,14},{7,15},{8,0},{9,1},... | collective-permute-start | bytes 393224 | tf_op jit(solution)/shard_map/ppermute | solution.py:410
  14.5 6.9 %collective-permute-start.3 = (bf16[4,64,256]{2,1,0:T(8,128)(2,1)S(1)}, bf16[4,64,256]{2,1,0:T(8,128)(2,1)S(1)}, u32[]{:S(2)}, u32[]{:S(2)}) collective-permute-start(bf16[4,64,256]{2,1,0:T(8,128)(2,1)S(1)} %pick_reload.1.own), channel_id=1, source_target_pairs={{0,4},{1,5},{2,6},{3,7},{4,0},{5,1},{6,2},{7,3},{8,12},{9,13},{10,... | collective-permute-start | bytes 393224 | tf_op jit(solution)/shard_map/ppermute | solution.py:410
  36.1 6.8 %collective-permute-start.7 = (bf16[64,1024]{1,0:T(8,128)(2,1)S(1)}, bf16[64,1024]{1,0:T(8,128)(2,1)S(1)}, u32[]{:S(2)}, u32[]{:S(2)}) collective-permute-start(bf16[64,1024]{1,0:T(8,128)(2,1)S(1)} %get-tuple-element.97), channel_id=1, source_target_pairs={{0,8},{1,9},{2,10},{3,11},{4,12},{5,13},{6,14},{7,15},{8,0},{9,1},... | collective-permute-start | bytes 393224 | tf_op jit(solution)/shard_map/ppermute | solution.py:410
  46.2 10.5 %collective-permute-start.11 = (bf16[32,1024]{1,0:T(8,128)(2,1)S(1)}, bf16[32,1024]{1,0:T(8,128)(2,1)S(1)}, u32[]{:S(2)}, u32[]{:S(2)}) collective-permute-start(bf16[32,1024]{1,0:T(8,128)(2,1)S(1)} %get-tuple-element.102), channel_id=1, source_target_pairs={{0,16},{1,17},{2,18},{3,19},{4,20},{5,21},{6,22},{7,23},{8,24},{9,... | collective-permute-start | bytes 196616 | tf_op jit(solution)/shard_map/ppermute | solution.py:410
  46.2 10.6 %collective-permute-start.12 = (bf16[32,1024]{1,0:T(8,128)(2,1)S(1)}, bf16[32,1024]{1,0:T(8,128)(2,1)S(1)}, u32[]{:S(2)}, u32[]{:S(2)}) collective-permute-start(bf16[32,1024]{1,0:T(8,128)(2,1)S(1)} %get-tuple-element.103), channel_id=1, source_target_pairs={{16,32},{17,33},{18,34},{19,35},{20,36},{21,37},{22,38},{23,39},{2... | collective-permute-start | bytes 196616 | tf_op jit(solution)/shard_map/ppermute | solution.py:410
  49.8 6.9 %collective-permute-start.13 = (bf16[32,1024]{1,0:T(8,128)(2,1)S(1)}, bf16[32,1024]{1,0:T(8,128)(2,1)S(1)}, u32[]{:S(2)}, u32[]{:S(2)}) collective-permute-start(bf16[32,1024]{1,0:T(8,128)(2,1)S(1)} %get-tuple-element.102), channel_id=1, source_target_pairs={{0,18},{1,19},{2,16},{3,17},{4,22},{5,23},{6,20},{7,21},{8,26},{9,... | collective-permute-start | bytes 196616 | tf_op jit(solution)/shard_map/ppermute | solution.py:410
  52.9 7.1 %collective-permute-start.14 = (bf16[32,1024]{1,0:T(8,128)(2,1)S(1)}, bf16[32,1024]{1,0:T(8,128)(2,1)S(1)}, u32[]{:S(2)}, u32[]{:S(2)}) collective-permute-start(bf16[32,1024]{1,0:T(8,128)(2,1)S(1)} %get-tuple-element.103), channel_id=1, source_target_pairs={{16,34},{17,35},{18,32},{19,33},{20,38},{21,39},{22,36},{23,37},{2... | collective-permute-start | bytes 196616 | tf_op jit(solution)/shard_map/ppermute | solution.py:410
  60.0 7.9 %collective-permute-start.15 = (bf16[64,1024]{1,0:T(8,128)(2,1)S(1)}, bf16[64,1024]{1,0:T(8,128)(2,1)S(1)}, u32[]{:S(2)}, u32[]{:S(2)}) collective-permute-start(bf16[64,1024]{1,0:T(8,128)(2,1)S(1)} %after_shift.2.refs_0_.z), channel_id=1, source_target_pairs={{0,4},{1,5},{2,6},{3,7},{4,0},{5,1},{6,2},{7,3},{8,12},{9,13},{10,... | collective-permute-start | bytes 393224 | tf_op jit(solution)/shard_map/ppermute | solution.py:410
  61.4 7.2 %collective-permute-start.16 = (bf16[64,1024]{1,0:T(8,128)(2,1)S(1)}, bf16[64,1024]{1,0:T(8,128)(2,1)S(1)}, u32[]{:S(2)}, u32[]{:S(2)}) collective-permute-start(bf16[64,1024]{1,0:T(8,128)(2,1)S(1)} %after_shift.2.refs_0_.z), channel_id=1, source_target_pairs={{0,8},{1,9},{2,10},{3,11},{4,12},{5,13},{6,14},{7,15},{8,0},{9,1},... | collective-permute-start | bytes 393224 | tf_op jit(solution)/shard_map/ppermute | solution.py:410
  64.2 7.3 %collective-permute-start.17 = (bf16[64,1024]{1,0:T(8,128)(2,1)S(1)}, bf16[64,1024]{1,0:T(8,128)(2,1)S(1)}, u32[]{:S(2)}, u32[]{:S(2)}) collective-permute-start(bf16[64,1024]{1,0:T(8,128)(2,1)S(1)} %after_shift.2.refs_0_.z), channel_id=1, source_target_pairs={{0,12},{1,13},{2,14},{3,15},{4,8},{5,9},{6,10},{7,11},{8,4},{9,5},... | collective-permute-start | bytes 393224 | tf_op jit(solution)/shard_map/ppermute | solution.py:410
  64.2 8.9 %collective-permute-start.18 = (bf16[64,1024]{1,0:T(8,128)(2,1)S(1)}, bf16[64,1024]{1,0:T(8,128)(2,1)S(1)}, u32[]{:S(2)}, u32[]{:S(2)}) collective-permute-start(bf16[64,1024]{1,0:T(8,128)(2,1)S(1)} %after_shift.2.refs_0_.z), channel_id=1, source_target_pairs={{0,1},{1,0},{2,3},{3,2},{4,5},{5,4},{6,7},{7,6},{8,9},{9,8},{10,11... | collective-permute-start | bytes 393224 | tf_op jit(solution)/shard_map/ppermute | solution.py:410
  84.0 12.2 %collective-permute-start.22 = (bf16[2,64,256]{2,1,0:T(8,128)(2,1)S(1)}, bf16[2,64,256]{2,1,0:T(8,128)(2,1)S(1)}, u32[]{:S(2)}, u32[]{:S(2)}) collective-permute-start(bf16[2,64,256]{2,1,0:T(8,128)(2,1)S(1)} %pick_share.1.refs_0_), channel_id=1, source_target_pairs={{0,112},{1,113},{2,114},{3,115},{4,116},{5,117},{6,118},{7,119},{8... | collective-permute-start | bytes 196616 | tf_op jit(solution)/shard_map/ppermute | solution.py:410
  88.0 8.2 %collective-permute-start.24 = (bf16[80,1024]{1,0:T(8,128)(2,1)S(1)}, bf16[80,1024]{1,0:T(8,128)(2,1)S(1)}, u32[]{:S(2)}, u32[]{:S(2)}) collective-permute-start(bf16[80,1024]{1,0:T(8,128)(2,1)S(1)} %get-tuple-element.118), channel_id=1, source_target_pairs={{0,8},{1,9},{2,10},{3,11},{4,12},{5,13},{6,14},{7,15},{8,0},{9,1},... | collective-permute-start | bytes 491528 | tf_op jit(solution)/shard_map/ppermute | solution.py:410
  88.8 8.0 %collective-permute-start.25 = (bf16[80,1024]{1,0:T(8,128)(2,1)S(1)}, bf16[80,1024]{1,0:T(8,128)(2,1)S(1)}, u32[]{:S(2)}, u32[]{:S(2)}) collective-permute-start(bf16[80,1024]{1,0:T(8,128)(2,1)S(1)} %get-tuple-element.119), channel_id=1, source_target_pairs={{0,4},{1,5},{2,6},{3,7},{4,0},{5,1},{6,2},{7,3},{8,12},{9,13},{10,... | collective-permute-start | bytes 491528 | tf_op jit(solution)/shard_map/ppermute | solution.py:410
  89.4 9.8 %collective-permute-start.26 = (bf16[80,1024]{1,0:T(8,128)(2,1)S(1)}, bf16[80,1024]{1,0:T(8,128)(2,1)S(1)}, u32[]{:S(2)}, u32[]{:S(2)}) collective-permute-start(bf16[80,1024]{1,0:T(8,128)(2,1)S(1)} %get-tuple-element.120), channel_id=1, source_target_pairs={{0,12},{1,13},{2,14},{3,15},{4,8},{5,9},{6,10},{7,11},{8,4},{9,5},... | collective-permute-start | bytes 491528 | tf_op jit(solution)/shard_map/ppermute | solution.py:410
  99.5 14.8 %collective-permute-start.28 = (bf16[32,1024]{1,0:T(8,128)(2,1)S(1)}, bf16[32,1024]{1,0:T(8,128)(2,1)S(1)}, u32[]{:S(2)}, u32[]{:S(2)}) collective-permute-start(bf16[32,1024]{1,0:T(8,128)(2,1)S(1)} %get-tuple-element.131.after), channel_id=1, source_target_pairs={{0,16},{1,17},{2,18},{3,19},{4,20},{5,21},{6,22},{7,23},{8,24},{9,... | collective-permute-start | bytes 196616 | tf_op jit(solution)/shard_map/ppermute | solution.py:410
  99.7 14.5 %collective-permute-start.30 = (bf16[32,1024]{1,0:T(8,128)(2,1)S(1)}, bf16[32,1024]{1,0:T(8,128)(2,1)S(1)}, u32[]{:S(2)}, u32[]{:S(2)}) collective-permute-start(bf16[32,1024]{1,0:T(8,128)(2,1)S(1)} %get-tuple-element.131.after), channel_id=1, source_target_pairs={{0,18},{1,19},{2,16},{3,17},{4,22},{5,23},{6,20},{7,21},{8,26},{9,... | collective-permute-start | bytes 196616 | tf_op jit(solution)/shard_map/ppermute | solution.py:410
  100.5 13.8 %collective-permute-start.29 = (bf16[32,1024]{1,0:T(8,128)(2,1)S(1)}, bf16[32,1024]{1,0:T(8,128)(2,1)S(1)}, u32[]{:S(2)}, u32[]{:S(2)}) collective-permute-start(bf16[32,1024]{1,0:T(8,128)(2,1)S(1)} %get-tuple-element.132), channel_id=1, source_target_pairs={{16,32},{17,33},{18,34},{19,35},{20,36},{21,37},{22,38},{23,39},{2... | collective-permute-start | bytes 196616 | tf_op jit(solution)/shard_map/ppermute | solution.py:410
  104.5 9.8 %collective-permute-start.31 = (bf16[32,1024]{1,0:T(8,128)(2,1)S(1)}, bf16[32,1024]{1,0:T(8,128)(2,1)S(1)}, u32[]{:S(2)}, u32[]{:S(2)}) collective-permute-start(bf16[32,1024]{1,0:T(8,128)(2,1)S(1)} %get-tuple-element.132), channel_id=1, source_target_pairs={{16,34},{17,35},{18,32},{19,33},{20,38},{21,39},{22,36},{23,37},{2... | collective-permute-start | bytes 196616 | tf_op jit(solution)/shard_map/ppermute | solution.py:410
  114.3 7.5 %collective-permute-start.32 = (bf16[64,1024]{1,0:T(8,128)(2,1)S(1)}, bf16[64,1024]{1,0:T(8,128)(2,1)S(1)}, u32[]{:S(2)}, u32[]{:S(2)}) collective-permute-start(bf16[64,1024]{1,0:T(8,128)(2,1)S(1)} %after_shift.3.refs_0_), channel_id=1, source_target_pairs={{0,4},{1,5},{2,6},{3,7},{4,0},{5,1},{6,2},{7,3},{8,12},{9,13},{10,... | collective-permute-start | bytes 393224 | tf_op jit(solution)/shard_map/ppermute | solution.py:410
  114.4 7.7 %collective-permute-start.33 = (bf16[64,1024]{1,0:T(8,128)(2,1)S(1)}, bf16[64,1024]{1,0:T(8,128)(2,1)S(1)}, u32[]{:S(2)}, u32[]{:S(2)}) collective-permute-start(bf16[64,1024]{1,0:T(8,128)(2,1)S(1)} %after_shift.3.refs_0_), channel_id=1, source_target_pairs={{0,8},{1,9},{2,10},{3,11},{4,12},{5,13},{6,14},{7,15},{8,0},{9,1},... | collective-permute-start | bytes 393224 | tf_op jit(solution)/shard_map/ppermute | solution.py:410
  115.9 8.1 %collective-permute-start.34 = (bf16[64,1024]{1,0:T(8,128)(2,1)S(1)}, bf16[64,1024]{1,0:T(8,128)(2,1)S(1)}, u32[]{:S(2)}, u32[]{:S(2)}) collective-permute-start(bf16[64,1024]{1,0:T(8,128)(2,1)S(1)} %after_shift.3.refs_0_), channel_id=1, source_target_pairs={{0,12},{1,13},{2,14},{3,15},{4,8},{5,9},{6,10},{7,11},{8,4},{9,5},... | collective-permute-start | bytes 393224 | tf_op jit(solution)/shard_map/ppermute | solution.py:410
  118.3 7.6 %collective-permute-start.35 = (bf16[64,1024]{1,0:T(8,128)(2,1)S(1)}, bf16[64,1024]{1,0:T(8,128)(2,1)S(1)}, u32[]{:S(2)}, u32[]{:S(2)}) collective-permute-start(bf16[64,1024]{1,0:T(8,128)(2,1)S(1)} %after_shift.3.refs_0_), channel_id=1, source_target_pairs={{0,1},{1,0},{2,3},{3,2},{4,5},{5,4},{6,7},{7,6},{8,9},{9,8},{10,11... | collective-permute-start | bytes 393224 | tf_op jit(solution)/shard_map/ppermute | solution.py:410
  (22 other events, 114.6 us)

commit v5 on v4

--- a/solution.py
+++ b/solution.py
@@ -336,7 +336,7 @@
         put_gain(gain_out, 0, gain_part[...])
 
 
-def after_shift(even0, odd0, even1, odd1, fresh, *refs):
+def after_shift(even1, even0, odd1, odd0, fresh, *refs):
     z = refs[-1]
     section = where_am_i()[3]
     rows = even0.shape[0]
@@ -561,7 +561,7 @@
         else:
             beside = []
         (z,) = kernel_call(
-            after_shift, "after_shift", (even0, odd0, even1, odd1, fresh[t], *beside),
+            after_shift, "after_shift", (even1, even0, odd1, odd0, fresh[t], *beside),
             [kept(BF16, 2 * rows, width)], (), 0, len(beside),
         )
         pieces = [z] + [moves.flip(z, 4 * j) for j in (1, 2, 3)]

time: 129 us -> 129 us (level)
  transfers between devices with their start and end apart: 39 -> 39, of which waited for: 11 -> 12; matrix products, arithmetic and copies ran while one was open for 0% -> 0% of each run, Pallas kernels for 15% -> 15%
where the time goes in v5:
time: 129 us; the launch traced here: 128 us
  starting transfers between devices  69.5 us (54%)
  Pallas kernels  41.4 us (32%)
  waiting for transfers between devices  14 us (11%)
  local copies, waits for them, and re-layouts  2.42 us (2%)
    ppermute x39, starting transfers between devices, send(): return lax.ppermute(value, ('section', 'head'), pairs)  69.5 us
    pallas_call x19, Pallas kernels, kernel_call(): pl.pallas_call(body, in_specs=[SMEM] * scalars + [VMEM] * (len(args) - sc...  33.5 us
    ppermute x39, waiting for transfers between devices, send(): return lax.ppermute(value, ('section', 'head'), pairs)  14 us
    pallas_call x2, Pallas kernels, weight_grads(): pl.pallas_call(body, grid=(steps,), in_specs=[pl.BlockSpec(memory_space=p...  7.94 us
  transfers between devices with their start and end apart: 39, of which 12 were waited for; matrix products, arithmetic and copies ran while one was open for 0% of the time, Pallas kernels for 15%

profile of v5, /device:TPU:9, one launch (start us, length us, event | category | flops | bytes accessed | tf_op | source)
XLA Modules:
  0.0 128.3 jit_solution(8613779240698904664)
XLA Ops:
  2.7 3.8 %collective-permute-start = (bf16[2,64,256]{2,1,0:T(8,128)(2,1)S(1)}, bf16[2,64,256]{2,1,0:T(8,128)(2,1)S(1)}, u32[]{:S(2)}, u32[]{:S(2)}) collective-permute-start(bf16[2,64,256]{2,1,0:T(8,128)(2,1)S(1)} %pick_held.1), channel_id=1, source_target_pairs={{0,112},{1,113},{2,114},{3,115},{4,116},{5,117},{6,118},{7,119},{8... | collective-permute-start | bytes 196616 | tf_op jit(solution)/shard_map/ppermute | solution.py:410
  11.7 2.8 %collective-permute-start.2 = (bf16[4,64,256]{2,1,0:T(8,128)(2,1)S(1)}, bf16[4,64,256]{2,1,0:T(8,128)(2,1)S(1)}, u32[]{:S(2)}, u32[]{:S(2)}) collective-permute-start(bf16[4,64,256]{2,1,0:T(8,128)(2,1)S(1)} %pick_reload.1.own), channel_id=1, source_target_pairs={{0,8},{1,9},{2,10},{3,11},{4,12},{5,13},{6,14},{7,15},{8,0},{9,1},... | collective-permute-start | bytes 393224 | tf_op jit(solution)/shard_map/ppermute | solution.py:410
  15.4 6.0 %forward_first.1 = (bf16[1024,1024]{1,0:T(8,128)(2,1)S(1)}, bf16[1024,1024]{1,0:T(8,128)(2,1)S(1)}, bf16[1024,1024]{1,0:T(8,128)(2,1)S(1)}, bf16[1024,1024]{1,0:...) custom-call(bf16[256,1024]{1,0:T(8,128)(2,1)S(1)} %get-tuple-element.77.rows, ...), custom_call_target="tpu_custom_call" | custom-call | flops 2684354560 | bytes 8916992 | tf_op jit(solution)/shard_map/forward_first/pallas_call | solution.py:72
  21.5 2.9 %collective-permute-start.5 = (bf16[8,64,256]{2,1,0:T(8,128)(2,1)S(1)}, bf16[8,64,256]{2,1,0:T(8,128)(2,1)S(1)}, u32[]{:S(2)}, u32[]{:S(2)}) collective-permute-start(bf16[8,64,256]{2,1,0:T(8,128)(2,1)S(1)} %get-tuple-element.84.refs_0_), channel_id=1, source_target_pairs={{0,1},{1,0},{2,3},{3,2},{4,5},{5,4},{6,7},{7,6},{8,9},{9,8},{10,11... | collective-permute-start | bytes 786440 | tf_op jit(solution)/shard_map/ppermute | solution.py:410
  25.5 3.2 %recompute.2 = (bf16[256,1024]{1,0:T(8,128)(2,1)S(1)}, bf16[1024,256]{1,0:T(8,128)(2,1)S(1)}, bf16[256,1024]{1,0:T(8,128)(2,1)S(1)}, bf16[256,1024]{1,0:T(8,128)...) custom-call(f32[1,1024]{1,0:T(1,128)S(1)} %get-tuple-element.76.gain, ...), custom_call_target="tpu_custom_call" | custom-call | flops 2684354560 | bytes 6819840 | tf_op jit(solution)/shard_map/recompute/pallas_call | solution.py:72
  28.8 5.2 %backward.2 = (f32[256,1024]{1,0:T(8,128)S(1)}, bf16[256,1024]{1,0:T(8,128)(2,1)S(1)}, bf16[256,1024]{1,0:T(8,128)(2,1)S(1)}, bf16[256,1024]{1,0:T(8,128)(2,1)S(...) custom-call(bf16[256,1024]{1,0:T(8,128)(2,1)S(1)} %bitcast.19, bf16[256,1024]{1,0:T(8,128)(2,1)S(1)} %get-tuple-element.85.block, ...), custom_call_target="tpu_custom_call" | custom-call | flops 3221225472 | bytes 13901824 | tf_op jit(solution)/shard_map/backward/pallas_call | solution.py:72
  36.1 2.7 %collective-permute-start.7 = (bf16[64,1024]{1,0:T(8,128)(2,1)S(1)}, bf16[64,1024]{1,0:T(8,128)(2,1)S(1)}, u32[]{:S(2)}, u32[]{:S(2)}) collective-permute-start(bf16[64,1024]{1,0:T(8,128)(2,1)S(1)} %get-tuple-element.97), channel_id=1, source_target_pairs={{0,8},{1,9},{2,10},{3,11},{4,12},{5,13},{6,14},{7,15},{8,0},{9,1},... | collective-permute-start | bytes 393224 | tf_op jit(solution)/shard_map/ppermute | solution.py:410
  39.7 3.2 %recompute.3 = (bf16[256,1024]{1,0:T(8,128)(2,1)S(1)}, bf16[1024,256]{1,0:T(8,128)(2,1)S(1)}, bf16[256,1024]{1,0:T(8,128)(2,1)S(1)}, bf16[256,1024]{1,0:T(8,128)...) custom-call(f32[1,1024]{1,0:T(1,128)S(1)} %get-tuple-element.76.gain, ...), custom_call_target="tpu_custom_call" | custom-call | flops 2684354560 | bytes 6819840 | tf_op jit(solution)/shard_map/recompute/pallas_call | solution.py:72
  42.9 2.3 %collective-permute-done.8.got1 = bf16[64,1024]{1,0:T(8,128)(2,1)S(1)} collective-permute-done((bf16[64,1024]{1,0:T(8,128)(2,1)S(1)}, bf16[64,1024]{1,0:T(8,128)(2,1)S(1)}, u32[]{:S(2)}, u32[]{:S(2)}) %collective-permute-start.8) | collective-permute-done | bytes 131104 | tf_op jit(solution)/shard_map/ppermute | solution.py:410
  47.8 3.2 %collective-permute-start.12 = (bf16[32,1024]{1,0:T(8,128)(2,1)S(1)}, bf16[32,1024]{1,0:T(8,128)(2,1)S(1)}, u32[]{:S(2)}, u32[]{:S(2)}) collective-permute-start(bf16[32,1024]{1,0:T(8,128)(2,1)S(1)} %get-tuple-element.102), channel_id=1, source_target_pairs={{0,16},{1,17},{2,18},{3,19},{4,20},{5,21},{6,22},{7,23},{8,24},{9,... | collective-permute-start | bytes 196616 | tf_op jit(solution)/shard_map/ppermute | solution.py:410
  52.9 4.3 %collective-permute-start.14 = (bf16[32,1024]{1,0:T(8,128)(2,1)S(1)}, bf16[32,1024]{1,0:T(8,128)(2,1)S(1)}, u32[]{:S(2)}, u32[]{:S(2)}) collective-permute-start(bf16[32,1024]{1,0:T(8,128)(2,1)S(1)} %get-tuple-element.103), channel_id=1, source_target_pairs={{16,32},{17,33},{18,34},{19,35},{20,36},{21,37},{22,38},{23,39},{2... | collective-permute-start | bytes 196616 | tf_op jit(solution)/shard_map/ppermute | solution.py:410
  62.1 2.4 %collective-permute-start.16 = (bf16[64,1024]{1,0:T(8,128)(2,1)S(1)}, bf16[64,1024]{1,0:T(8,128)(2,1)S(1)}, u32[]{:S(2)}, u32[]{:S(2)}) collective-permute-start(bf16[64,1024]{1,0:T(8,128)(2,1)S(1)} %after_shift.2.refs_0_.z), channel_id=1, source_target_pairs={{0,8},{1,9},{2,10},{3,11},{4,12},{5,13},{6,14},{7,15},{8,0},{9,1},... | collective-permute-start | bytes 393224 | tf_op jit(solution)/shard_map/ppermute | solution.py:410
  64.6 3.3 %collective-permute-start.18 = (bf16[64,1024]{1,0:T(8,128)(2,1)S(1)}, bf16[64,1024]{1,0:T(8,128)(2,1)S(1)}, u32[]{:S(2)}, u32[]{:S(2)}) collective-permute-start(bf16[64,1024]{1,0:T(8,128)(2,1)S(1)} %after_shift.2.refs_0_.z), channel_id=1, source_target_pairs={{0,1},{1,0},{2,3},{3,2},{4,5},{5,4},{6,7},{7,6},{8,9},{9,8},{10,11... | collective-permute-start | bytes 393224 | tf_op jit(solution)/shard_map/ppermute | solution.py:410
  68.9 3.0 %collective-permute-start.20 = (bf16[64,1024]{1,0:T(8,128)(2,1)S(1)}, bf16[64,1024]{1,0:T(8,128)(2,1)S(1)}, u32[]{:S(2)}, u32[]{:S(2)}) collective-permute-start(bf16[64,1024]{1,0:T(8,128)(2,1)S(1)} %collective-permute-done.16.refs_2_), channel_id=1, source_target_pairs={{0,1},{1,0},{2,3},{3,2},{4,5},{5,4},{6,7},{7,6},{8,9},{9,8},{10,11... | collective-permute-start | bytes 393224 | tf_op jit(solution)/shard_map/ppermute | solution.py:410
  74.3 4.0 %forward_next.1 = (bf16[256,1024]{1,0:T(8,128)(2,1)S(1)}, bf16[256,1024]{1,0:T(8,128)(2,1)S(1)}, f32[128,1024]{1,0:T(8,128)S(1)}, bf16[128,1024]{1,0:T(8,128)(2,1)S(1)}) custom-call(f32[1,1024]{1,0:T(1,128)S(1)} %get-tuple-element.76.gain, bf16[1024,1024]{1,0:T(8,128)(2,1)S(1)} %get-tuple-element.78.wq, bf16[1024,1024]{1,0:T(8,128)(2,1)S(1)} %get-tuple-element.79.wk, ...), custom_call_target="tpu_custom_call" | custom-call | flops 2684354560 | bytes 9441280 | tf_op jit(solution)/shard_map/forward_next/pallas_call | solution.py:72
  78.3 5.2 %backward.3 = (f32[256,1024]{1,0:T(8,128)S(1)}, bf16[272,1024]{1,0:T(8,128)(2,1)S(1)}, bf16[256,1024]{1,0:T(8,128)(2,1)S(1)}, bf16[256,1024]{1,0:T(8,128)(2,1)S(...) custom-call(bf16[256,1024]{1,0:T(8,128)(2,1)S(1)} %get-tuple-element.106.g.g1, ...), custom_call_target="tpu_custom_call" | custom-call | flops 3221225472 | bytes 13901824 | tf_op jit(solution)/shard_map/backward/pallas_call | solution.py:72
  84.1 2.7 %collective-permute-start.22 = (bf16[2,64,256]{2,1,0:T(8,128)(2,1)S(1)}, bf16[2,64,256]{2,1,0:T(8,128)(2,1)S(1)}, u32[]{:S(2)}, u32[]{:S(2)}) collective-permute-start(bf16[2,64,256]{2,1,0:T(8,128)(2,1)S(1)} %pick_share.1.refs_0_), channel_id=1, source_target_pairs={{0,112},{1,113},{2,114},{3,115},{4,116},{5,117},{6,118},{7,119},{8... | collective-permute-start | bytes 196616 | tf_op jit(solution)/shard_map/ppermute | solution.py:410
  90.4 4.9 %in_grads.1 = (bf16[1024,1024]{1,0:T(8,128)(2,1)}, bf16[1024,1024]{1,0:T(8,128)(2,1)}, bf16[1024,1024]{1,0:T(8,128)(2,1)}) custom-call(f32[64,1024]{1,0:T(8,128)S(1)} %get-tuple-element.116.after.own, bf16[1024,256]{1,0:T(8,128)(2,1)S(1)} %get-tuple-element.121.n0, bf16[1024,256]{1,0:T(8,128)(2,1)S(1)} %get-tuple-element.122.n1, ...), custom_call_target="tpu_custom_call" | custom-call | flops 3221225472 | bytes 6291456 | tf_op jit(solution)/shard_map/in_grads/pallas_call | solution.py:384
  95.9 2.4 %collective-permute-done.26.got3 = bf16[80,1024]{1,0:T(8,128)(2,1)S(1)} collective-permute-done((bf16[80,1024]{1,0:T(8,128)(2,1)S(1)}, bf16[80,1024]{1,0:T(8,128)(2,1)S(1)}, u32[]{:S(2)}, u32[]{:S(2)}) %collective-permute-start.26) | collective-permute-done | bytes 163872 | tf_op jit(solution)/shard_map/ppermute | solution.py:410
  98.6 3.5 %collective-permute-start.29 = (bf16[32,1024]{1,0:T(8,128)(2,1)S(1)}, bf16[32,1024]{1,0:T(8,128)(2,1)S(1)}, u32[]{:S(2)}, u32[]{:S(2)}) collective-permute-start(bf16[32,1024]{1,0:T(8,128)(2,1)S(1)} %get-tuple-element.131.after), channel_id=1, source_target_pairs={{0,16},{1,17},{2,18},{3,19},{4,20},{5,21},{6,22},{7,23},{8,24},{9,... | collective-permute-start | bytes 196616 | tf_op jit(solution)/shard_map/ppermute | solution.py:410
  104.2 5.4 %collective-permute-start.31 = (bf16[32,1024]{1,0:T(8,128)(2,1)S(1)}, bf16[32,1024]{1,0:T(8,128)(2,1)S(1)}, u32[]{:S(2)}, u32[]{:S(2)}) collective-permute-start(bf16[32,1024]{1,0:T(8,128)(2,1)S(1)} %get-tuple-element.132), channel_id=1, source_target_pairs={{16,32},{17,33},{18,34},{19,35},{20,36},{21,37},{22,38},{23,39},{2... | collective-permute-start | bytes 196616 | tf_op jit(solution)/shard_map/ppermute | solution.py:410
  110.7 3.0 %out_grad.1.refs_1_ = bf16[1024,1024]{1,0:T(8,128)(2,1)} custom-call(bf16[32,1024]{1,0:T(8,128)(2,1)S(1)} %get-tuple-element.131.after, bf16[256,1024]{1,0:T(8,128)(2,1)S(1)} %get-tuple-element.134.c0, bf16[256,1024]{1,0:T(8,128)(2,1)S(1)} %get-tuple-element.135.c1, bf16[256,1024]{1,0:T(8,128)(2,1)S(1)} %bitcast.20, ...), custom_call_target="tpu_custom_call" | custom-call | flops 1073741824 | bytes 2097152 | tf_op jit(solution)/shard_map/out_grad/pallas_call | solution.py:384
  115.6 2.7 %collective-permute-start.34 = (bf16[64,1024]{1,0:T(8,128)(2,1)S(1)}, bf16[64,1024]{1,0:T(8,128)(2,1)S(1)}, u32[]{:S(2)}, u32[]{:S(2)}) collective-permute-start(bf16[64,1024]{1,0:T(8,128)(2,1)S(1)} %after_shift.3.refs_0_), channel_id=1, source_target_pairs={{0,12},{1,13},{2,14},{3,15},{4,8},{5,9},{6,10},{7,11},{8,4},{9,5},... | collective-permute-start | bytes 393224 | tf_op jit(solution)/shard_map/ppermute | solution.py:410
  118.3 3.3 %collective-permute-start.35 = (bf16[64,1024]{1,0:T(8,128)(2,1)S(1)}, bf16[64,1024]{1,0:T(8,128)(2,1)S(1)}, u32[]{:S(2)}, u32[]{:S(2)}) collective-permute-start(bf16[64,1024]{1,0:T(8,128)(2,1)S(1)} %after_shift.3.refs_0_), channel_id=1, source_target_pairs={{0,1},{1,0},{2,3},{3,2},{4,5},{5,4},{6,7},{7,6},{8,9},{9,8},{10,11... | collective-permute-start | bytes 393224 | tf_op jit(solution)/shard_map/ppermute | solution.py:410
  (90 shorter events, 42.0 us)
Async XLA Ops:
  2.7 7.5 %collective-permute-start = (bf16[2,64,256]{2,1,0:T(8,128)(2,1)S(1)}, bf16[2,64,256]{2,1,0:T(8,128)(2,1)S(1)}, u32[]{:S(2)}, u32[]{:S(2)}) collective-permute-start(bf16[2,64,256]{2,1,0:T(8,128)(2,1)S(1)} %pick_held.1), channel_id=1, source_target_pairs={{0,112},{1,113},{2,114},{3,115},{4,116},{5,117},{6,118},{7,119},{8... | collective-permute-start | bytes 196616 | tf_op jit(solution)/shard_map/ppermute | solution.py:410
  11.7 9.7 %collective-permute-start.2 = (bf16[4,64,256]{2,1,0:T(8,128)(2,1)S(1)}, bf16[4,64,256]{2,1,0:T(8,128)(2,1)S(1)}, u32[]{:S(2)}, u32[]{:S(2)}) collective-permute-start(bf16[4,64,256]{2,1,0:T(8,128)(2,1)S(1)} %pick_reload.1.own), channel_id=1, source_target_pairs={{0,8},{1,9},{2,10},{3,11},{4,12},{5,13},{6,14},{7,15},{8,0},{9,1},... | collective-permute-start | bytes 393224 | tf_op jit(solution)/shard_map/ppermute | solution.py:410
  14.5 6.9 %collective-permute-start.3 = (bf16[4,64,256]{2,1,0:T(8,128)(2,1)S(1)}, bf16[4,64,256]{2,1,0:T(8,128)(2,1)S(1)}, u32[]{:S(2)}, u32[]{:S(2)}) collective-permute-start(bf16[4,64,256]{2,1,0:T(8,128)(2,1)S(1)} %pick_reload.1.own), channel_id=1, source_target_pairs={{0,4},{1,5},{2,6},{3,7},{4,0},{5,1},{6,2},{7,3},{8,12},{9,13},{10,... | collective-permute-start | bytes 393224 | tf_op jit(solution)/shard_map/ppermute | solution.py:410
  36.1 6.8 %collective-permute-start.7 = (bf16[64,1024]{1,0:T(8,128)(2,1)S(1)}, bf16[64,1024]{1,0:T(8,128)(2,1)S(1)}, u32[]{:S(2)}, u32[]{:S(2)}) collective-permute-start(bf16[64,1024]{1,0:T(8,128)(2,1)S(1)} %get-tuple-element.97), channel_id=1, source_target_pairs={{0,8},{1,9},{2,10},{3,11},{4,12},{5,13},{6,14},{7,15},{8,0},{9,1},... | collective-permute-start | bytes 393224 | tf_op jit(solution)/shard_map/ppermute | solution.py:410
  46.2 11.0 %collective-permute-start.11 = (bf16[32,1024]{1,0:T(8,128)(2,1)S(1)}, bf16[32,1024]{1,0:T(8,128)(2,1)S(1)}, u32[]{:S(2)}, u32[]{:S(2)}) collective-permute-start(bf16[32,1024]{1,0:T(8,128)(2,1)S(1)} %get-tuple-element.102), channel_id=1, source_target_pairs={{0,18},{1,19},{2,16},{3,17},{4,22},{5,23},{6,20},{7,21},{8,26},{9,... | collective-permute-start | bytes 196616 | tf_op jit(solution)/shard_map/ppermute | solution.py:410
  47.8 9.4 %collective-permute-start.12 = (bf16[32,1024]{1,0:T(8,128)(2,1)S(1)}, bf16[32,1024]{1,0:T(8,128)(2,1)S(1)}, u32[]{:S(2)}, u32[]{:S(2)}) collective-permute-start(bf16[32,1024]{1,0:T(8,128)(2,1)S(1)} %get-tuple-element.102), channel_id=1, source_target_pairs={{0,16},{1,17},{2,18},{3,19},{4,20},{5,21},{6,22},{7,23},{8,24},{9,... | collective-permute-start | bytes 196616 | tf_op jit(solution)/shard_map/ppermute | solution.py:410
  50.9 7.1 %collective-permute-start.13 = (bf16[32,1024]{1,0:T(8,128)(2,1)S(1)}, bf16[32,1024]{1,0:T(8,128)(2,1)S(1)}, u32[]{:S(2)}, u32[]{:S(2)}) collective-permute-start(bf16[32,1024]{1,0:T(8,128)(2,1)S(1)} %get-tuple-element.103), channel_id=1, source_target_pairs={{16,34},{17,35},{18,32},{19,33},{20,38},{21,39},{22,36},{23,37},{2... | collective-permute-start | bytes 196616 | tf_op jit(solution)/shard_map/ppermute | solution.py:410
  52.9 7.4 %collective-permute-start.14 = (bf16[32,1024]{1,0:T(8,128)(2,1)S(1)}, bf16[32,1024]{1,0:T(8,128)(2,1)S(1)}, u32[]{:S(2)}, u32[]{:S(2)}) collective-permute-start(bf16[32,1024]{1,0:T(8,128)(2,1)S(1)} %get-tuple-element.103), channel_id=1, source_target_pairs={{16,32},{17,33},{18,34},{19,35},{20,36},{21,37},{22,38},{23,39},{2... | collective-permute-start | bytes 196616 | tf_op jit(solution)/shard_map/ppermute | solution.py:410
  60.3 7.6 %collective-permute-start.15 = (bf16[64,1024]{1,0:T(8,128)(2,1)S(1)}, bf16[64,1024]{1,0:T(8,128)(2,1)S(1)}, u32[]{:S(2)}, u32[]{:S(2)}) collective-permute-start(bf16[64,1024]{1,0:T(8,128)(2,1)S(1)} %after_shift.2.refs_0_.z), channel_id=1, source_target_pairs={{0,4},{1,5},{2,6},{3,7},{4,0},{5,1},{6,2},{7,3},{8,12},{9,13},{10,... | collective-permute-start | bytes 393224 | tf_op jit(solution)/shard_map/ppermute | solution.py:410
  62.1 6.8 %collective-permute-start.16 = (bf16[64,1024]{1,0:T(8,128)(2,1)S(1)}, bf16[64,1024]{1,0:T(8,128)(2,1)S(1)}, u32[]{:S(2)}, u32[]{:S(2)}) collective-permute-start(bf16[64,1024]{1,0:T(8,128)(2,1)S(1)} %after_shift.2.refs_0_.z), channel_id=1, source_target_pairs={{0,8},{1,9},{2,10},{3,11},{4,12},{5,13},{6,14},{7,15},{8,0},{9,1},... | collective-permute-start | bytes 393224 | tf_op jit(solution)/shard_map/ppermute | solution.py:410
  64.5 7.4 %collective-permute-start.17 = (bf16[64,1024]{1,0:T(8,128)(2,1)S(1)}, bf16[64,1024]{1,0:T(8,128)(2,1)S(1)}, u32[]{:S(2)}, u32[]{:S(2)}) collective-permute-start(bf16[64,1024]{1,0:T(8,128)(2,1)S(1)} %after_shift.2.refs_0_.z), channel_id=1, source_target_pairs={{0,12},{1,13},{2,14},{3,15},{4,8},{5,9},{6,10},{7,11},{8,4},{9,5},... | collective-permute-start | bytes 393224 | tf_op jit(solution)/shard_map/ppermute | solution.py:410
  64.6 8.7 %collective-permute-start.18 = (bf16[64,1024]{1,0:T(8,128)(2,1)S(1)}, bf16[64,1024]{1,0:T(8,128)(2,1)S(1)}, u32[]{:S(2)}, u32[]{:S(2)}) collective-permute-start(bf16[64,1024]{1,0:T(8,128)(2,1)S(1)} %after_shift.2.refs_0_.z), channel_id=1, source_target_pairs={{0,1},{1,0},{2,3},{3,2},{4,5},{5,4},{6,7},{7,6},{8,9},{9,8},{10,11... | collective-permute-start | bytes 393224 | tf_op jit(solution)/shard_map/ppermute | solution.py:410
  84.1 11.1 %collective-permute-start.22 = (bf16[2,64,256]{2,1,0:T(8,128)(2,1)S(1)}, bf16[2,64,256]{2,1,0:T(8,128)(2,1)S(1)}, u32[]{:S(2)}, u32[]{:S(2)}) collective-permute-start(bf16[2,64,256]{2,1,0:T(8,128)(2,1)S(1)} %pick_share.1.refs_0_), channel_id=1, source_target_pairs={{0,112},{1,113},{2,114},{3,115},{4,116},{5,117},{6,118},{7,119},{8... | collective-permute-start | bytes 196616 | tf_op jit(solution)/shard_map/ppermute | solution.py:410
  87.0 8.2 %collective-permute-start.24 = (bf16[80,1024]{1,0:T(8,128)(2,1)S(1)}, bf16[80,1024]{1,0:T(8,128)(2,1)S(1)}, u32[]{:S(2)}, u32[]{:S(2)}) collective-permute-start(bf16[80,1024]{1,0:T(8,128)(2,1)S(1)} %get-tuple-element.118), channel_id=1, source_target_pairs={{0,8},{1,9},{2,10},{3,11},{4,12},{5,13},{6,14},{7,15},{8,0},{9,1},... | collective-permute-start | bytes 491528 | tf_op jit(solution)/shard_map/ppermute | solution.py:410
  87.9 8.0 %collective-permute-start.25 = (bf16[80,1024]{1,0:T(8,128)(2,1)S(1)}, bf16[80,1024]{1,0:T(8,128)(2,1)S(1)}, u32[]{:S(2)}, u32[]{:S(2)}) collective-permute-start(bf16[80,1024]{1,0:T(8,128)(2,1)S(1)} %get-tuple-element.119), channel_id=1, source_target_pairs={{0,4},{1,5},{2,6},{3,7},{4,0},{5,1},{6,2},{7,3},{8,12},{9,13},{10,... | collective-permute-start | bytes 491528 | tf_op jit(solution)/shard_map/ppermute | solution.py:410
  88.5 9.8 %collective-permute-start.26 = (bf16[80,1024]{1,0:T(8,128)(2,1)S(1)}, bf16[80,1024]{1,0:T(8,128)(2,1)S(1)}, u32[]{:S(2)}, u32[]{:S(2)}) collective-permute-start(bf16[80,1024]{1,0:T(8,128)(2,1)S(1)} %get-tuple-element.120), channel_id=1, source_target_pairs={{0,12},{1,13},{2,14},{3,15},{4,8},{5,9},{6,10},{7,11},{8,4},{9,5},... | collective-permute-start | bytes 491528 | tf_op jit(solution)/shard_map/ppermute | solution.py:410
  98.5 15.8 %collective-permute-start.28 = (bf16[32,1024]{1,0:T(8,128)(2,1)S(1)}, bf16[32,1024]{1,0:T(8,128)(2,1)S(1)}, u32[]{:S(2)}, u32[]{:S(2)}) collective-permute-start(bf16[32,1024]{1,0:T(8,128)(2,1)S(1)} %get-tuple-element.131.after), channel_id=1, source_target_pairs={{0,18},{1,19},{2,16},{3,17},{4,22},{5,23},{6,20},{7,21},{8,26},{9,... | collective-permute-start | bytes 196616 | tf_op jit(solution)/shard_map/ppermute | solution.py:410
  98.6 15.7 %collective-permute-start.29 = (bf16[32,1024]{1,0:T(8,128)(2,1)S(1)}, bf16[32,1024]{1,0:T(8,128)(2,1)S(1)}, u32[]{:S(2)}, u32[]{:S(2)}) collective-permute-start(bf16[32,1024]{1,0:T(8,128)(2,1)S(1)} %get-tuple-element.131.after), channel_id=1, source_target_pairs={{0,16},{1,17},{2,18},{3,19},{4,20},{5,21},{6,22},{7,23},{8,24},{9,... | collective-permute-start | bytes 196616 | tf_op jit(solution)/shard_map/ppermute | solution.py:410
  102.1 12.2 %collective-permute-start.30 = (bf16[32,1024]{1,0:T(8,128)(2,1)S(1)}, bf16[32,1024]{1,0:T(8,128)(2,1)S(1)}, u32[]{:S(2)}, u32[]{:S(2)}) collective-permute-start(bf16[32,1024]{1,0:T(8,128)(2,1)S(1)} %get-tuple-element.132), channel_id=1, source_target_pairs={{16,34},{17,35},{18,32},{19,33},{20,38},{21,39},{22,36},{23,37},{2... | collective-permute-start | bytes 196616 | tf_op jit(solution)/shard_map/ppermute | solution.py:410
  104.2 10.1 %collective-permute-start.31 = (bf16[32,1024]{1,0:T(8,128)(2,1)S(1)}, bf16[32,1024]{1,0:T(8,128)(2,1)S(1)}, u32[]{:S(2)}, u32[]{:S(2)}) collective-permute-start(bf16[32,1024]{1,0:T(8,128)(2,1)S(1)} %get-tuple-element.132), channel_id=1, source_target_pairs={{16,32},{17,33},{18,34},{19,35},{20,36},{21,37},{22,38},{23,39},{2... | collective-permute-start | bytes 196616 | tf_op jit(solution)/shard_map/ppermute | solution.py:410
  114.3 7.2 %collective-permute-start.32 = (bf16[64,1024]{1,0:T(8,128)(2,1)S(1)}, bf16[64,1024]{1,0:T(8,128)(2,1)S(1)}, u32[]{:S(2)}, u32[]{:S(2)}) collective-permute-start(bf16[64,1024]{1,0:T(8,128)(2,1)S(1)} %after_shift.3.refs_0_), channel_id=1, source_target_pairs={{0,4},{1,5},{2,6},{3,7},{4,0},{5,1},{6,2},{7,3},{8,12},{9,13},{10,... | collective-permute-start | bytes 393224 | tf_op jit(solution)/shard_map/ppermute | solution.py:410
  114.4 7.4 %collective-permute-start.33 = (bf16[64,1024]{1,0:T(8,128)(2,1)S(1)}, bf16[64,1024]{1,0:T(8,128)(2,1)S(1)}, u32[]{:S(2)}, u32[]{:S(2)}) collective-permute-start(bf16[64,1024]{1,0:T(8,128)(2,1)S(1)} %after_shift.3.refs_0_), channel_id=1, source_target_pairs={{0,8},{1,9},{2,10},{3,11},{4,12},{5,13},{6,14},{7,15},{8,0},{9,1},... | collective-permute-start | bytes 393224 | tf_op jit(solution)/shard_map/ppermute | solution.py:410
  115.6 8.1 %collective-permute-start.34 = (bf16[64,1024]{1,0:T(8,128)(2,1)S(1)}, bf16[64,1024]{1,0:T(8,128)(2,1)S(1)}, u32[]{:S(2)}, u32[]{:S(2)}) collective-permute-start(bf16[64,1024]{1,0:T(8,128)(2,1)S(1)} %after_shift.3.refs_0_), channel_id=1, source_target_pairs={{0,12},{1,13},{2,14},{3,15},{4,8},{5,9},{6,10},{7,11},{8,4},{9,5},... | collective-permute-start | bytes 393224 | tf_op jit(solution)/shard_map/ppermute | solution.py:410
  118.3 7.2 %collective-permute-start.35 = (bf16[64,1024]{1,0:T(8,128)(2,1)S(1)}, bf16[64,1024]{1,0:T(8,128)(2,1)S(1)}, u32[]{:S(2)}, u32[]{:S(2)}) collective-permute-start(bf16[64,1024]{1,0:T(8,128)(2,1)S(1)} %after_shift.3.refs_0_), channel_id=1, source_target_pairs={{0,1},{1,0},{2,3},{3,2},{4,5},{5,4},{6,7},{7,6},{8,9},{9,8},{10,11... | collective-permute-start | bytes 393224 | tf_op jit(solution)/shard_map/ppermute | solution.py:410
  (22 other events, 113.1 us)
